TPU v7x, 768 devices: a whole 4x8x12 slice. The times are simulated.
768 devices in a mesh: owner: 32 (over y, x), rep: 24 (over z, core).
Axes of the slice: x: 4, y: 8, z: 12, core: 2. Of those that a mesh axis runs over, the one named last changes fastest.
Arguments:
- cotangent: bfloat16 [589824, 256], P(('owner', 'rep')), may hold values from -6 to 6
- pre_two: bfloat16 [589824, 256], P(('owner', 'rep')), may hold values from -6 to 6
- pre_one: bfloat16 [589824, 256], P(('owner', 'rep')), may hold values from -6 to 6
- message_two: bfloat16 [589824, 256], P(('owner', 'rep')), may hold values from -6 to 6
- message_one: bfloat16 [589824, 256], P(('owner', 'rep')), may hold values from -6 to 6
- users_zero: bfloat16 [589824, 256], P(('owner', 'rep')), may hold values from -6 to 6
- w_self: bfloat16 [2, 256, 256], replicated, may hold values from -0.375 to 0.375
- w_inter: bfloat16 [2, 256, 256], replicated, may hold values from -0.375 to 0.375
- adjacency: bfloat16 [3072, 256, 256], P(('owner', 'rep')), may hold values from 0 to 0.125
- tile_user: int32 [3072], P(('owner', 'rep')), may hold values from 0 to 2
- counts: int32 [3072], P(('owner', 'rep')), may hold values from 1 to 256
- dest: int32 [24576, 1], P(('owner', 'rep')), may hold values from 0 to 31; in each aligned block of 32 rows (0 to 31, 32 to 63, ...) at most 2 rows name the same one
- item_block: int32 [24576], P(('owner', 'rep')), may hold values from 0 to 31
Outputs:
- user_grad: bfloat16 [589824, 256], P(('owner', 'rep'))
- item_grad_one: bfloat16 [786432, 256], P(('owner', 'rep'))
- item_grad_zero: bfloat16 [786432, 256], P(('owner', 'rep'))
- w_self_grad: float32 [2, 256, 256], replicated
- w_inter_grad: float32 [2, 256, 256], replicated
Inputs may be any that keep to these rules, and one draw needn't show every extreme that they name: `dest`: among the 32 row blocks of one device no owner index appears more than 2 times, and in every draw some owner is named exactly 2 times by some device.
All inputs are finite; a program needn't handle non-finite values.
Results may differ from a plain program's by a relative error of at most 0.009.
Values may be sent and summed in bfloat16 or wider, within the bound.
No kernel may reach another device: no remote copies, remote signals or barrier semaphores. Data moves between devices by JAX's collectives and lax.ppermute only.
A program may use at most 32 MiB of HBM per device.

v0:
```python
import jax
import jax.numpy as jnp
from jax import lax
from jax.sharding import PartitionSpec as P

RB = 32
IBD = 32


SLOPE = 0.2


def layer_back(gradient, pre_act, message, previous, w_self, w_inter):
    deltas = (gradient * jnp.where(pre_act > 0, 1.0, SLOPE)).astype(jnp.bfloat16)
    summed = (message.astype(jnp.float32) + previous.astype(jnp.float32)).astype(jnp.bfloat16)
    product = (message.astype(jnp.float32) * previous.astype(jnp.float32)).astype(jnp.bfloat16)
    grad_self = jnp.einsum("rf,rg->fg", summed, deltas, preferred_element_type=jnp.float32)
    grad_inter = jnp.einsum("rf,rg->fg", product, deltas, preferred_element_type=jnp.float32)
    back_self = jnp.einsum("rg,fg->rf", deltas, w_self, preferred_element_type=jnp.float32)
    back_inter = jnp.einsum("rg,fg->rf", deltas, w_inter, preferred_element_type=jnp.float32)
    d_message = (back_self + back_inter * previous.astype(jnp.float32)).astype(jnp.bfloat16)
    d_previous = back_self + back_inter * message.astype(jnp.float32)
    return (grad_self, grad_inter, d_message, d_previous)


def item_terms(d_message, masked_adj, tile_user, selector):
    tile_count, user_rows, item_cols = masked_adj.shape
    features = d_message.shape[1]
    user_blocks = d_message.reshape(-1, user_rows, features)
    picked = user_blocks[tile_user]
    partial_value = jnp.einsum(
        "kui,kuf->kif", masked_adj, picked, preferred_element_type=jnp.float32
    )
    partial_value = partial_value.astype(jnp.bfloat16).reshape(
        tile_count * item_cols // RB, RB, features
    )
    placed = jnp.einsum("sj,jrf->srf", selector, partial_value, preferred_element_type=jnp.float32)
    return placed.astype(jnp.bfloat16)


def collect(slot_items, received):
    gathered = jnp.einsum("si,srf->irf", slot_items, received, preferred_element_type=jnp.float32)
    return gathered.reshape(-1, received.shape[2]).astype(jnp.bfloat16)


def deliver(placed, slot_items):
    received, arrived = (
        lax.all_to_all(placed, "owner", split_axis=0, concat_axis=0, tiled=True),
        lax.all_to_all(slot_items, "owner", split_axis=0, concat_axis=0, tiled=True),
    )
    return collect(arrived, received)


def reduce_pair(grad_self, grad_inter):
    return lax.psum((grad_self, grad_inter), ("owner", "rep"))


def local(
    cotangent,
    pre_two,
    pre_one,
    message_two,
    message_one,
    users_zero,
    w_self,
    w_inter,
    adjacency,
    tile_user,
    counts,
    dest,
    item_block,
):
    owner_count = lax.axis_size("owner")
    row_blocks = dest.shape[0]
    capacity = max(2, 2 * row_blocks // owner_count)
    live_cols = (
        lax.broadcasted_iota(jnp.int32, (adjacency.shape[0], adjacency.shape[2]), 1)
        < counts[:, None]
    )
    masked_adj = jnp.where(live_cols[:, None, :], adjacency, jnp.zeros((), jnp.bfloat16))
    owner_of = dest[:, 0]
    positions = lax.broadcasted_iota(jnp.int32, (row_blocks,), 0)
    same_owner = owner_of[:, None] == owner_of[None, :]
    earlier = positions[None, :] < positions[:, None]
    slot_rank = jnp.sum(jnp.logical_and(same_owner, earlier).astype(jnp.int32), axis=1)
    slot_index = owner_of * capacity + slot_rank
    all_slots = lax.broadcasted_iota(jnp.int32, (owner_count * capacity, row_blocks), 0)
    selector = (all_slots == slot_index[None, :]).astype(jnp.bfloat16)
    item_slots = lax.broadcasted_iota(jnp.int32, (row_blocks, IBD), 1)
    target = (item_block[:, None] == item_slots).astype(jnp.bfloat16)
    slot_items = jnp.dot(selector, target, preferred_element_type=jnp.float32).astype(jnp.bfloat16)
    one_f = pre_one.astype(jnp.float32)
    users_one = jnp.where(one_f > 0, one_f, SLOPE * one_f).astype(jnp.bfloat16)
    self_two, inter_two, msg_two, prev_two = layer_back(
        cotangent.astype(jnp.float32), pre_two, message_two, users_one, w_self[1], w_inter[1]
    )
    placed_two = item_terms(msg_two, masked_adj, tile_user, selector)
    item_one = deliver(placed_two, slot_items)
    self_two, inter_two = reduce_pair(self_two, inter_two)
    self_one, inter_one, msg_one, prev_one = layer_back(
        prev_two, pre_one, message_one, users_zero, w_self[0], w_inter[0]
    )
    placed_one = item_terms(msg_one, masked_adj, tile_user, selector)
    item_zero = deliver(placed_one, slot_items)
    self_one, inter_one = reduce_pair(self_one, inter_one)
    return (
        prev_one.astype(jnp.bfloat16),
        item_one,
        item_zero,
        jnp.stack([self_one, self_two]),
        jnp.stack([inter_one, inter_two]),
    )


def solution(mesh):
    return jax.shard_map(
        local,
        mesh=mesh,
        in_specs=(
            P(("owner", "rep"), None),
            P(("owner", "rep"), None),
            P(("owner", "rep"), None),
            P(("owner", "rep"), None),
            P(("owner", "rep"), None),
            P(("owner", "rep"), None),
            P(),
            P(),
            P(("owner", "rep"), None, None),
            P(("owner", "rep")),
            P(("owner", "rep")),
            P(("owner", "rep"), None),
            P(("owner", "rep")),
        ),
        out_specs=(
            P(("owner", "rep"), None),
            P(("owner", "rep"), None),
            P(("owner", "rep"), None),
            P(),
            P(),
        ),
        check_vma=False,
    )
```

profile of v0, /device:TPU:1, one launch (start us, length us, event | category | flops | bytes accessed | tf_op | source)
XLA Modules:
  0.0 585.3 jit_solution(8571123051254407244)
XLA Ops:
  7.2 0.0 copy-start.5
  7.2 0.9 convert_reduce_fusion
  8.1 0.7 multiply_add_fusion
  8.8 0.0 copy-start.11
  8.8 0.9 convolution_convert_fusion.6
  9.7 0.7 copy.40
  10.4 10.5 %all-to-all-start = ((bf16[32,2,32]{2,1,0:T(2,128)(2,1)}), bf16[32,2,32]{2,1,0:T(2,128)(2,1)S(1)}, u32[]{:S(2)}, u32[]{:S(2)}) async-start(bf16[32,2,32]{2,1,0:T(2,128)(2,1)} %bitcast.5), calls=%async_computation | async-start | bytes 32768 | tf_op jit(solution)/shard_map/all_to_all | solution.py:49
  20.9 0.7 compare_select_fusion.1
  21.5 0.0 copy-start.8
  21.6 0.7 iota_compare_fusion.5
  22.3 0.0 copy-start.9
  22.3 0.0 copy-start.15
  22.3 1.3 multiply_convert_fusion
  23.6 0.0 copy-done.5
  23.7 0.0 copy-start.3
  23.7 0.3 fusion.28
  24.0 0.0 copy-done.6
  24.0 0.0 copy-done.13
  24.0 0.0 copy-done.15
  24.0 0.4 fusion.8
  24.4 0.0 copy-done.3
  24.4 0.0 copy-start.2
  24.5 0.0 copy-done.8
  24.5 0.6 gather_fusion
  25.1 0.0 copy-done.9
  25.1 0.4 copy-done.2
  25.5 0.4 convolution_convert_fusion.5
  25.9 0.0 copy-done.11
  25.9 0.6 convolution_convert_fusion.1
  26.4 1.6 copy.43
  28.0 1.4 all-to-all-done
  29.4 7.8 %all-to-all-start.1 = ((bf16[64,32,256]{2,1,0:T(8,128)(2,1)}), bf16[64,32,256]{2,1,0:T(8,128)(2,1)S(1)}, u32[]{:S(2)}, u32[]{:S(2)}) async-start(bf16[64,32,256]{2,1,0:T(8,128)(2,1)} %copy.43), calls=%async_computation.1 | async-start | bytes 2097152 | tf_op jit(solution)/shard_map/all_to_all | solution.py:48
  37.2 0.0 copy-start
  37.2 0.0 copy-start.1
  37.2 0.0 copy-start.7
  37.3 0.3 fusion.24
  37.6 0.7 copy-done
  38.2 0.1 copy-done.1
  38.3 0.1 copy-done.7
  38.4 1.1 fusion.12
  39.5 1.6 gather_fusion.1
  41.1 0.0 copy-done.10
  41.1 1.4 convolution_convert_fusion.3
  42.5 0.0 copy-done.12
  42.5 0.6 convolution_convert_fusion
  43.1 1.6 copy.49
  44.7 15.5 %all-to-all-done.1 = bf16[64,32,256]{2,1,0:T(8,128)(2,1)S(1)} async-done(((bf16[64,32,256]{2,1,0:T(8,128)(2,1)}), bf16[64,32,256]{2,1,0:T(8,128)(2,1)S(1)}, u32[]{:S(2)}, u32[]{:S(2)}) %all-to-all-start.1) | async-done | bytes 1048608 | tf_op jit(solution)/shard_map/all_to_all | solution.py:48
  60.2 7.1 %all-to-all-start.2 = ((bf16[64,32,256]{2,1,0:T(8,128)(2,1)}), bf16[64,32,256]{2,1,0:T(8,128)(2,1)S(1)}, u32[]{:S(2)}, u32[]{:S(2)}) async-start(bf16[64,32,256]{2,1,0:T(8,128)(2,1)} %copy.49), calls=%async_computation.2 | async-start | bytes 2097152 | tf_op jit(solution)/shard_map/all_to_all | solution.py:48
  67.3 0.0 all-reduce.3.cloned.1.call-start
  67.3 1.0 convolution_bitcast_fusion.3
  68.4 1.0 convolution_bitcast_fusion.1
  69.4 0.0 copy-done.4
  69.4 0.1 copy-done.14
  69.5 0.2 copy-done.16
  69.6 1.1 convolution_bitcast_fusion.2
  70.7 1.1 convolution_bitcast_fusion
  71.8 0.0 all-reduce.3.cloned.1.call-update
  71.8 500.6 %all-reduce.3.cloned.1.call-done = (f32[1,256,256]{2,1,0:T(8,128)}, f32[1,256,256]{2,1,0:T(8,128)}, f32[1,256,256]{2,1,0:T(8,128)}, f32[1,256,256]{2,1,0:T(8,128)}) async-done(((f32[1,256,256]{2,1,0:T(8,128)}, f32[1,256,256]{2,1,0:T(8,128)}, f32[1,256,256]{2,1,0:T(8,128)}, f32[1,256,256]{2,1,0:T(8,128)}), (f32[1,256,256]{2,1,0:T(8,128)}, f32[1,256,256]{2,1,0:T(8,128)}, f32[1,256,256]{2,1,0:T(8,128)}, ...) | async-done | bytes 1048592 | tf_op jit(solution)/shard_map/psum | solution.py:55
  572.3 2.2 pad_maximum_fusion
  574.6 0.8 convolution_convert_fusion.4
  575.4 1.1 copy.46
  576.5 0.0 all-to-all-done.2
  576.5 0.8 convolution_convert_fusion.2
  577.4 1.1 copy.52
  (8 shorter events, 0.0 us)
Async XLA Ops:
  7.2 16.5 %copy-start.5 = (bf16[2,256,256]{2,1,0:T(8,128)(2,1)S(1)}, bf16[2,256,256]{2,1,0:T(8,128)(2,1)}, u32[]{:S(2)}) copy-start(bf16[2,256,256]{2,1,0:T(8,128)(2,1)} %param.20) | copy-start | bytes 786436
  8.8 17.1 %copy-start.11 = (s32[32]{0:T(128)}, s32[32]{0:T(128)S(1)}, u32[]{:S(2)}) copy-start(s32[32]{0:T(128)S(1)} %multiply_add_fusion) | copy-start | bytes 388
  10.4 19.0 %all-to-all-start = ((bf16[32,2,32]{2,1,0:T(2,128)(2,1)}), bf16[32,2,32]{2,1,0:T(2,128)(2,1)S(1)}, u32[]{:S(2)}, u32[]{:S(2)}) async-start(bf16[32,2,32]{2,1,0:T(2,128)(2,1)} %bitcast.5), calls=%async_computation | async-start | bytes 32768 | tf_op jit(solution)/shard_map/all_to_all | solution.py:49
  21.5 2.9 copy-start.8
  22.3 2.8 copy-start.9
  22.3 1.7 copy-start.6
  22.3 1.7 copy-start.13
  22.3 1.7 copy-start.15
  23.7 0.8 copy-start.3
  24.4 1.0 copy-start.2
  29.4 30.8 %all-to-all-start.1 = ((bf16[64,32,256]{2,1,0:T(8,128)(2,1)}), bf16[64,32,256]{2,1,0:T(8,128)(2,1)S(1)}, u32[]{:S(2)}, u32[]{:S(2)}) async-start(bf16[64,32,256]{2,1,0:T(8,128)(2,1)} %copy.43), calls=%async_computation.1 | async-start | bytes 2097152 | tf_op jit(solution)/shard_map/all_to_all | solution.py:48
  37.2 1.0 copy-start
  37.2 1.1 copy-start.1
  37.2 1.2 copy-start.7
  39.5 1.6 copy-start.10
  41.1 1.4 copy-start.12
  60.2 516.4 %all-to-all-start.2 = ((bf16[64,32,256]{2,1,0:T(8,128)(2,1)}), bf16[64,32,256]{2,1,0:T(8,128)(2,1)S(1)}, u32[]{:S(2)}, u32[]{:S(2)}) async-start(bf16[64,32,256]{2,1,0:T(8,128)(2,1)} %copy.49), calls=%async_computation.2 | async-start | bytes 2097152 | tf_op jit(solution)/shard_map/all_to_all | solution.py:48
  67.3 505.1 %all-reduce.3.cloned.1.call-start = ((), (), s32[]{:S(2)}) async-start(), calls=%async_computation.3 | async-start | bytes 2097152 | tf_op jit(solution)/shard_map/psum | solution.py:55
  68.3 1.0 copy-start.4
  68.4 1.1 copy-start.14
  68.4 1.3 copy-start.16
Sparse Core Ops, SparseCore 0:
  74.9 497.4 all-reduce.2
where the time goes:
time: 587 us; the launch traced here: 585 us
  waiting for transfers between devices  517 us (88%)
  starting transfers between devices  25.5 us (4%)
  between operations  14.3 us (2%)
  matrix products  11.7 us (2%)
  local copies, waits for them, and re-layouts  9.84 us (2%)
  other arithmetic  6.56 us (1%)
    psum x1, waiting for transfers between devices, reduce_pair(): return lax.psum((grad_self, grad_inter), ('owner', 'rep'))  501 us
    all_to_all x2, waiting for transfers between devices, deliver(): lax.all_to_all(placed, 'owner', split_axis=0, concat_axis=0, tiled=True)  15.5 us
    all_to_all x2, starting transfers between devices, deliver(): lax.all_to_all(placed, 'owner', split_axis=0, concat_axis=0, tiled=True)  14.9 us
  transfers between devices with their start and end apart: 4, of which 3 were waited for; matrix products, arithmetic and copies ran while one was open for 4% of the time, Pallas kernels for 0%

commit v1 on v0

v1 whole, which is shorter than its diff:
```python
import functools

import jax
import jax.numpy as jnp
from jax import lax
from jax.experimental import pallas as pl
from jax.experimental.pallas import tpu as pltpu
from jax.sharding import PartitionSpec as P

BF = jnp.bfloat16
F32 = jnp.float32
SLOPE = 0.2
RB = 32
FEAT = 256
HALF = 128
BLK = 256
OWNERS = 32
TRASH = 32
VMEM = pl.BlockSpec(memory_space=pltpu.VMEM)
SMEM = pl.BlockSpec(memory_space=pltpu.SMEM)
PARAMS = pltpu.CompilerParams(vmem_limit_bytes=40 * 1024 * 1024)


def tdot(a, b):
    return lax.dot_general(a, b, (((0,), (0,)), ((), ())), preferred_element_type=F32)


def dot_t(a, b):
    return lax.dot_general(a, b, (((1,), (1,)), ((), ())), preferred_element_type=F32)


def layer_math(layer, grad_ref, pre_ref, msg_ref, prev_ref, ws_ref, wi_ref, dprev_ref, delta_s, sum_s, prod_s, dmsg_s):
    for b in range(grad_ref.shape[0] // BLK):
        rows = pl.ds(b * BLK, BLK)
        pre = pre_ref[rows, :].astype(F32)
        deltas = (grad_ref[rows, :].astype(F32) * jnp.where(pre > 0, 1.0, SLOPE)).astype(BF)
        prev = prev_ref[rows, :].astype(F32)
        if layer == 1:
            prev = jnp.where(prev > 0, prev, SLOPE * prev).astype(BF).astype(F32)
        msg = msg_ref[rows, :].astype(F32)
        delta_s[rows, :] = deltas
        sum_s[rows, :] = (msg + prev).astype(BF)
        prod_s[rows, :] = (msg * prev).astype(BF)
        back_self = dot_t(deltas, ws_ref[layer])
        back_inter = dot_t(deltas, wi_ref[layer])
        dmsg_s[rows, :] = (back_self + back_inter * prev).astype(BF)
        dprev_ref[rows, :] = (back_self + back_inter * msg).astype(dprev_ref.dtype)


def split_grads(delta_s, sum_s, prod_s, keep_ref, send_ref):
    grad_self = tdot(sum_s[...], delta_s[...])
    grad_inter = tdot(prod_s[...], delta_s[...])
    core = lax.rem(lax.axis_index("rep"), 2)
    even = core == 0
    keep_ref[...] = jnp.where(even, grad_self, grad_inter)
    send_ref[...] = jnp.where(even, grad_inter, grad_self)


def rank_blocks(dest_ref, rank_s, seen_s):
    for o in range(OWNERS):
        seen_s[o] = 0
    for j in range(dest_ref.shape[0]):
        o = dest_ref[j, 0]
        rank_s[j] = seen_s[o]
        seen_s[o] = seen_s[o] + 1


def tile_terms(adj_ref, user_ref, count_ref, dmsg_s, store):
    for t in range(adj_ref.shape[0]):
        start = pl.multiple_of(user_ref[t] * BLK, BLK)
        part = tdot(adj_ref[t], dmsg_s[pl.ds(start, BLK), :])
        live = lax.broadcasted_iota(jnp.int32, part.shape, 0) < count_ref[t]
        part = jnp.where(live, part, 0.0).astype(BF)
        for b in range(part.shape[0] // RB):
            store(t * (part.shape[0] // RB) + b, part[b * RB : (b + 1) * RB, :])


def two_kernel(user_ref, count_ref, dest_ref, item_ref, cot_ref, pre_ref, msg_ref, one_ref, ws_ref, wi_ref, adj_ref,
               dprev_ref, a_ref, second_ref, keep_ref, send_ref, delta_s, sum_s, prod_s, dmsg_s, rank_s, seen_s, tab_s):
    rank_blocks(dest_ref, rank_s, seen_s)
    for i in range(2 * OWNERS):
        tab_s[i] = TRASH
    for j in range(dest_ref.shape[0]):
        tab_s[2 * dest_ref[j, 0] + rank_s[j]] = item_ref[j]
    a_ref[...] = jnp.zeros_like(a_ref)
    second_ref[...] = jnp.zeros_like(second_ref)
    top = lax.broadcasted_iota(jnp.int32, (16, HALF), 0) < 8
    for o in range(OWNERS):
        a_ref[o, 64:80, :] = jnp.where(top, tab_s[2 * o], tab_s[2 * o + 1]).astype(F32).astype(BF)
    layer_math(1, cot_ref, pre_ref, msg_ref, one_ref, ws_ref, wi_ref, dprev_ref, delta_s, sum_s, prod_s, dmsg_s)

    def store(j, block):
        o = dest_ref[j, 0]

        @pl.when(rank_s[j] == 0)
        def _():
            a_ref[o, 0:32, :] = block[:, :HALF]
            a_ref[o, 32:64, :] = block[:, HALF:]

        @pl.when(rank_s[j] != 0)
        def _():
            second_ref[o, 0:32, :] = block[:, :HALF]
            second_ref[o, 32:64, :] = block[:, HALF:]

    tile_terms(adj_ref, user_ref, count_ref, dmsg_s, store)
    split_grads(delta_s, sum_s, prod_s, keep_ref, send_ref)


def one_kernel(user_ref, count_ref, dest_ref, grad_ref, pre_ref, msg_ref, zero_ref, ws_ref, wi_ref, adj_ref,
               user_grad_ref, c_ref, d_ref, keep_ref, send_ref, delta_s, sum_s, prod_s, dmsg_s, rank_s, seen_s):
    rank_blocks(dest_ref, rank_s, seen_s)
    c_ref[...] = jnp.zeros_like(c_ref)
    d_ref[...] = jnp.zeros_like(d_ref)
    layer_math(0, grad_ref, pre_ref, msg_ref, zero_ref, ws_ref, wi_ref, user_grad_ref, delta_s, sum_s, prod_s, dmsg_s)
    split_grads(delta_s, sum_s, prod_s, keep_ref, send_ref)

    def store(j, block):
        o = dest_ref[j, 0]

        @pl.when(rank_s[j] == 0)
        def _():
            c_ref[o, 0:32, :] = block[:, :HALF]
            c_ref[o, 32:64, :] = block[:, HALF:]

        @pl.when(rank_s[j] != 0)
        def _():
            c_ref[o, 64:96, :] = block[:, :HALF]
            d_ref[o, :, :] = block[:, HALF:]

    tile_terms(adj_ref, user_ref, count_ref, dmsg_s, store)


def pack_kernel(second_ref, keep2_ref, got2_ref, keep1_ref, got1_ref, b_ref):
    for o in range(OWNERS):
        b_ref[o, 0:64, :] = second_ref[o]
        rows = slice(8 * o, 8 * o + 8)
        for at, keep_ref, got_ref in ((64, keep2_ref, got2_ref), (80, keep1_ref, got1_ref)):
            total = keep_ref[rows, :] + got_ref[rows, :]
            b_ref[o, at : at + 16, :] = jnp.concatenate([total[:, :HALF], total[:, HALF:]], axis=0).astype(BF)


def chunk_kernel(b_ref, total_ref):
    acc = b_ref[0, 64:96, :].astype(F32)
    for s in range(1, OWNERS):
        acc = acc + b_ref[s, 64:96, :].astype(F32)
    total_ref[...] = acc


def collect_kernel(cuts, index_ref, *refs):
    *in_refs, out_ref, acc_s = refs
    acc_s[...] = jnp.zeros_like(acc_s)

    def body(s, carry):
        for ref, pieces in zip(in_refs, cuts):
            for slot, at, to, rows in pieces:
                i = index_ref[2 * s + slot]
                acc_s[i, to : to + rows, :] += ref[s, at : at + rows, :].astype(F32)
        return carry

    lax.fori_loop(0, OWNERS, body, 0, unroll=4)
    for i in range(TRASH):
        out_ref[RB * i : RB * i + RB, :HALF] = acc_s[i, 0:32, :].astype(BF)
        out_ref[RB * i : RB * i + RB, HALF:] = acc_s[i, 32:64, :].astype(BF)


def unpack_kernel(mine_ref, other_ref, self_ref, inter_ref):
    even = lax.rem(lax.axis_index("rep"), 2) == 0
    for o in range(OWNERS):
        mine = mine_ref[o, 32:64, :].astype(F32)
        other = other_ref[o].astype(F32)
        a = jnp.where(even, mine, other)
        b = jnp.where(even, other, mine)
        rows = slice(8 * o, 8 * o + 8)
        for ref, value in ((self_ref, a), (inter_ref, b)):
            ref[1, rows, :HALF] = value[0:8]
            ref[1, rows, HALF:] = value[8:16]
            ref[0, rows, :HALF] = value[16:24]
            ref[0, rows, HALF:] = value[24:32]


def call(kernel, outs, in_specs, scratch=(), **cost):
    return pl.pallas_call(
        kernel,
        out_shape=[jax.ShapeDtypeStruct(s, d) for s, d in outs],
        in_specs=in_specs,
        out_specs=[VMEM] * len(outs),
        scratch_shapes=list(scratch),
        compiler_params=PARAMS,
        cost_estimate=pl.CostEstimate(transcendentals=0, **cost),
    )


def local(cotangent, pre_two, pre_one, message_two, message_one, users_zero, w_self, w_inter, adjacency, tile_user,
          counts, dest, item_block):
    users = cotangent.shape[0]
    reps = lax.axis_size("rep")
    swap = [(i, i ^ 1) for i in range(reps)]

    def along_z(step):
        return [(2 * z + c, 2 * step(z) + c) for z in range(reps // 2) for c in range(2)]

    def to_owners(x):
        return lax.all_to_all(x, "owner", split_axis=0, concat_axis=0, tiled=True)

    scratch = [pltpu.VMEM((users, FEAT), BF)] * 4 + [pltpu.SMEM((OWNERS,), jnp.int32)] * 2
    cost = dict(flops=1_100_000_000, bytes_accessed=5 << 20)

    dprev, a, second, keep2, send2 = call(
        two_kernel,
        [((users, FEAT), F32), ((OWNERS, 80, HALF), BF), ((OWNERS, 64, HALF), BF), ((FEAT, FEAT), F32), ((FEAT, FEAT), F32)],
        [SMEM] * 4 + [VMEM] * 7,
        scratch + [pltpu.SMEM((2 * OWNERS,), jnp.int32)],
        **cost,
    )(tile_user, counts, dest, item_block, cotangent, pre_two, message_two, pre_one, w_self, w_inter, adjacency)
    got_a = to_owners(a)

    user_grad, c, d_items, keep1, send1 = call(
        one_kernel,
        [((users, FEAT), BF), ((OWNERS, 96, HALF), BF), ((OWNERS, 32, HALF), BF), ((FEAT, FEAT), F32), ((FEAT, FEAT), F32)],
        [SMEM] * 3 + [VMEM] * 7,
        scratch,
        **cost,
    )(tile_user, counts, dest, dprev, pre_one, message_one, users_zero, w_self, w_inter, adjacency)
    got2 = lax.ppermute(send2, "rep", swap)
    got1 = lax.ppermute(send1, "rep", swap)
    (b,) = call(pack_kernel, [((OWNERS, 96, HALF), BF)], [VMEM] * 5, flops=1_000_000, bytes_accessed=2 << 20)(
        second, keep2, got2, keep1, got1
    )
    got_b = to_owners(b)

    (total,) = call(chunk_kernel, [((32, HALF), F32)], [VMEM], flops=1_000_000, bytes_accessed=1 << 18)(got_b)
    got_c = to_owners(c)
    total = total + lax.ppermute(total, "rep", along_z(lambda z: z ^ 1))
    total = total + lax.ppermute(total, "rep", along_z(lambda z: z ^ 2))
    z_chips = reps // 2
    total = (
        total
        + lax.ppermute(total, "rep", along_z(lambda z: (z + 4) % z_chips))
        + lax.ppermute(total, "rep", along_z(lambda z: (z + 8) % z_chips))
    )
    d = jnp.concatenate([d_items, jnp.broadcast_to(total.astype(BF)[None], (OWNERS, 32, HALF))], axis=1)
    got_d = to_owners(d)

    index = got_a[:, 64:80:8, 0].astype(jnp.int32).reshape(2 * OWNERS)
    acc = [pltpu.VMEM((TRASH + 1, 64, HALF), F32)]
    item = [((OWNERS * RB, FEAT), BF)]
    (item_one,) = call(
        functools.partial(collect_kernel, (((0, 0, 0, 64),), ((1, 0, 0, 64),))),
        item, [SMEM, VMEM, VMEM], acc, flops=1_000_000, bytes_accessed=3 << 20,
    )(index, got_a, got_b)
    other = lax.ppermute(got_d[:, 32:64], "rep", swap)
    (item_zero,) = call(
        functools.partial(collect_kernel, (((0, 0, 0, 64), (1, 64, 0, 32)), ((1, 0, 32, 32),))),
        item, [SMEM, VMEM, VMEM], acc, flops=1_000_000, bytes_accessed=3 << 20,
    )(index, got_c, got_d)
    self_grad, inter_grad = call(
        unpack_kernel, [((2, FEAT, FEAT), F32)] * 2, [VMEM] * 2, flops=1_000_000, bytes_accessed=2 << 20
    )(got_d, other)
    return user_grad, item_one, item_zero, self_grad, inter_grad


def solution(mesh):
    both = ("owner", "rep")
    rows = P(both, None)
    return jax.shard_map(
        local,
        mesh=mesh,
        in_specs=(rows,) * 6 + (P(), P(), P(both, None, None), P(both), P(both), rows, P(both)),
        out_specs=(rows, rows, rows, P(), P()),
        check_vma=False,
    )
```

time: 587 us -> 145 us (0.25)
  the two profiles are of different devices: /device:TPU:1 before, /device:TPU:2 now
where the time goes in v1:
time: 145 us; the launch traced here: 144 us
  blocking collectives  57.8 us (40%)
  starting transfers between devices  37 us (26%)
  waiting for transfers between devices  27.4 us (19%)
  Pallas kernels  12.7 us (9%)
  local copies, waits for them, and re-layouts  8.04 us (6%)
    all_to_all x2, blocking collectives, to_owners(): return lax.all_to_all(x, 'owner', split_axis=0, concat_axis=0, tiled=True)  57.8 us
    all_to_all x2, waiting for transfers between devices, to_owners(): return lax.all_to_all(x, 'owner', split_axis=0, concat_axis=0, tiled=True)  12.4 us
    ppermute x1, starting transfers between devices, local(): lax.ppermute(total, 'rep', along_z(lambda z: (z + 8) % z_chips))  12 us
    all_to_all x2, starting transfers between devices, to_owners(): return lax.all_to_all(x, 'owner', split_axis=0, concat_axis=0, tiled=True)  11 us
    unnamed x33, local copies, waits for them, and re-layouts  7.71 us
    ppermute x1, waiting for transfers between devices, local(): lax.ppermute(total, 'rep', along_z(lambda z: (z + 4) % z_chips))  7.62 us
    pallas_call x1, Pallas kernels, local(): call(one_kernel, [((users, FEAT), BF), ((OWNERS, 96, HALF), BF), ((OWNERS...  3.95 us
    pallas_call x1, Pallas kernels, local(): call(two_kernel, [((users, FEAT), F32), ((OWNERS, 80, HALF), BF), ((OWNER...  3.92 us
  transfers between devices with their start and end apart: 9, of which 5 were waited for; matrix products, arithmetic and copies ran while one was open for 1% of the time, Pallas kernels for 5%

profile of v1, /device:TPU:2, one launch (start us, length us, event | category | flops | bytes accessed | tf_op | source)
XLA Modules:
  0.0 144.5 jit_solution(2622795182003552381)
XLA Ops:
  0.6 0.0 copy-start.14
  0.6 0.0 copy-start.15
  0.7 0.0 copy-start.13
  0.7 0.8 copy.21.dest_ref
  1.4 0.0 copy-done.14
  1.4 0.0 copy-done.15
  1.4 0.0 copy-done.13
  1.4 0.0 copy-start
  1.4 1.0 copy-done
  2.5 0.0 copy-start.2
  2.5 1.0 copy-done.2
  3.5 0.0 copy-start.3
  3.5 1.0 copy-done.3
  4.5 0.0 copy-start.4
  4.5 1.0 copy-done.4
  5.5 0.0 copy-start.5
  5.5 1.0 copy-done.5
  6.5 0.0 copy-start.9
  6.5 0.9 copy-done.9
  7.4 0.0 copy-start.11
  7.4 0.9 copy-done.11
  8.4 0.0 copy-start.1
  8.4 0.0 copy-start.6
  8.4 0.0 copy-start.7
  8.4 0.0 copy-start.8
  8.4 0.0 copy-start.10
  8.4 0.0 copy-start.12
  8.4 3.9 %shard_map.164 = (f32[768,256]{1,0:T(8,128)S(1)}, bf16[32,80,128]{2,1,0:T(8,128)(2,1)}, bf16[32,64,128]{2,1,0:T(8,128)(2,1)S(1)}, f32[256,256]{1,0:T(8,128)S(1)}, f32[256,256]{1,0:T(8,128)S(1)}) custom-call(s32[4]{0:T(128)S(1)} %copy-done.14, s32[4]{0:T(128)S(1)} %copy-done.15, s32[32,1]{1,0:T(8,128)S(1)} %copy.21.dest_ref, s32[32]{0:T(128)S(1)} %copy-done.13, ...), custom_call_target="tpu_custom_call" | custom-call | flops 1100000000 | bytes 5242880 | tf_op jit(solution)/shard_map/pallas_call | solution.py:208
  12.3 1.9 %collective-permute-start = (f32[256,256]{1,0:T(8,128)S(1)}, f32[256,256]{1,0:T(8,128)S(1)}, u32[]{:S(2)}, u32[]{:S(2)}) collective-permute-start(f32[256,256]{1,0:T(8,128)S(1)} %get-tuple-element.22), channel_id=1, source_target_pairs={{0,1},{1,0},{2,3},{3,2},{4,5},{5,4},{6,7},{7,6},{8,9},{9,8},{10,11... | collective-permute-start | bytes 786440 | tf_op jit(solution)/shard_map/ppermute | solution.py:224
  14.2 0.0 copy-done.1
  14.2 0.0 copy-done.6
  14.2 0.0 copy-done.7
  14.3 0.0 copy-done.8
  14.3 0.0 copy-done.10
  14.3 0.0 copy-done.12
  14.3 3.9 %shard_map.165 = (bf16[768,256]{1,0:T(8,128)(2,1)}, bf16[32,96,128]{2,1,0:T(8,128)(2,1)}, bf16[32,32,128]{2,1,0:T(8,128)(2,1)S(1)}, f32[256,256]{1,0:T(8,128)S(1)}, f32[256,256]{1,0:T(8,128)S(1)}) custom-call(s32[4]{0:T(128)S(1)} %copy-done.14, s32[4]{0:T(128)S(1)} %copy-done.15, s32[32,1]{1,0:T(8,128)S(1)} %copy.21.dest_ref, ...), custom_call_target="tpu_custom_call" | custom-call | flops 1100000000 | bytes 5242880 | tf_op jit(solution)/shard_map/pallas_call | solution.py:217
  18.2 2.4 %collective-permute-start.1 = (f32[256,256]{1,0:T(8,128)S(1)}, f32[256,256]{1,0:T(8,128)S(1)}, u32[]{:S(2)}, u32[]{:S(2)}) collective-permute-start(f32[256,256]{1,0:T(8,128)S(1)} %get-tuple-element.24), channel_id=1, source_target_pairs={{0,1},{1,0},{2,3},{3,2},{4,5},{5,4},{6,7},{7,6},{8,9},{9,8},{10,11... | collective-permute-start | bytes 786440 | tf_op jit(solution)/shard_map/ppermute | solution.py:225
  20.6 0.0 collective-permute-done.got2_ref
  20.6 1.1 collective-permute-done.1.got1_ref
  21.8 0.1 shard_map.166
  21.9 35.6 %all_to_all.20.refs_1_.b_ref = bf16[32,96,128]{2,1,0:T(8,128)(2,1)S(1)} all-to-all(bf16[32,96,128]{2,1,0:T(8,128)(2,1)S(1)} %shard_map.166), channel_id=1, replica_groups=mesh['owner'=32,'rep'=24] {'owner'}, dimensions={0} | all-to-all | bytes 1572864 | tf_op jit(solution)/shard_map/all_to_all | solution.py:203
  57.4 5.6 %all-to-all-start = ((bf16[32,80,128]{2,1,0:T(8,128)(2,1)}), bf16[32,80,128]{2,1,0:T(8,128)(2,1)S(1)}, u32[]{:S(2)}, u32[]{:S(2)}) async-start(bf16[32,80,128]{2,1,0:T(8,128)(2,1)} %get-tuple-element.19), calls=%async_computation | async-start | bytes 1310720 | tf_op jit(solution)/shard_map/all_to_all | solution.py:203
  63.1 1.9 %collective-permute-start.2 = (f32[32,128]{1,0:T(8,128)S(1)}, f32[32,128]{1,0:T(8,128)S(1)}, u32[]{:S(2)}, u32[]{:S(2)}) collective-permute-start(f32[32,128]{1,0:T(8,128)S(1)} %shard_map.168), channel_id=1, source_target_pairs={{0,2},{1,3},{2,0},{3,1},{4,6},{5,7},{6,4},{7,5},{8,10},{9,11},{10,... | collective-permute-start | bytes 49160 | tf_op jit(solution)/shard_map/ppermute | solution.py:233
  65.0 3.7 %collective-permute-done.2 = f32[32,128]{1,0:T(8,128)S(1)} collective-permute-done((f32[32,128]{1,0:T(8,128)S(1)}, f32[32,128]{1,0:T(8,128)S(1)}, u32[]{:S(2)}, u32[]{:S(2)}) %collective-permute-start.2) | collective-permute-done | bytes 16416 | tf_op jit(solution)/shard_map/ppermute | solution.py:233
  68.7 3.9 %collective-permute-start.3 = (f32[32,128]{1,0:T(8,128)S(1)}, f32[32,128]{1,0:T(8,128)S(1)}, u32[]{:S(2)}, u32[]{:S(2)}) collective-permute-start(f32[32,128]{1,0:T(8,128)S(1)} %add.12), channel_id=1, source_target_pairs={{0,4},{1,5},{2,6},{3,7},{4,0},{5,1},{6,2},{7,3},{8,12},{9,13},{10,... | collective-permute-start | bytes 49160 | tf_op jit(solution)/shard_map/ppermute | solution.py:234
  72.6 2.6 %collective-permute-done.3 = f32[32,128]{1,0:T(8,128)S(1)} collective-permute-done((f32[32,128]{1,0:T(8,128)S(1)}, f32[32,128]{1,0:T(8,128)S(1)}, u32[]{:S(2)}, u32[]{:S(2)}) %collective-permute-start.3) | collective-permute-done | bytes 16416 | tf_op jit(solution)/shard_map/ppermute | solution.py:234
  75.2 12.0 %collective-permute-start.5 = (f32[32,128]{1,0:T(8,128)S(1)}, f32[32,128]{1,0:T(8,128)S(1)}, u32[]{:S(2)}, u32[]{:S(2)}) collective-permute-start(f32[32,128]{1,0:T(8,128)S(1)} %add.13), channel_id=1, source_target_pairs={{0,16},{1,17},{2,18},{3,19},{4,20},{5,21},{6,22},{7,23},{8,0},{9,1... | collective-permute-start | bytes 49160 | tf_op jit(solution)/shard_map/ppermute | solution.py:239
  87.3 1.9 %collective-permute-start.4 = (f32[32,128]{1,0:T(8,128)S(1)}, f32[32,128]{1,0:T(8,128)S(1)}, u32[]{:S(2)}, u32[]{:S(2)}) collective-permute-start(f32[32,128]{1,0:T(8,128)S(1)} %add.13), channel_id=1, source_target_pairs={{0,8},{1,9},{2,10},{3,11},{4,12},{5,13},{6,14},{7,15},{8,16},{9,17... | collective-permute-start | bytes 49160 | tf_op jit(solution)/shard_map/ppermute | solution.py:238
  89.2 0.0 collective-permute-done.5
  89.2 7.6 %collective-permute-done.4 = f32[32,128]{1,0:T(8,128)S(1)} collective-permute-done((f32[32,128]{1,0:T(8,128)S(1)}, f32[32,128]{1,0:T(8,128)S(1)}, u32[]{:S(2)}, u32[]{:S(2)}) %collective-permute-start.4) | collective-permute-done | bytes 16416 | tf_op jit(solution)/shard_map/ppermute | solution.py:238
  96.9 0.1 pad_maximum_fusion
  96.9 0.0 all-to-all-done.refs_0_
  97.0 22.2 %all_to_all.21.refs_1_.mine_ref = bf16[32,64,128]{2,1,0:T(8,128)(2,1)S(1)} all-to-all(bf16[32,64,128]{2,1,0:T(8,128)(2,1)S(1)} %pad_maximum_fusion), channel_id=1, replica_groups=mesh['owner'=32,'rep'=24] {'owner'}, dimensions={0} | all-to-all | bytes 1048576 | tf_op jit(solution)/shard_map/all_to_all | solution.py:203
  119.2 5.4 %all-to-all-start.2 = ((bf16[32,96,128]{2,1,0:T(8,128)(2,1)}), bf16[32,96,128]{2,1,0:T(8,128)(2,1)S(1)}, u32[]{:S(2)}, u32[]{:S(2)}) async-start(bf16[32,96,128]{2,1,0:T(8,128)(2,1)} %get-tuple-element.25), calls=%async_computation.2 | async-start | bytes 1572864 | tf_op jit(solution)/shard_map/all_to_all | solution.py:203
  124.6 1.9 %collective-permute-start.6 = (bf16[32,32,128]{2,1,0:T(8,128)(2,1)S(1)}, bf16[32,32,128]{2,1,0:T(8,128)(2,1)S(1)}, u32[]{:S(2)}, u32[]{:S(2)}) collective-permute-start(bf16[32,32,128]{2,1,0:T(8,128)(2,1)S(1)} %slice.8), channel_id=1, source_target_pairs={{0,1},{1,0},{2,3},{3,2},{4,5},{5,4},{6,7},{7,6},{8,9},{9,8},{10,11... | collective-permute-start | bytes 786440 | tf_op jit(solution)/shard_map/ppermute | solution.py:251
  126.5 0.2 slice.6
  126.7 0.6 convert_reduce_fusion
  127.3 0.1 reshape.15.index_ref
  127.4 1.8 %shard_map.167 = bf16[1024,256]{1,0:T(8,128)(2,1)} custom-call(s32[64]{0:T(128)S(1)} %reshape.15.index_ref, bf16[32,80,128]{2,1,0:T(8,128)(2,1)S(1)} %all-to-all-done.refs_0_, bf16[32,96,128]{2,1,0:T(8,128)(2,1)S(1)} %all_to_all.20.refs_1_.b_ref), custom_call_target="tpu_custom_call" | custom-call | flops 1000000 | bytes 3145728 | tf_op jit(solution)/shard_map/pallas_call | solution.py:247
  129.2 12.4 %all-to-all-done.2.refs_0_ = bf16[32,96,128]{2,1,0:T(8,128)(2,1)S(1)} async-done(((bf16[32,96,128]{2,1,0:T(8,128)(2,1)}), bf16[32,96,128]{2,1,0:T(8,128)(2,1)S(1)}, u32[]{:S(2)}, u32[]{:S(2)}) %all-to-all-start.2) | async-done | bytes 786464 | tf_op jit(solution)/shard_map/all_to_all | solution.py:203
  141.5 1.9 %shard_map.169 = bf16[1024,256]{1,0:T(8,128)(2,1)} custom-call(s32[64]{0:T(128)S(1)} %reshape.15.index_ref, bf16[32,96,128]{2,1,0:T(8,128)(2,1)S(1)} %all-to-all-done.2.refs_0_, bf16[32,64,128]{2,1,0:T(8,128)(2,1)S(1)} %all_to_all.21.refs_1_.mine_ref), custom_call_target="tpu_custom_call" | custom-call | flops 1000000 | bytes 3145728 | tf_op jit(solution)/shard_map/pallas_call | solution.py:252
  143.4 0.0 collective-permute-done.6.other_ref
  143.4 1.1 shard_map.170
  (6 shorter events, 0.1 us)
Async XLA Ops:
  0.6 0.8 copy-start.14
  0.6 0.8 copy-start.15
  0.7 0.8 copy-start.13
  1.4 1.0 copy-start
  2.5 1.0 copy-start.2
  3.5 1.0 copy-start.3
  4.5 1.0 copy-start.4
  5.5 1.0 copy-start.5
  6.5 0.9 copy-start.9
  7.4 0.9 copy-start.11
  8.4 5.9 %copy-start.1 = (bf16[4,256,256]{2,1,0:T(8,128)(2,1)S(1)}, bf16[4,256,256]{2,1,0:T(8,128)(2,1)}, u32[]{:S(2)}) copy-start(bf16[4,256,256]{2,1,0:T(8,128)(2,1)} %adj_ref.3) | copy-start | bytes 1572868
  8.4 5.9 %copy-start.6 = (bf16[768,256]{1,0:T(8,128)(2,1)S(1)}, bf16[768,256]{1,0:T(8,128)(2,1)}, u32[]{:S(2)}) copy-start(bf16[768,256]{1,0:T(8,128)(2,1)} %pre_ref.3) | copy-start | bytes 1179652
  8.4 5.9 %copy-start.7 = (bf16[768,256]{1,0:T(8,128)(2,1)S(1)}, bf16[768,256]{1,0:T(8,128)(2,1)}, u32[]{:S(2)}) copy-start(bf16[768,256]{1,0:T(8,128)(2,1)} %msg_ref.3) | copy-start | bytes 1179652
  8.4 5.9 %copy-start.8 = (bf16[768,256]{1,0:T(8,128)(2,1)S(1)}, bf16[768,256]{1,0:T(8,128)(2,1)}, u32[]{:S(2)}) copy-start(bf16[768,256]{1,0:T(8,128)(2,1)} %zero_ref.1) | copy-start | bytes 1179652
  8.4 5.9 %copy-start.10 = (bf16[2,256,256]{2,1,0:T(8,128)(2,1)S(1)}, bf16[2,256,256]{2,1,0:T(8,128)(2,1)}, u32[]{:S(2)}) copy-start(bf16[2,256,256]{2,1,0:T(8,128)(2,1)} %ws_ref.3) | copy-start | bytes 786436
  8.4 5.9 %copy-start.12 = (bf16[2,256,256]{2,1,0:T(8,128)(2,1)S(1)}, bf16[2,256,256]{2,1,0:T(8,128)(2,1)}, u32[]{:S(2)}) copy-start(bf16[2,256,256]{2,1,0:T(8,128)(2,1)} %wi_ref.3) | copy-start | bytes 786436
  12.3 8.3 %collective-permute-start = (f32[256,256]{1,0:T(8,128)S(1)}, f32[256,256]{1,0:T(8,128)S(1)}, u32[]{:S(2)}, u32[]{:S(2)}) collective-permute-start(f32[256,256]{1,0:T(8,128)S(1)} %get-tuple-element.22), channel_id=1, source_target_pairs={{0,1},{1,0},{2,3},{3,2},{4,5},{5,4},{6,7},{7,6},{8,9},{9,8},{10,11... | collective-permute-start | bytes 786440 | tf_op jit(solution)/shard_map/ppermute | solution.py:224
  18.2 3.5 %collective-permute-start.1 = (f32[256,256]{1,0:T(8,128)S(1)}, f32[256,256]{1,0:T(8,128)S(1)}, u32[]{:S(2)}, u32[]{:S(2)}) collective-permute-start(f32[256,256]{1,0:T(8,128)S(1)} %get-tuple-element.24), channel_id=1, source_target_pairs={{0,1},{1,0},{2,3},{3,2},{4,5},{5,4},{6,7},{7,6},{8,9},{9,8},{10,11... | collective-permute-start | bytes 786440 | tf_op jit(solution)/shard_map/ppermute | solution.py:225
  57.4 39.5 %all-to-all-start = ((bf16[32,80,128]{2,1,0:T(8,128)(2,1)}), bf16[32,80,128]{2,1,0:T(8,128)(2,1)S(1)}, u32[]{:S(2)}, u32[]{:S(2)}) async-start(bf16[32,80,128]{2,1,0:T(8,128)(2,1)} %get-tuple-element.19), calls=%async_computation | async-start | bytes 1310720 | tf_op jit(solution)/shard_map/all_to_all | solution.py:203
  63.1 5.6 %collective-permute-start.2 = (f32[32,128]{1,0:T(8,128)S(1)}, f32[32,128]{1,0:T(8,128)S(1)}, u32[]{:S(2)}, u32[]{:S(2)}) collective-permute-start(f32[32,128]{1,0:T(8,128)S(1)} %shard_map.168), channel_id=1, source_target_pairs={{0,2},{1,3},{2,0},{3,1},{4,6},{5,7},{6,4},{7,5},{8,10},{9,11},{10,... | collective-permute-start | bytes 49160 | tf_op jit(solution)/shard_map/ppermute | solution.py:233
  68.7 6.5 %collective-permute-start.3 = (f32[32,128]{1,0:T(8,128)S(1)}, f32[32,128]{1,0:T(8,128)S(1)}, u32[]{:S(2)}, u32[]{:S(2)}) collective-permute-start(f32[32,128]{1,0:T(8,128)S(1)} %add.12), channel_id=1, source_target_pairs={{0,4},{1,5},{2,6},{3,7},{4,0},{5,1},{6,2},{7,3},{8,12},{9,13},{10,... | collective-permute-start | bytes 49160 | tf_op jit(solution)/shard_map/ppermute | solution.py:234
  75.2 14.0 %collective-permute-start.5 = (f32[32,128]{1,0:T(8,128)S(1)}, f32[32,128]{1,0:T(8,128)S(1)}, u32[]{:S(2)}, u32[]{:S(2)}) collective-permute-start(f32[32,128]{1,0:T(8,128)S(1)} %add.13), channel_id=1, source_target_pairs={{0,16},{1,17},{2,18},{3,19},{4,20},{5,21},{6,22},{7,23},{8,0},{9,1... | collective-permute-start | bytes 49160 | tf_op jit(solution)/shard_map/ppermute | solution.py:239
  87.3 9.6 %collective-permute-start.4 = (f32[32,128]{1,0:T(8,128)S(1)}, f32[32,128]{1,0:T(8,128)S(1)}, u32[]{:S(2)}, u32[]{:S(2)}) collective-permute-start(f32[32,128]{1,0:T(8,128)S(1)} %add.13), channel_id=1, source_target_pairs={{0,8},{1,9},{2,10},{3,11},{4,12},{5,13},{6,14},{7,15},{8,16},{9,17... | collective-permute-start | bytes 49160 | tf_op jit(solution)/shard_map/ppermute | solution.py:238
  119.2 22.4 %all-to-all-start.2 = ((bf16[32,96,128]{2,1,0:T(8,128)(2,1)}), bf16[32,96,128]{2,1,0:T(8,128)(2,1)S(1)}, u32[]{:S(2)}, u32[]{:S(2)}) async-start(bf16[32,96,128]{2,1,0:T(8,128)(2,1)} %get-tuple-element.25), calls=%async_computation.2 | async-start | bytes 1572864 | tf_op jit(solution)/shard_map/all_to_all | solution.py:203
  124.6 18.8 %collective-permute-start.6 = (bf16[32,32,128]{2,1,0:T(8,128)(2,1)S(1)}, bf16[32,32,128]{2,1,0:T(8,128)(2,1)S(1)}, u32[]{:S(2)}, u32[]{:S(2)}) collective-permute-start(bf16[32,32,128]{2,1,0:T(8,128)(2,1)S(1)} %slice.8), channel_id=1, source_target_pairs={{0,1},{1,0},{2,3},{3,2},{4,5},{5,4},{6,7},{7,6},{8,9},{9,8},{10,11... | collective-permute-start | bytes 786440 | tf_op jit(solution)/shard_map/ppermute | solution.py:251

commit v2 on v1

v2 whole, which is shorter than its diff:
```python
import functools

import jax
import jax.numpy as jnp
from jax import lax
from jax.experimental import pallas as pl
from jax.experimental.pallas import tpu as pltpu
from jax.sharding import PartitionSpec as P

BF = jnp.bfloat16
F32 = jnp.float32
SLOPE = 0.2
RB = 32
FEAT = 256
HALF = 128
BLK = 256
OWNERS = 32
TRASH = 32
VMEM = pl.BlockSpec(memory_space=pltpu.VMEM)
SMEM = pl.BlockSpec(memory_space=pltpu.SMEM)
HBM = pl.BlockSpec(memory_space=pltpu.HBM)
ANY = pl.BlockSpec(memory_space=pl.ANY)
PARAMS = pltpu.CompilerParams(vmem_limit_bytes=12 * 1024 * 1024)
WIDE = pltpu.CompilerParams(vmem_limit_bytes=60 * 1024 * 1024)


def tdot(a, b):
    return lax.dot_general(a, b, (((0,), (0,)), ((), ())), preferred_element_type=F32)


def dot_t(a, b):
    return lax.dot_general(a, b, (((1,), (1,)), ((), ())), preferred_element_type=F32)


def user_kernel(*refs):
    ins, rest = refs[:8], refs[8:]
    dmsg2_ref, dmsg1_ref, user_grad_ref, keep_ref, send_ref = rest[:5]
    bufs, sum2_s, prod2_s, delta2_s, sum1_s, prod1_s, delta1_s, sems = rest[5:13], *rest[13:]
    blocks = ins[0].shape[0] // BLK
    weights = [pltpu.make_async_copy(ins[i], bufs[i], sems.at[i]) for i in (6, 7)]
    for copy in weights:
        copy.start()
    loads = []
    for b in range(blocks):
        rows = pl.ds(b * BLK, BLK)
        loads.append(
            [pltpu.make_async_copy(ins[i].at[rows], bufs[i].at[rows], sems.at[8 + 6 * b + i]) for i in range(6)]
        )
        for copy in loads[-1]:
            copy.start()
    cot, pre2, pre1, msg2, msg1, zero, ws, wi = bufs
    for copy in weights:
        copy.wait()
    for b in range(blocks):
        rows = pl.ds(b * BLK, BLK)
        for copy in loads[b]:
            copy.wait()
        one = pre1[rows, :].astype(F32)
        prev = jnp.where(one > 0, one, SLOPE * one).astype(BF).astype(F32)
        deltas = (cot[rows, :].astype(F32) * jnp.where(pre2[rows, :].astype(F32) > 0, 1.0, SLOPE)).astype(BF)
        msg = msg2[rows, :].astype(F32)
        delta2_s[rows, :] = deltas
        sum2_s[rows, :] = (msg + prev).astype(BF)
        prod2_s[rows, :] = (msg * prev).astype(BF)
        back_self = dot_t(deltas, ws[1])
        back_inter = dot_t(deltas, wi[1])
        dmsg2_ref[rows, :] = (back_self + back_inter * prev).astype(BF)
        dprev = back_self + back_inter * msg
        deltas = (dprev * jnp.where(one > 0, 1.0, SLOPE)).astype(BF)
        msg = msg1[rows, :].astype(F32)
        prev = zero[rows, :].astype(F32)
        delta1_s[rows, :] = deltas
        sum1_s[rows, :] = (msg + prev).astype(BF)
        prod1_s[rows, :] = (msg * prev).astype(BF)
        back_self = dot_t(deltas, ws[0])
        back_inter = dot_t(deltas, wi[0])
        dmsg1_ref[rows, :] = (back_self + back_inter * prev).astype(BF)
        user_grad_ref[rows, :] = (back_self + back_inter * msg).astype(BF)
    even = lax.rem(lax.axis_index("rep"), 2) == 0
    for at, (sum_s, prod_s, delta_s) in enumerate(((sum2_s, prod2_s, delta2_s), (sum1_s, prod1_s, delta1_s))):
        grad_self = tdot(sum_s[...], delta_s[...])
        grad_inter = tdot(prod_s[...], delta_s[...])
        keep_ref[at] = jnp.where(even, grad_self, grad_inter)
        send_ref[at] = jnp.where(even, grad_inter, grad_self)


def rank_blocks(dest_ref, rank_s, seen_s):
    for o in range(OWNERS):
        seen_s[o] = 0
    for j in range(dest_ref.shape[0]):
        o = dest_ref[j]
        rank_s[j] = seen_s[o]
        seen_s[o] = seen_s[o] + 1


def tile_terms(user_ref, count_ref, dest_ref, adj_ref, dmsg_ref, rank_s, out_ref):
    for t in range(adj_ref.shape[0]):
        start = pl.multiple_of(user_ref[t] * BLK, BLK)
        part = tdot(adj_ref[t], dmsg_ref[pl.ds(start, BLK), :])
        live = lax.broadcasted_iota(jnp.int32, part.shape, 0) < count_ref[t]
        part = jnp.where(live, part, 0.0).astype(BF)
        for b in range(part.shape[0] // RB):
            j = t * (part.shape[0] // RB) + b
            at = pl.multiple_of(rank_s[j] * 64, 64)
            block = part[b * RB : (b + 1) * RB, :]
            out_ref[dest_ref[j], pl.ds(at, RB), :] = block[:, :HALF]
            out_ref[dest_ref[j], pl.ds(at + RB, RB), :] = block[:, HALF:]


def two_kernel(user_ref, count_ref, dest_ref, item_ref, adj_ref, dmsg_ref, a_ref, rank_s, seen_s, tab_s):
    rank_blocks(dest_ref, rank_s, seen_s)
    for i in range(2 * OWNERS):
        tab_s[i] = TRASH
    for j in range(dest_ref.shape[0]):
        tab_s[2 * dest_ref[j] + rank_s[j]] = item_ref[j]
    a_ref[...] = jnp.zeros_like(a_ref)
    top = lax.broadcasted_iota(jnp.int32, (16, HALF), 0) < 8
    for o in range(OWNERS):
        a_ref[o, 128:144, :] = jnp.where(top, tab_s[2 * o], tab_s[2 * o + 1]).astype(F32).astype(BF)
    tile_terms(user_ref, count_ref, dest_ref, adj_ref, dmsg_ref, rank_s, a_ref)


def one_kernel(user_ref, count_ref, dest_ref, adj_ref, dmsg_ref, b_ref, rank_s, seen_s):
    rank_blocks(dest_ref, rank_s, seen_s)
    b_ref[...] = jnp.zeros_like(b_ref)
    tile_terms(user_ref, count_ref, dest_ref, adj_ref, dmsg_ref, rank_s, b_ref)


def pack_kernel(keep_ref, got_ref, items_ref, a_ref, grads_s, sem):
    for o in range(OWNERS):
        rows = slice(8 * o, 8 * o + 8)
        for at in range(2):
            total = keep_ref[at, rows, :] + got_ref[at, rows, :]
            grads_s[o, 16 * at : 16 * at + 16, :] = jnp.concatenate([total[:, :HALF], total[:, HALF:]], axis=0).astype(BF)
    copy = pltpu.make_async_copy(grads_s, a_ref.at[:, pl.ds(144, 32), :], sem)
    copy.start()
    copy.wait()


def chunk_kernel(a_ref, total_ref):
    acc = a_ref[0, 144:176, :].astype(F32)
    for s in range(1, OWNERS):
        acc = acc + a_ref[s, 144:176, :].astype(F32)
    total_ref[...] = acc


def collect_kernel(index_ref, in_ref, out_ref, acc_s):
    acc_s[...] = jnp.zeros_like(acc_s)

    def body(s, carry):
        for slot in range(2):
            i = index_ref[2 * s + slot]
            acc_s[i] += in_ref[s, 64 * slot : 64 * slot + 64, :].astype(F32)
        return carry

    lax.fori_loop(0, OWNERS, body, 0, unroll=4)
    for i in range(TRASH):
        out_ref[RB * i : RB * i + RB, :HALF] = acc_s[i, 0:32, :].astype(BF)
        out_ref[RB * i : RB * i + RB, HALF:] = acc_s[i, 32:64, :].astype(BF)


def unpack_kernel(mine_ref, other_ref, self_ref, inter_ref):
    even = lax.rem(lax.axis_index("rep"), 2) == 0
    for o in range(OWNERS):
        mine = mine_ref[o].astype(F32)
        other = other_ref[o].astype(F32)
        a = jnp.where(even, mine, other)
        b = jnp.where(even, other, mine)
        rows = slice(8 * o, 8 * o + 8)
        for ref, value in ((self_ref, a), (inter_ref, b)):
            ref[1, rows, :HALF] = value[0:8]
            ref[1, rows, HALF:] = value[8:16]
            ref[0, rows, :HALF] = value[16:24]
            ref[0, rows, HALF:] = value[24:32]


def call(kernel, outs, in_specs, scratch=(), aliases=(), params=PARAMS, out_spec=VMEM, **cost):
    return pl.pallas_call(
        kernel,
        out_shape=[jax.ShapeDtypeStruct(s, d) for s, d in outs],
        in_specs=in_specs,
        out_specs=[out_spec] * len(outs),
        scratch_shapes=list(scratch),
        compiler_params=params,
        input_output_aliases=dict(aliases),
        cost_estimate=pl.CostEstimate(transcendentals=0, **cost),
    )


def local(cotangent, pre_two, pre_one, message_two, message_one, users_zero, w_self, w_inter, adjacency, tile_user,
          counts, dest, item_block):
    users = cotangent.shape[0]
    reps = lax.axis_size("rep")
    z_chips = reps // 2
    swap = [(i, i ^ 1) for i in range(reps)]
    dest = dest.reshape(dest.shape[0])

    def along_z(step):
        return [(2 * z + c, 2 * step(z) + c) for z in range(z_chips) for c in range(2)]

    def to_owners(x):
        return lax.all_to_all(x, "owner", split_axis=0, concat_axis=0, tiled=True)

    user = ((users, FEAT), BF)
    both = ((2, FEAT, FEAT), F32)
    ranks = [pltpu.SMEM((OWNERS,), jnp.int32)] * 2
    dmsg2, dmsg1, user_grad, keep, send = call(
        user_kernel,
        [user, user, user, both, both],
        [HBM] * 8,
        [pltpu.VMEM((users, FEAT), BF)] * 6 + [pltpu.VMEM((2, FEAT, FEAT), BF)] * 2
        + [pltpu.VMEM((users, FEAT), BF)] * 6 + [pltpu.SemaphoreType.DMA((8 + 6 * (users // BLK),))],
        params=WIDE, flops=900_000_000, bytes_accessed=6 << 20,
    )(cotangent, pre_two, pre_one, message_two, message_one, users_zero, w_self, w_inter)
    got = lax.ppermute(send, "rep", swap)
    (items,) = call(
        two_kernel, [((OWNERS, 176, HALF), BF)], [SMEM] * 4 + [VMEM] * 2,
        ranks + [pltpu.SMEM((2 * OWNERS,), jnp.int32)], flops=140_000_000, bytes_accessed=2 << 20,
    )(tile_user, counts, dest, item_block, adjacency, dmsg2)
    (a,) = call(
        pack_kernel, [((OWNERS, 176, HALF), BF)], [VMEM, VMEM, ANY],
        [pltpu.VMEM((OWNERS, 32, HALF), BF), pltpu.SemaphoreType.DMA], aliases={2: 0}, out_spec=ANY,
        flops=1_000_000, bytes_accessed=2 << 20,
    )(keep, got, items)
    got_a = to_owners(a)

    (b,) = call(
        one_kernel, [((OWNERS, 128, HALF), BF)], [SMEM] * 3 + [VMEM] * 2, ranks,
        flops=140_000_000, bytes_accessed=2 << 20,
    )(tile_user, counts, dest, adjacency, dmsg1)
    b, got_a = lax.optimization_barrier((b, got_a))
    got_b = to_owners(b)

    (total,) = call(chunk_kernel, [((32, HALF), F32)], [VMEM], flops=1_000_000, bytes_accessed=1 << 18)(got_a)
    total = total + lax.ppermute(total, "rep", along_z(lambda z: z ^ 1))
    total = total + lax.ppermute(total, "rep", along_z(lambda z: z ^ 2))
    total = (
        total
        + lax.ppermute(total, "rep", along_z(lambda z: (z + 4) % z_chips))
        + lax.ppermute(total, "rep", along_z(lambda z: (z + 8) % z_chips))
    )
    index = got_a[:, 128:144:8, 0].astype(jnp.int32).reshape(2 * OWNERS)
    acc = [pltpu.VMEM((TRASH + 1, 64, HALF), F32)]
    item = [((OWNERS * RB, FEAT), BF)]

    def collect(x):
        return call(collect_kernel, item, [SMEM, VMEM], acc, flops=1_000_000, bytes_accessed=3 << 20)(index, x)[0]

    item_one = collect(got_a)
    got_b, total = lax.optimization_barrier((got_b, total))
    mine = to_owners(jnp.broadcast_to(total.astype(BF)[None], (OWNERS, 32, HALF)))
    item_zero = collect(got_b)
    other = lax.ppermute(mine, "rep", swap)
    self_grad, inter_grad = call(
        unpack_kernel, [both] * 2, [VMEM] * 2, flops=1_000_000, bytes_accessed=2 << 20
    )(mine, other)
    return user_grad, item_one, item_zero, self_grad, inter_grad


def solution(mesh):
    both = ("owner", "rep")
    rows = P(both, None)
    return jax.shard_map(
        local,
        mesh=mesh,
        in_specs=(rows,) * 6 + (P(), P(), P(both, None, None), P(both), P(both), rows, P(both)),
        out_specs=(rows, rows, rows, P(), P()),
        check_vma=False,
    )
```

time: 145 us -> 128 us (0.88)
  the two profiles are of different devices: /device:TPU:2 before, /device:TPU:1 now
where the time goes in v2:
time: 128 us
  starting transfers between devices  48.1 us (38%)
  waiting for transfers between devices  43.7 us (34%)
  blocking collectives  19.4 us (15%)
  Pallas kernels  13.8 us (11%)
  local copies, waits for them, and re-layouts  1.31 us (1%)
    all_to_all x2, waiting for transfers between devices, to_owners(): return lax.all_to_all(x, 'owner', split_axis=0, concat_axis=0, tiled=True)  33.3 us
    all_to_all x1, blocking collectives, to_owners(): return lax.all_to_all(x, 'owner', split_axis=0, concat_axis=0, tiled=True)  19.4 us
    ppermute x1, starting transfers between devices, local(): got = lax.ppermute(send, 'rep', swap)  12.6 us
    all_to_all x2, starting transfers between devices, to_owners(): return lax.all_to_all(x, 'owner', split_axis=0, concat_axis=0, tiled=True)  10.5 us
    ppermute x1, starting transfers between devices, local(): lax.ppermute(total, 'rep', along_z(lambda z: (z + 4) % z_chips))  8.93 us
    ppermute x1, starting transfers between devices, local(): other = lax.ppermute(mine, 'rep', swap)  7.52 us
    ppermute x1, waiting for transfers between devices, local(): lax.ppermute(total, 'rep', along_z(lambda z: (z + 8) % z_chips))  5 us
    pallas_call x1, Pallas kernels, local(): call(user_kernel, [user, user, user, both, both], [HBM] * 8, [pltpu.VMEM(...  4.23 us
  transfers between devices with their start and end apart: 8, of which 4 were waited for; matrix products, arithmetic and copies ran while one was open for 1% of the time, Pallas kernels for 6%

profile of v2, /device:TPU:1, one launch (start us, length us, event | category | flops | bytes accessed | tf_op | source)
XLA Modules:
  0.0 127.8 jit_solution(17264269033321491346)
XLA Ops:
  0.6 0.0 copy-start.6
  0.6 0.0 copy-start
  0.7 0.0 copy-start.4
  0.7 0.0 copy-start.5
  0.7 0.0 copy-start.7
  0.7 4.2 %shard_map.164 = (bf16[768,256]{1,0:T(8,128)(2,1)}, bf16[768,256]{1,0:T(8,128)(2,1)}, bf16[768,256]{1,0:T(8,128)(2,1)}, f32[2,256,256]{2,1,0:T(8,128)}, f32[2,256,256]{2,1,0:T(8,128)}) custom-call(bf16[768,256]{1,0:T(8,128)(2,1)} %refs_0_.1, bf16[768,256]{1,0:T(8,128)(2,1)} %refs_1_.1, bf16[768,256]{1,0:T(8,128)(2,1)} %refs_2_.1, bf16[768,256]{1,0:T(8,128)(2,1)} %refs_3_.1, ...), custom_call_target="tpu_custom_call" | custom-call | flops 900000000 | bytes 6291456 | tf_op jit(solution)/shard_map/pallas_call | solution.py:207
  4.9 0.0 copy-start.1
  4.9 12.6 %collective-permute-start = (f32[2,256,256]{2,1,0:T(8,128)}, f32[2,256,256]{2,1,0:T(8,128)S(1)}, u32[]{:S(2)}, u32[]{:S(2)}) collective-permute-start(f32[2,256,256]{2,1,0:T(8,128)} %get-tuple-element.19), channel_id=1, source_target_pairs={{0,1},{1,0},{2,3},{3,2},{4,5},{5,4},{6,7},{7,6},{8,9},{9,8},{10,11... | collective-permute-start | bytes 1572872 | tf_op jit(solution)/shard_map/ppermute | solution.py:215
  17.5 0.0 copy-done.6
  17.5 0.0 copy-done
  17.5 0.0 copy-done.4
  17.5 0.0 copy-done.5
  17.5 0.0 copy-done.7
  17.5 0.0 copy-start.3
  17.6 1.0 copy-done.3
  18.5 2.1 %shard_map.166.items_ref = bf16[32,176,128]{2,1,0:T(8,128)(2,1)} custom-call(s32[4]{0:T(128)S(1)} %copy-done.4, s32[4]{0:T(128)S(1)} %copy-done.5, s32[32]{0:T(128)S(1)} %bitcast.1, s32[32]{0:T(128)S(1)} %copy-done.7, bf16[4,256,256]{2,1,0:T(8,128)(2,1)S(1)} %copy-done, bf16[768,256]{1,0:T(8,128)(2,1)S(1)} %copy-done.3), custom_call_target="tpu_custom_call" | custom-call | flops 140000000 | bytes 2097152 | tf_op jit(solution)/shard_map/pallas_call | solution.py:216
  20.7 0.0 collective-permute-done.got_ref
  20.7 0.0 copy-done.1
  20.7 0.8 shard_map.167
  21.5 0.0 copy-start.2
  21.5 4.1 %all-to-all-start = ((bf16[32,176,128]{2,1,0:T(8,128)(2,1)}), bf16[32,176,128]{2,1,0:T(8,128)(2,1)S(1)}, u32[]{:S(2)}, u32[]{:S(2)}) async-start(bf16[32,176,128]{2,1,0:T(8,128)(2,1)} %shard_map.167), calls=%async_computation | async-start | bytes 2883584 | tf_op jit(solution)/shard_map/all_to_all | solution.py:202
  25.6 0.0 copy-done.2
  25.6 1.9 %shard_map.165 = bf16[32,128,128]{2,1,0:T(8,128)(2,1)} custom-call(s32[4]{0:T(128)S(1)} %copy-done.4, s32[4]{0:T(128)S(1)} %copy-done.5, s32[32]{0:T(128)S(1)} %bitcast.2, bf16[4,256,256]{2,1,0:T(8,128)(2,1)S(1)} %copy-done, bf16[768,256]{1,0:T(8,128)(2,1)S(1)} %copy-done.2), custom_call_target="tpu_custom_call" | custom-call | flops 140000000 | bytes 2097152 | tf_op jit(solution)/shard_map/pallas_call | solution.py:227
  27.6 33.3 %all-to-all-done.in_ref.a_ref = bf16[32,176,128]{2,1,0:T(8,128)(2,1)S(1)} async-done(((bf16[32,176,128]{2,1,0:T(8,128)(2,1)}), bf16[32,176,128]{2,1,0:T(8,128)(2,1)S(1)}, u32[]{:S(2)}, u32[]{:S(2)}) %all-to-all-start) | async-done | bytes 1441824 | tf_op jit(solution)/shard_map/all_to_all | solution.py:202
  60.8 6.4 %all-to-all-start.1 = ((bf16[32,128,128]{2,1,0:T(8,128)(2,1)}), bf16[32,128,128]{2,1,0:T(8,128)(2,1)S(1)}, u32[]{:S(2)}, u32[]{:S(2)}) async-start(bf16[32,128,128]{2,1,0:T(8,128)(2,1)} %shard_map.165), calls=%async_computation.1 | async-start | bytes 2097152 | tf_op jit(solution)/shard_map/all_to_all | solution.py:202
  67.3 1.9 %collective-permute-start.1 = (f32[32,128]{1,0:T(8,128)S(1)}, f32[32,128]{1,0:T(8,128)S(1)}, u32[]{:S(2)}, u32[]{:S(2)}) collective-permute-start(f32[32,128]{1,0:T(8,128)S(1)} %shard_map.169), channel_id=1, source_target_pairs={{0,2},{1,3},{2,0},{3,1},{4,6},{5,7},{6,4},{7,5},{8,10},{9,11},{10,... | collective-permute-start | bytes 49160 | tf_op jit(solution)/shard_map/ppermute | solution.py:235
  69.2 2.6 %collective-permute-done.1 = f32[32,128]{1,0:T(8,128)S(1)} collective-permute-done((f32[32,128]{1,0:T(8,128)S(1)}, f32[32,128]{1,0:T(8,128)S(1)}, u32[]{:S(2)}, u32[]{:S(2)}) %collective-permute-start.1) | collective-permute-done | bytes 16416 | tf_op jit(solution)/shard_map/ppermute | solution.py:235
  71.8 3.0 %collective-permute-start.2 = (f32[32,128]{1,0:T(8,128)S(1)}, f32[32,128]{1,0:T(8,128)S(1)}, u32[]{:S(2)}, u32[]{:S(2)}) collective-permute-start(f32[32,128]{1,0:T(8,128)S(1)} %add.12), channel_id=1, source_target_pairs={{0,4},{1,5},{2,6},{3,7},{4,0},{5,1},{6,2},{7,3},{8,12},{9,13},{10,... | collective-permute-start | bytes 49160 | tf_op jit(solution)/shard_map/ppermute | solution.py:236
  74.8 2.8 %collective-permute-done.2 = f32[32,128]{1,0:T(8,128)S(1)} collective-permute-done((f32[32,128]{1,0:T(8,128)S(1)}, f32[32,128]{1,0:T(8,128)S(1)}, u32[]{:S(2)}, u32[]{:S(2)}) %collective-permute-start.2) | collective-permute-done | bytes 16416 | tf_op jit(solution)/shard_map/ppermute | solution.py:236
  77.6 8.9 %collective-permute-start.3 = (f32[32,128]{1,0:T(8,128)S(1)}, f32[32,128]{1,0:T(8,128)S(1)}, u32[]{:S(2)}, u32[]{:S(2)}) collective-permute-start(f32[32,128]{1,0:T(8,128)S(1)} %add.13), channel_id=1, source_target_pairs={{0,8},{1,9},{2,10},{3,11},{4,12},{5,13},{6,14},{7,15},{8,16},{9,17... | collective-permute-start | bytes 49160 | tf_op jit(solution)/shard_map/ppermute | solution.py:239
  86.6 3.7 %collective-permute-start.4 = (f32[32,128]{1,0:T(8,128)S(1)}, f32[32,128]{1,0:T(8,128)S(1)}, u32[]{:S(2)}, u32[]{:S(2)}) collective-permute-start(f32[32,128]{1,0:T(8,128)S(1)} %add.13), channel_id=1, source_target_pairs={{0,16},{1,17},{2,18},{3,19},{4,20},{5,21},{6,22},{7,23},{8,0},{9,1... | collective-permute-start | bytes 49160 | tf_op jit(solution)/shard_map/ppermute | solution.py:240
  90.2 0.0 collective-permute-done.3
  90.3 5.0 %collective-permute-done.4 = f32[32,128]{1,0:T(8,128)S(1)} collective-permute-done((f32[32,128]{1,0:T(8,128)S(1)}, f32[32,128]{1,0:T(8,128)S(1)}, u32[]{:S(2)}, u32[]{:S(2)}) %collective-permute-start.4) | collective-permute-done | bytes 16416 | tf_op jit(solution)/shard_map/ppermute | solution.py:240
  95.3 0.0 all-to-all-done.1.in_ref
  95.3 19.4 %all_to_all.15.mine_ref = bf16[32,32,128]{2,1,0:T(8,128)(2,1)S(1)} all-to-all(bf16[32,32,128]{2,1,0:T(8,128)(2,1)S(1)} %broadcast_in_dim.2), channel_id=1, replica_groups=mesh['owner'=32,'rep'=24] {'owner'}, dimensions={0} | all-to-all | bytes 524288 | tf_op jit(solution)/shard_map/all_to_all | solution.py:202
  114.7 7.5 %collective-permute-start.5 = (bf16[32,32,128]{2,1,0:T(8,128)(2,1)S(1)}, bf16[32,32,128]{2,1,0:T(8,128)(2,1)S(1)}, u32[]{:S(2)}, u32[]{:S(2)}) collective-permute-start(bf16[32,32,128]{2,1,0:T(8,128)(2,1)S(1)} %all_to_all.15.mine_ref), channel_id=1, source_target_pairs={{0,1},{1,0},{2,3},{3,2},{4,5},{5,4},{6,7},{7,6},{8,9},{9,8},{10,11... | collective-permute-start | bytes 786440 | tf_op jit(solution)/shard_map/ppermute | solution.py:253
  122.3 0.1 slice.3
  122.4 0.6 convert_reduce_fusion
  123.0 0.1 reshape.19.index_ref
  123.1 1.8 %shard_map.168 = bf16[1024,256]{1,0:T(8,128)(2,1)} custom-call(s32[64]{0:T(128)S(1)} %reshape.19.index_ref, bf16[32,176,128]{2,1,0:T(8,128)(2,1)S(1)} %all-to-all-done.in_ref.a_ref), custom_call_target="tpu_custom_call" | custom-call | flops 1000000 | bytes 3145728 | tf_op jit(solution)/shard_map/pallas_call | solution.py:247
  125.0 1.8 %shard_map.170 = bf16[1024,256]{1,0:T(8,128)(2,1)} custom-call(s32[64]{0:T(128)S(1)} %reshape.19.index_ref, bf16[32,128,128]{2,1,0:T(8,128)(2,1)S(1)} %all-to-all-done.1.in_ref), custom_call_target="tpu_custom_call" | custom-call | flops 1000000 | bytes 3145728 | tf_op jit(solution)/shard_map/pallas_call | solution.py:247
  126.8 0.0 collective-permute-done.5.other_ref
  126.8 1.1 shard_map.171
  (5 shorter events, 0.1 us)
Async XLA Ops:
  0.6 16.9 %copy-start.6 = (s32[32,1]{0,1:T(1,128)S(1)}, s32[32,1]{0,1:T(1,128)}, u32[]{:S(2)}) copy-start(s32[32,1]{0,1:T(1,128)} %param.24) | copy-start | bytes 388
  0.6 16.9 %copy-start = (bf16[4,256,256]{2,1,0:T(8,128)(2,1)S(1)}, bf16[4,256,256]{2,1,0:T(8,128)(2,1)}, u32[]{:S(2)}) copy-start(bf16[4,256,256]{2,1,0:T(8,128)(2,1)} %adj_ref.3) | copy-start | bytes 1572868
  0.7 16.9 %copy-start.4 = (s32[4]{0:T(128)S(1)}, s32[4]{0:T(128)}, u32[]{:S(2)}) copy-start(s32[4]{0:T(128)} %user_ref.3) | copy-start | bytes 52
  0.7 16.9 %copy-start.5 = (s32[4]{0:T(128)S(1)}, s32[4]{0:T(128)}, u32[]{:S(2)}) copy-start(s32[4]{0:T(128)} %count_ref.3) | copy-start | bytes 52
  0.7 16.9 %copy-start.7 = (s32[32]{0:T(128)S(1)}, s32[32]{0:T(128)}, u32[]{:S(2)}) copy-start(s32[32]{0:T(128)} %item_ref.1) | copy-start | bytes 388
  4.9 15.8 %copy-start.1 = (f32[2,256,256]{2,1,0:T(8,128)S(1)}, f32[2,256,256]{2,1,0:T(8,128)}, u32[]{:S(2)}) copy-start(f32[2,256,256]{2,1,0:T(8,128)} %get-tuple-element.18.keep_ref) | copy-start | bytes 1572868
  4.9 15.8 %collective-permute-start = (f32[2,256,256]{2,1,0:T(8,128)}, f32[2,256,256]{2,1,0:T(8,128)S(1)}, u32[]{:S(2)}, u32[]{:S(2)}) collective-permute-start(f32[2,256,256]{2,1,0:T(8,128)} %get-tuple-element.19), channel_id=1, source_target_pairs={{0,1},{1,0},{2,3},{3,2},{4,5},{5,4},{6,7},{7,6},{8,9},{9,8},{10,11... | collective-permute-start | bytes 1572872 | tf_op jit(solution)/shard_map/ppermute | solution.py:215
  17.5 1.0 copy-start.3
  21.5 4.1 %copy-start.2 = (bf16[768,256]{1,0:T(8,128)(2,1)S(1)}, bf16[768,256]{1,0:T(8,128)(2,1)}, u32[]{:S(2)}) copy-start(bf16[768,256]{1,0:T(8,128)(2,1)} %get-tuple-element.17.dmsg_ref) | copy-start | bytes 1179652
  21.5 39.4 %all-to-all-start = ((bf16[32,176,128]{2,1,0:T(8,128)(2,1)}), bf16[32,176,128]{2,1,0:T(8,128)(2,1)S(1)}, u32[]{:S(2)}, u32[]{:S(2)}) async-start(bf16[32,176,128]{2,1,0:T(8,128)(2,1)} %shard_map.167), calls=%async_computation | async-start | bytes 2883584 | tf_op jit(solution)/shard_map/all_to_all | solution.py:202
  60.8 34.4 %all-to-all-start.1 = ((bf16[32,128,128]{2,1,0:T(8,128)(2,1)}), bf16[32,128,128]{2,1,0:T(8,128)(2,1)S(1)}, u32[]{:S(2)}, u32[]{:S(2)}) async-start(bf16[32,128,128]{2,1,0:T(8,128)(2,1)} %shard_map.165), calls=%async_computation.1 | async-start | bytes 2097152 | tf_op jit(solution)/shard_map/all_to_all | solution.py:202
  67.3 4.5 %collective-permute-start.1 = (f32[32,128]{1,0:T(8,128)S(1)}, f32[32,128]{1,0:T(8,128)S(1)}, u32[]{:S(2)}, u32[]{:S(2)}) collective-permute-start(f32[32,128]{1,0:T(8,128)S(1)} %shard_map.169), channel_id=1, source_target_pairs={{0,2},{1,3},{2,0},{3,1},{4,6},{5,7},{6,4},{7,5},{8,10},{9,11},{10,... | collective-permute-start | bytes 49160 | tf_op jit(solution)/shard_map/ppermute | solution.py:235
  71.8 5.8 %collective-permute-start.2 = (f32[32,128]{1,0:T(8,128)S(1)}, f32[32,128]{1,0:T(8,128)S(1)}, u32[]{:S(2)}, u32[]{:S(2)}) collective-permute-start(f32[32,128]{1,0:T(8,128)S(1)} %add.12), channel_id=1, source_target_pairs={{0,4},{1,5},{2,6},{3,7},{4,0},{5,1},{6,2},{7,3},{8,12},{9,13},{10,... | collective-permute-start | bytes 49160 | tf_op jit(solution)/shard_map/ppermute | solution.py:236
  77.6 12.6 %collective-permute-start.3 = (f32[32,128]{1,0:T(8,128)S(1)}, f32[32,128]{1,0:T(8,128)S(1)}, u32[]{:S(2)}, u32[]{:S(2)}) collective-permute-start(f32[32,128]{1,0:T(8,128)S(1)} %add.13), channel_id=1, source_target_pairs={{0,8},{1,9},{2,10},{3,11},{4,12},{5,13},{6,14},{7,15},{8,16},{9,17... | collective-permute-start | bytes 49160 | tf_op jit(solution)/shard_map/ppermute | solution.py:239
  86.6 8.7 %collective-permute-start.4 = (f32[32,128]{1,0:T(8,128)S(1)}, f32[32,128]{1,0:T(8,128)S(1)}, u32[]{:S(2)}, u32[]{:S(2)}) collective-permute-start(f32[32,128]{1,0:T(8,128)S(1)} %add.13), channel_id=1, source_target_pairs={{0,16},{1,17},{2,18},{3,19},{4,20},{5,21},{6,22},{7,23},{8,0},{9,1... | collective-permute-start | bytes 49160 | tf_op jit(solution)/shard_map/ppermute | solution.py:240
  114.7 12.0 %collective-permute-start.5 = (bf16[32,32,128]{2,1,0:T(8,128)(2,1)S(1)}, bf16[32,32,128]{2,1,0:T(8,128)(2,1)S(1)}, u32[]{:S(2)}, u32[]{:S(2)}) collective-permute-start(bf16[32,32,128]{2,1,0:T(8,128)(2,1)S(1)} %all_to_all.15.mine_ref), channel_id=1, source_target_pairs={{0,1},{1,0},{2,3},{3,2},{4,5},{5,4},{6,7},{7,6},{8,9},{9,8},{10,11... | collective-permute-start | bytes 786440 | tf_op jit(solution)/shard_map/ppermute | solution.py:253

commit v3 on v2

--- a/solution.py
+++ b/solution.py
@@ -1,3 +1,5 @@
+import functools
+
 import functools
 
 import jax
@@ -16,11 +18,13 @@
 BLK = 256
 OWNERS = 32
 TRASH = 32
+NEAR = 3
 VMEM = pl.BlockSpec(memory_space=pltpu.VMEM)
 SMEM = pl.BlockSpec(memory_space=pltpu.SMEM)
 HBM = pl.BlockSpec(memory_space=pltpu.HBM)
 ANY = pl.BlockSpec(memory_space=pl.ANY)
 PARAMS = pltpu.CompilerParams(vmem_limit_bytes=12 * 1024 * 1024)
+FIT = pltpu.CompilerParams(vmem_limit_bytes=58 * 1024 * 1024)
 WIDE = pltpu.CompilerParams(vmem_limit_bytes=60 * 1024 * 1024)
 
 
@@ -93,7 +97,7 @@
         seen_s[o] = seen_s[o] + 1
 
 
-def tile_terms(user_ref, count_ref, dest_ref, adj_ref, dmsg_ref, rank_s, out_ref):
+def tile_terms(user_ref, count_ref, dest_ref, adj_ref, dmsg_ref, rank_s, store):
     for t in range(adj_ref.shape[0]):
         start = pl.multiple_of(user_ref[t] * BLK, BLK)
         part = tdot(adj_ref[t], dmsg_ref[pl.ds(start, BLK), :])
@@ -101,56 +105,127 @@
         part = jnp.where(live, part, 0.0).astype(BF)
         for b in range(part.shape[0] // RB):
             j = t * (part.shape[0] // RB) + b
-            at = pl.multiple_of(rank_s[j] * 64, 64)
-            block = part[b * RB : (b + 1) * RB, :]
-            out_ref[dest_ref[j], pl.ds(at, RB), :] = block[:, :HALF]
-            out_ref[dest_ref[j], pl.ds(at + RB, RB), :] = block[:, HALF:]
-
-
-def two_kernel(user_ref, count_ref, dest_ref, item_ref, adj_ref, dmsg_ref, a_ref, rank_s, seen_s, tab_s):
+            store(dest_ref[j], rank_s[j], part[b * RB : (b + 1) * RB, :])
+
+
+def two_kernel(user_ref, count_ref, dest_ref, item_ref, adj_hbm, dmsg_hbm, a_ref, b_ref, adj_s, dmsg_s, sems, rank_s,
+               seen_s, tab_s):
+    copies = [pltpu.make_async_copy(dmsg_hbm, dmsg_s, sems.at[0]), pltpu.make_async_copy(adj_hbm, adj_s, sems.at[1])]
+    for copy in copies:
+        copy.start()
     rank_blocks(dest_ref, rank_s, seen_s)
     for i in range(2 * OWNERS):
         tab_s[i] = TRASH
     for j in range(dest_ref.shape[0]):
         tab_s[2 * dest_ref[j] + rank_s[j]] = item_ref[j]
     a_ref[...] = jnp.zeros_like(a_ref)
+    b_ref[...] = jnp.zeros_like(b_ref)
     top = lax.broadcasted_iota(jnp.int32, (16, HALF), 0) < 8
     for o in range(OWNERS):
-        a_ref[o, 128:144, :] = jnp.where(top, tab_s[2 * o], tab_s[2 * o + 1]).astype(F32).astype(BF)
-    tile_terms(user_ref, count_ref, dest_ref, adj_ref, dmsg_ref, rank_s, a_ref)
-
-
-def one_kernel(user_ref, count_ref, dest_ref, adj_ref, dmsg_ref, b_ref, rank_s, seen_s):
+        b_ref[o, 64:80, :] = jnp.where(top, tab_s[2 * o], tab_s[2 * o + 1]).astype(F32).astype(BF)
+    for copy in copies:
+        copy.wait()
+
+    def store(o, rank, block):
+        @pl.when(rank == 0)
+        def _():
+            a_ref[o, 0:32, :] = block[:, :HALF]
+            a_ref[o, 32:64, :] = block[:, HALF:]
+
+        @pl.when(rank != 0)
+        def _():
+            b_ref[o, 0:32, :] = block[:, :HALF]
+            b_ref[o, 32:64, :] = block[:, HALF:]
+
+    tile_terms(user_ref, count_ref, dest_ref, adj_s, dmsg_s, rank_s, store)
+
+
+def one_kernel(user_ref, count_ref, dest_ref, adj_hbm, dmsg_hbm, items_ref, b_ref, c_ref, adj_s, dmsg_s, part_s, sems,
+               rank_s, seen_s):
+    copies = [pltpu.make_async_copy(dmsg_hbm, dmsg_s, sems.at[0]), pltpu.make_async_copy(adj_hbm, adj_s, sems.at[1])]
+    for copy in copies:
+        copy.start()
     rank_blocks(dest_ref, rank_s, seen_s)
-    b_ref[...] = jnp.zeros_like(b_ref)
-    tile_terms(user_ref, count_ref, dest_ref, adj_ref, dmsg_ref, rank_s, b_ref)
-
-
-def pack_kernel(keep_ref, got_ref, items_ref, a_ref, grads_s, sem):
+    part_s[...] = jnp.zeros_like(part_s)
+    c_ref[...] = jnp.zeros_like(c_ref)
+    for copy in copies:
+        copy.wait()
+
+    def store(o, rank, block):
+        @pl.when(rank == 0)
+        def _():
+            c_ref[o, 0:32, :] = block[:, :HALF]
+            c_ref[o, 32:64, :] = block[:, HALF:]
+
+        @pl.when(rank != 0)
+        def _():
+            c_ref[o, 64:96, :] = block[:, :HALF]
+            part_s[o] = block[:, HALF:]
+
+    tile_terms(user_ref, count_ref, dest_ref, adj_s, dmsg_s, rank_s, store)
+    copy = pltpu.make_async_copy(part_s, b_ref.at[:, pl.ds(80, 32), :], sems.at[2])
+    copy.start()
+    copy.wait()
+
+
+def pack_kernel(keep_hbm, got_hbm, items_ref, a_ref, keep_s, got_s, grads_s, sems):
+    copies = [pltpu.make_async_copy(keep_hbm, keep_s, sems.at[0]), pltpu.make_async_copy(got_hbm, got_s, sems.at[1])]
+    for copy in copies:
+        copy.start()
+    for copy in copies:
+        copy.wait()
     for o in range(OWNERS):
         rows = slice(8 * o, 8 * o + 8)
         for at in range(2):
-            total = keep_ref[at, rows, :] + got_ref[at, rows, :]
+            total = keep_s[at, rows, :] + got_s[at, rows, :]
             grads_s[o, 16 * at : 16 * at + 16, :] = jnp.concatenate([total[:, :HALF], total[:, HALF:]], axis=0).astype(BF)
-    copy = pltpu.make_async_copy(grads_s, a_ref.at[:, pl.ds(144, 32), :], sem)
+    copy = pltpu.make_async_copy(grads_s, a_ref.at[:, pl.ds(64, 32), :], sems.at[2])
     copy.start()
     copy.wait()
 
 
 def chunk_kernel(a_ref, total_ref):
-    acc = a_ref[0, 144:176, :].astype(F32)
+    acc = a_ref[0, 64:96, :].astype(F32)
     for s in range(1, OWNERS):
-        acc = acc + a_ref[s, 144:176, :].astype(F32)
+        acc = acc + a_ref[s, 64:96, :].astype(F32)
     total_ref[...] = acc
 
 
-def collect_kernel(index_ref, in_ref, out_ref, acc_s):
+def ordered_sum(position, refs, slots_s):
+    for k, ref in enumerate(refs):
+        slots_s[lax.rem(position + len(refs) - k, len(refs))] = ref[...]
+    total = slots_s[0]
+    for k in range(1, len(refs)):
+        total = total + slots_s[k]
+    return total
+
+
+def near_kernel(*refs):
+    *ins, out_ref, slots_s = refs
+    chip = lax.axis_index("rep") // 2
+    out_ref[...] = ordered_sum(lax.rem(chip, NEAR), ins, slots_s)
+
+
+def far_kernel(*refs):
+    *ins, items_ref, c_ref, slots_s, copies_s, sem = refs
+    chip = lax.axis_index("rep") // 2
+    total = ordered_sum(chip // NEAR, ins, slots_s).astype(BF)
+    for o in range(OWNERS):
+        copies_s[o] = total
+    copy = pltpu.make_async_copy(copies_s, c_ref.at[:, pl.ds(96, 32), :], sem)
+    copy.start()
+    copy.wait()
+
+
+def collect_kernel(cuts, index_ref, *refs):
+    *in_refs, out_ref, acc_s = refs
     acc_s[...] = jnp.zeros_like(acc_s)
 
     def body(s, carry):
-        for slot in range(2):
-            i = index_ref[2 * s + slot]
-            acc_s[i] += in_ref[s, 64 * slot : 64 * slot + 64, :].astype(F32)
+        for ref, pieces in zip(in_refs, cuts):
+            for slot, at, to, rows in pieces:
+                i = index_ref[2 * s + slot]
+                acc_s[i, to : to + rows, :] += ref[s, at : at + rows, :].astype(F32)
         return carry
 
     lax.fori_loop(0, OWNERS, body, 0, unroll=4)
@@ -162,7 +237,7 @@
 def unpack_kernel(mine_ref, other_ref, self_ref, inter_ref):
     even = lax.rem(lax.axis_index("rep"), 2) == 0
     for o in range(OWNERS):
-        mine = mine_ref[o].astype(F32)
+        mine = mine_ref[o, 96:128, :].astype(F32)
         other = other_ref[o].astype(F32)
         a = jnp.where(even, mine, other)
         b = jnp.where(even, other, mine)
@@ -174,12 +249,12 @@
             ref[0, rows, HALF:] = value[24:32]
 
 
-def call(kernel, outs, in_specs, scratch=(), aliases=(), params=PARAMS, out_spec=VMEM, **cost):
+def call(kernel, outs, in_specs, scratch=(), aliases=(), params=PARAMS, out_specs=None, **cost):
     return pl.pallas_call(
         kernel,
         out_shape=[jax.ShapeDtypeStruct(s, d) for s, d in outs],
         in_specs=in_specs,
-        out_specs=[out_spec] * len(outs),
+        out_specs=out_specs or [VMEM] * len(outs),
         scratch_shapes=list(scratch),
         compiler_params=params,
         input_output_aliases=dict(aliases),
@@ -195,15 +270,18 @@
     swap = [(i, i ^ 1) for i in range(reps)]
     dest = dest.reshape(dest.shape[0])
 
-    def along_z(step):
-        return [(2 * z + c, 2 * step(z) + c) for z in range(z_chips) for c in range(2)]
+    def from_z(x, before):
+        return lax.ppermute(x, "rep", [(2 * before(z) + c, 2 * z + c) for z in range(z_chips) for c in range(2)])
 
     def to_owners(x):
         return lax.all_to_all(x, "owner", split_axis=0, concat_axis=0, tiled=True)
 
     user = ((users, FEAT), BF)
     both = ((2, FEAT, FEAT), F32)
+    chunk = ((32, HALF), F32)
+    tiles = [pltpu.VMEM(adjacency.shape, BF), pltpu.VMEM((users, FEAT), BF)]
     ranks = [pltpu.SMEM((OWNERS,), jnp.int32)] * 2
+    small = dict(flops=1_000_000, bytes_accessed=2 << 20)
     dmsg2, dmsg1, user_grad, keep, send = call(
         user_kernel,
         [user, user, user, both, both],
@@ -213,47 +291,52 @@
         params=WIDE, flops=900_000_000, bytes_accessed=6 << 20,
     )(cotangent, pre_two, pre_one, message_two, message_one, users_zero, w_self, w_inter)
     got = lax.ppermute(send, "rep", swap)
-    (items,) = call(
-        two_kernel, [((OWNERS, 176, HALF), BF)], [SMEM] * 4 + [VMEM] * 2,
-        ranks + [pltpu.SMEM((2 * OWNERS,), jnp.int32)], flops=140_000_000, bytes_accessed=2 << 20,
+    a_items, b_items = call(
+        two_kernel, [((OWNERS, 96, HALF), BF), ((OWNERS, 112, HALF), BF)], [SMEM] * 4 + [HBM] * 2,
+        tiles + [pltpu.SemaphoreType.DMA((2,))] + ranks + [pltpu.SMEM((2 * OWNERS,), jnp.int32)],
+        params=WIDE, flops=140_000_000, bytes_accessed=2 << 20,
     )(tile_user, counts, dest, item_block, adjacency, dmsg2)
     (a,) = call(
-        pack_kernel, [((OWNERS, 176, HALF), BF)], [VMEM, VMEM, ANY],
-        [pltpu.VMEM((OWNERS, 32, HALF), BF), pltpu.SemaphoreType.DMA], aliases={2: 0}, out_spec=ANY,
-        flops=1_000_000, bytes_accessed=2 << 20,
-    )(keep, got, items)
+        pack_kernel, [((OWNERS, 96, HALF), BF)], [HBM, HBM, ANY],
+        [pltpu.VMEM(both[0], F32)] * 2 + [pltpu.VMEM((OWNERS, 32, HALF), BF), pltpu.SemaphoreType.DMA((3,))],
+        aliases={2: 0}, out_specs=[ANY], params=FIT, **small,
+    )(keep, got, a_items)
     got_a = to_owners(a)
 
-    (b,) = call(
-        one_kernel, [((OWNERS, 128, HALF), BF)], [SMEM] * 3 + [VMEM] * 2, ranks,
-        flops=140_000_000, bytes_accessed=2 << 20,
-    )(tile_user, counts, dest, adjacency, dmsg1)
+    b, c_items = call(
+        one_kernel, [((OWNERS, 112, HALF), BF), ((OWNERS, 128, HALF), BF)], [SMEM] * 3 + [HBM] * 2 + [ANY],
+        tiles + [pltpu.VMEM((OWNERS, 32, HALF), BF), pltpu.SemaphoreType.DMA((3,))] + ranks,
+        aliases={5: 0}, out_specs=[ANY, VMEM], params=WIDE, flops=140_000_000, bytes_accessed=2 << 20,
+    )(tile_user, counts, dest, adjacency, dmsg1, b_items)
     b, got_a = lax.optimization_barrier((b, got_a))
     got_b = to_owners(b)
 
-    (total,) = call(chunk_kernel, [((32, HALF), F32)], [VMEM], flops=1_000_000, bytes_accessed=1 << 18)(got_a)
-    total = total + lax.ppermute(total, "rep", along_z(lambda z: z ^ 1))
-    total = total + lax.ppermute(total, "rep", along_z(lambda z: z ^ 2))
-    total = (
-        total
-        + lax.ppermute(total, "rep", along_z(lambda z: (z + 4) % z_chips))
-        + lax.ppermute(total, "rep", along_z(lambda z: (z + 8) % z_chips))
-    )
-    index = got_a[:, 128:144:8, 0].astype(jnp.int32).reshape(2 * OWNERS)
-    acc = [pltpu.VMEM((TRASH + 1, 64, HALF), F32)]
-    item = [((OWNERS * RB, FEAT), BF)]
-
-    def collect(x):
-        return call(collect_kernel, item, [SMEM, VMEM], acc, flops=1_000_000, bytes_accessed=3 << 20)(index, x)[0]
-
-    item_one = collect(got_a)
-    got_b, total = lax.optimization_barrier((got_b, total))
-    mine = to_owners(jnp.broadcast_to(total.astype(BF)[None], (OWNERS, 32, HALF)))
-    item_zero = collect(got_b)
-    other = lax.ppermute(mine, "rep", swap)
-    self_grad, inter_grad = call(
-        unpack_kernel, [both] * 2, [VMEM] * 2, flops=1_000_000, bytes_accessed=2 << 20
-    )(mine, other)
+    (total,) = call(chunk_kernel, [chunk], [VMEM], **small)(got_a)
+    near = [total] + [from_z(total, lambda z, k=k: z - z % NEAR + (z + NEAR - k) % NEAR) for k in range(1, NEAR)]
+    (total,) = call(near_kernel, [chunk], [VMEM] * NEAR, [pltpu.VMEM((NEAR, 32, HALF), F32)], **small)(*near)
+    groups = z_chips // NEAR
+    far = [total] + [from_z(total, lambda z, k=k: (z + z_chips - NEAR * k) % z_chips) for k in range(1, groups)]
+    (c,) = call(
+        far_kernel, [((OWNERS, 128, HALF), BF)], [VMEM] * groups + [ANY],
+        [pltpu.VMEM((groups, 32, HALF), F32), pltpu.VMEM((OWNERS, 32, HALF), BF), pltpu.SemaphoreType.DMA],
+        aliases={groups: 0}, out_specs=[ANY], params=FIT, **small,
+    )(*far, c_items)
+    c, got_b = lax.optimization_barrier((c, got_b))
+    got_c = to_owners(c)
+
+    index = got_b[:, 64:80:8, 0].astype(jnp.int32).reshape(2 * OWNERS)
+
+    def collect(cuts, *arrays):
+        return call(
+            functools.partial(collect_kernel, cuts), [((OWNERS * RB, FEAT), BF)], [SMEM] + [VMEM] * len(arrays),
+            [pltpu.VMEM((TRASH + 1, 64, HALF), F32)], **small,
+        )(index, *arrays)[0]
+
+    item_one = collect((((0, 0, 0, 64),), ((1, 0, 0, 64),)), got_a, got_b)
+    got_c, item_one = lax.optimization_barrier((got_c, item_one))
+    other = lax.ppermute(got_c[:, 96:128], "rep", swap)
+    item_zero = collect((((0, 0, 0, 64), (1, 64, 0, 32)), ((1, 80, 32, 32),)), got_c, got_b)
+    self_grad, inter_grad = call(unpack_kernel, [both] * 2, [VMEM] * 2, **small)(got_c, other)
     return user_grad, item_one, item_zero, self_grad, inter_grad
 
 

time: 128 us -> 134 us (1.047)
  blocking collectives: 19.4 us -> 0 us
  starting transfers between devices: 48.1 us -> 67.5 us
  Pallas kernels: 13.8 us -> 21.7 us
  waiting for transfers between devices: 43.7 us -> 41.3 us
    all_to_all x1 -> x0, blocking collectives: 19.4 us -> none  [to_owners(): return lax.all_to_all(x, 'owner', split_axis=0, concat_axis=0, tiled=True)]
    ppermute x5 -> x6, starting transfers between devices: 25.1 us -> 37 us  [the longest x5 27.8 us: from_z(): lax.ppermute(x, 'rep', [(2 * before(z) + c, 2 * z + c) for z in range(z_c...]
    pallas_call x7 -> x9, Pallas kernels: 9.6 us -> 17.6 us  [the longest x1 4.87 us: local(): call(one_kernel, [((OWNERS, 112, HALF), BF), ((OWNERS, 128, HALF), BF)],...]
    all_to_all x2 -> x3, starting transfers between devices: 10.5 us -> 18.1 us  [to_owners(): return lax.all_to_all(x, 'owner', split_axis=0, concat_axis=0, tiled=True)]
    ppermute x5 -> x6, waiting for transfers between devices: 10.4 us -> 4.39 us  [the longest x5 4.39 us: from_z(): lax.ppermute(x, 'rep', [(2 * before(z) + c, 2 * z + c) for z in range(z_c...]
    all_to_all x2 -> x3, waiting for transfers between devices: 33.3 us -> 36.9 us  [to_owners(): return lax.all_to_all(x, 'owner', split_axis=0, concat_axis=0, tiled=True)]
  transfers between devices with their start and end apart: 8 -> 10, of which waited for: 4 -> 5; matrix products, arithmetic and copies ran while one was open for 1% -> 1% of each run, Pallas kernels for 6% -> 11%
where the time goes in v3:
time: 134 us
  starting transfers between devices  67.5 us (50%)
  waiting for transfers between devices  41.3 us (31%)
  Pallas kernels  21.7 us (16%)
  local copies, waits for them, and re-layouts  1.66 us (1%)
    all_to_all x3, waiting for transfers between devices, to_owners(): return lax.all_to_all(x, 'owner', split_axis=0, concat_axis=0, tiled=True)  36.9 us
    ppermute x5, starting transfers between devices, from_z(): lax.ppermute(x, 'rep', [(2 * before(z) + c, 2 * z + c) for z in range(z_c...  27.8 us
    all_to_all x3, starting transfers between devices, to_owners(): return lax.all_to_all(x, 'owner', split_axis=0, concat_axis=0, tiled=True)  18.1 us
    ppermute x1, starting transfers between devices, local(): got = lax.ppermute(send, 'rep', swap)  12.4 us
    ppermute x1, starting transfers between devices, local(): other = lax.ppermute(got_c[:, 96:128], 'rep', swap)  9.16 us
    pallas_call x1, Pallas kernels, local(): call(one_kernel, [((OWNERS, 112, HALF), BF), ((OWNERS, 128, HALF), BF)],...  4.87 us
    pallas_call x1, Pallas kernels, local(): call(two_kernel, [((OWNERS, 96, HALF), BF), ((OWNERS, 112, HALF), BF)], [...  4.4 us
    ppermute x5, waiting for transfers between devices, from_z(): lax.ppermute(x, 'rep', [(2 * before(z) + c, 2 * z + c) for z in range(z_c...  4.39 us
  transfers between devices with their start and end apart: 10, of which 5 were waited for; matrix products, arithmetic and copies ran while one was open for 1% of the time, Pallas kernels for 11%

profile of v3, /device:TPU:1, one launch (start us, length us, event | category | flops | bytes accessed | tf_op | source)
XLA Modules:
  0.0 133.7 jit_solution(2598664967668400160)
XLA Ops:
  0.6 4.2 %shard_map.164 = (bf16[768,256]{1,0:T(8,128)(2,1)}, bf16[768,256]{1,0:T(8,128)(2,1)}, bf16[768,256]{1,0:T(8,128)(2,1)}, f32[2,256,256]{2,1,0:T(8,128)}, f32[2,256,256]{2,1,0:T(8,128)}) custom-call(bf16[768,256]{1,0:T(8,128)(2,1)} %refs_0_.1, bf16[768,256]{1,0:T(8,128)(2,1)} %refs_1_.1, bf16[768,256]{1,0:T(8,128)(2,1)} %refs_2_.1, bf16[768,256]{1,0:T(8,128)(2,1)} %refs_3_.1, ...), custom_call_target="tpu_custom_call" | custom-call | flops 900000000 | bytes 6291456 | tf_op jit(solution)/shard_map/pallas_call | solution.py:285
  4.8 12.4 %collective-permute-start = (f32[2,256,256]{2,1,0:T(8,128)}, f32[2,256,256]{2,1,0:T(8,128)S(1)}, u32[]{:S(2)}, u32[]{:S(2)}) collective-permute-start(f32[2,256,256]{2,1,0:T(8,128)} %get-tuple-element.28), channel_id=1, source_target_pairs={{0,1},{1,0},{2,3},{3,2},{4,5},{5,4},{6,7},{7,6},{8,9},{9,8},{10,11... | collective-permute-start | bytes 1572872 | tf_op jit(solution)/shard_map/ppermute | solution.py:293
  17.2 4.4 %shard_map.165 = (bf16[32,96,128]{2,1,0:T(8,128)(2,1)}, bf16[32,112,128]{2,1,0:T(8,128)(2,1)}) custom-call(s32[4]{0:T(128)} %user_ref.3, s32[4]{0:T(128)} %count_ref.3, s32[32]{0:T(128)} %bitcast.1, s32[32]{0:T(128)} %item_ref.1, bf16[4,256,256]{2,1,0:T(8,128)(2,1)} %adj_hbm.3, bf16[768,256]{1,0:T(8,128)(2,1)} %get-tuple-element.24.dmsg_hbm), custom_call_target="tpu_custom_call" | custom-call | flops 140000000 | bytes 2097152 | tf_op jit(solution)/shard_map/pallas_call | solution.py:294
  21.7 0.0 collective-permute-done.got_hbm
  21.7 0.0 copy-start.1
  21.7 0.8 copy-done.1
  22.5 2.0 %shard_map.167 = bf16[32,96,128]{2,1,0:T(8,128)(2,1)} custom-call(f32[2,256,256]{2,1,0:T(8,128)} %get-tuple-element.27.keep_hbm, f32[2,256,256]{2,1,0:T(8,128)} %copy-done.1, bf16[32,96,128]{2,1,0:T(8,128)(2,1)} %get-tuple-element.29.items_ref), custom_call_target="tpu_custom_call", output_to_operand_aliasing={{}: (2, {})} | custom-call | flops 1000000 | bytes 2097152 | tf_op jit(solution)/shard_map/pallas_call | solution.py:299
  24.5 3.9 %all-to-all-start = ((bf16[32,96,128]{2,1,0:T(8,128)(2,1)}), bf16[32,96,128]{2,1,0:T(8,128)(2,1)S(1)}, u32[]{:S(2)}, u32[]{:S(2)}) async-start(bf16[32,96,128]{2,1,0:T(8,128)(2,1)} %shard_map.167), calls=%async_computation | async-start | bytes 1572864 | tf_op jit(solution)/shard_map/all_to_all | solution.py:277
  28.4 4.9 %shard_map.166 = (bf16[32,112,128]{2,1,0:T(8,128)(2,1)}, bf16[32,128,128]{2,1,0:T(8,128)(2,1)}) custom-call(s32[4]{0:T(128)} %user_ref.3, s32[4]{0:T(128)} %count_ref.3, s32[32]{0:T(128)} %bitcast.2, bf16[4,256,256]{2,1,0:T(8,128)(2,1)} %adj_hbm.3, bf16[768,256]{1,0:T(8,128)(2,1)} %get-tuple-element.23.dmsg_hbm, ...), custom_call_target="tpu_custom_call", output_to_operand_aliasing={{0}: (5, {})} | custom-call | flops 140000000 | bytes 2097152 | tf_op jit(solution)/shard_map/pallas_call | solution.py:306
  33.3 17.7 %all-to-all-done.a_ref.refs_0_ = bf16[32,96,128]{2,1,0:T(8,128)(2,1)S(1)} async-done(((bf16[32,96,128]{2,1,0:T(8,128)(2,1)}), bf16[32,96,128]{2,1,0:T(8,128)(2,1)S(1)}, u32[]{:S(2)}, u32[]{:S(2)}) %all-to-all-start) | async-done | bytes 786464 | tf_op jit(solution)/shard_map/all_to_all | solution.py:277
  51.0 5.0 %all-to-all-start.1 = ((bf16[32,112,128]{2,1,0:T(8,128)(2,1)}), bf16[32,112,128]{2,1,0:T(8,128)(2,1)S(1)}, u32[]{:S(2)}, u32[]{:S(2)}) async-start(bf16[32,112,128]{2,1,0:T(8,128)(2,1)} %get-tuple-element.32), calls=%async_computation.1 | async-start | bytes 1835008 | tf_op jit(solution)/shard_map/all_to_all | solution.py:277
  56.1 2.2 %collective-permute-start.2 = (f32[32,128]{1,0:T(8,128)S(1)}, f32[32,128]{1,0:T(8,128)S(1)}, u32[]{:S(2)}, u32[]{:S(2)}) collective-permute-start(f32[32,128]{1,0:T(8,128)S(1)} %shard_map.168.refs_0_), channel_id=1, source_target_pairs={{2,0},{3,1},{4,2},{5,3},{0,4},{1,5},{8,6},{9,7},{10,8},{11,9},{6,1... | collective-permute-start | bytes 49160 | tf_op jit(solution)/shard_map/ppermute | solution.py:274
  58.2 3.1 %collective-permute-start.1 = (f32[32,128]{1,0:T(8,128)S(1)}, f32[32,128]{1,0:T(8,128)S(1)}, u32[]{:S(2)}, u32[]{:S(2)}) collective-permute-start(f32[32,128]{1,0:T(8,128)S(1)} %shard_map.168.refs_0_), channel_id=1, source_target_pairs={{4,0},{5,1},{0,2},{1,3},{2,4},{3,5},{10,6},{11,7},{6,8},{7,9},{8,1... | collective-permute-start | bytes 49160 | tf_op jit(solution)/shard_map/ppermute | solution.py:274
  61.4 0.0 collective-permute-done.2.refs_2_
  61.4 2.5 %collective-permute-done.1.refs_1_ = f32[32,128]{1,0:T(8,128)S(1)} collective-permute-done((f32[32,128]{1,0:T(8,128)S(1)}, f32[32,128]{1,0:T(8,128)S(1)}, u32[]{:S(2)}, u32[]{:S(2)}) %collective-permute-start.1) | collective-permute-done | bytes 16416 | tf_op jit(solution)/shard_map/ppermute | solution.py:274
  63.9 0.0 copy-start
  63.9 12.5 %collective-permute-start.5 = (f32[32,128]{1,0:T(8,128)S(1)}, f32[32,128]{1,0:T(8,128)S(1)}, u32[]{:S(2)}, u32[]{:S(2)}) collective-permute-start(f32[32,128]{1,0:T(8,128)S(1)} %shard_map.169.refs_0_), channel_id=1, source_target_pairs={{6,0},{7,1},{8,2},{9,3},{10,4},{11,5},{12,6},{13,7},{14,8},{15,9},... | collective-permute-start | bytes 49160 | tf_op jit(solution)/shard_map/ppermute | solution.py:274
  76.4 4.3 %collective-permute-start.4 = (f32[32,128]{1,0:T(8,128)S(1)}, f32[32,128]{1,0:T(8,128)S(1)}, u32[]{:S(2)}, u32[]{:S(2)}) collective-permute-start(f32[32,128]{1,0:T(8,128)S(1)} %shard_map.169.refs_0_), channel_id=1, source_target_pairs={{12,0},{13,1},{14,2},{15,3},{16,4},{17,5},{18,6},{19,7},{20,8},{21... | collective-permute-start | bytes 49160 | tf_op jit(solution)/shard_map/ppermute | solution.py:274
  80.7 5.8 %collective-permute-start.3 = (f32[32,128]{1,0:T(8,128)S(1)}, f32[32,128]{1,0:T(8,128)S(1)}, u32[]{:S(2)}, u32[]{:S(2)}) collective-permute-start(f32[32,128]{1,0:T(8,128)S(1)} %shard_map.169.refs_0_), channel_id=1, source_target_pairs={{18,0},{19,1},{20,2},{21,3},{22,4},{23,5},{0,6},{1,7},{2,8},{3,9},... | collective-permute-start | bytes 49160 | tf_op jit(solution)/shard_map/ppermute | solution.py:274
  86.5 0.0 collective-permute-done.5.refs_3_
  86.5 0.0 copy-start.2
  86.5 0.7 collective-permute-done.4.refs_2_
  87.2 0.0 copy-start.3
  87.2 1.2 collective-permute-done.3.refs_1_
  88.4 0.0 copy-start.4
  88.4 0.0 copy-done
  88.4 0.0 copy-done.2
  88.4 0.0 copy-done.3
  88.4 0.6 copy-done.4
  89.0 1.5 %shard_map.170 = bf16[32,128,128]{2,1,0:T(8,128)(2,1)} custom-call(f32[32,128]{1,0:T(8,128)} %copy-done, f32[32,128]{1,0:T(8,128)} %copy-done.4, f32[32,128]{1,0:T(8,128)} %copy-done.3, f32[32,128]{1,0:T(8,128)} %copy-done.2, bf16[32,128,128]{2,1,0:T(8,128)(2,1)} %get-tuple-element.31.refs_4_), custom_call_target="tpu_custom_call", output_to_operand_aliasing={{}: (4, {})} | custom-call | flops 1000000 | bytes 2097152 | tf_op jit(solution)/shard_map/pallas_call | solution.py:319
  90.5 0.0 all-to-all-done.1.refs_1_
  90.6 9.2 %all-to-all-start.2 = ((bf16[32,128,128]{2,1,0:T(8,128)(2,1)}), bf16[32,128,128]{2,1,0:T(8,128)(2,1)S(1)}, u32[]{:S(2)}, u32[]{:S(2)}) async-start(bf16[32,128,128]{2,1,0:T(8,128)(2,1)} %shard_map.170), calls=%async_computation.2 | async-start | bytes 2097152 | tf_op jit(solution)/shard_map/all_to_all | solution.py:277
  99.7 0.1 slice.6
  99.9 0.6 convert_reduce_fusion
  100.5 0.1 reshape.18.index_ref
  100.6 1.8 %shard_map.171 = bf16[1024,256]{1,0:T(8,128)(2,1)} custom-call(s32[64]{0:T(128)S(1)} %reshape.18.index_ref, bf16[32,96,128]{2,1,0:T(8,128)(2,1)S(1)} %all-to-all-done.a_ref.refs_0_, bf16[32,112,128]{2,1,0:T(8,128)(2,1)S(1)} %all-to-all-done.1.refs_1_), custom_call_target="tpu_custom_call" | custom-call | flops 1000000 | bytes 2097152 | tf_op jit(solution)/shard_map/pallas_call | solution.py:330
  102.4 19.2 %all-to-all-done.2.refs_0_.mine_ref = bf16[32,128,128]{2,1,0:T(8,128)(2,1)S(1)} async-done(((bf16[32,128,128]{2,1,0:T(8,128)(2,1)}), bf16[32,128,128]{2,1,0:T(8,128)(2,1)S(1)}, u32[]{:S(2)}, u32[]{:S(2)}) %all-to-all-start.2) | async-done | bytes 1048608 | tf_op jit(solution)/shard_map/all_to_all | solution.py:277
  121.6 9.2 %collective-permute-start.6 = (bf16[32,32,128]{2,1,0:T(8,128)(2,1)S(1)}, bf16[32,32,128]{2,1,0:T(8,128)(2,1)S(1)}, u32[]{:S(2)}, u32[]{:S(2)}) collective-permute-start(bf16[32,32,128]{2,1,0:T(8,128)(2,1)S(1)} %slice.7), channel_id=1, source_target_pairs={{0,1},{1,0},{2,3},{3,2},{4,5},{5,4},{6,7},{7,6},{8,9},{9,8},{10,11... | collective-permute-start | bytes 786440 | tf_op jit(solution)/shard_map/ppermute | solution.py:337
  130.8 1.9 %shard_map.172 = bf16[1024,256]{1,0:T(8,128)(2,1)} custom-call(s32[64]{0:T(128)S(1)} %reshape.18.index_ref, bf16[32,128,128]{2,1,0:T(8,128)(2,1)S(1)} %all-to-all-done.2.refs_0_.mine_ref, bf16[32,112,128]{2,1,0:T(8,128)(2,1)S(1)} %all-to-all-done.1.refs_1_), custom_call_target="tpu_custom_call" | custom-call | flops 1000000 | bytes 2097152 | tf_op jit(solution)/shard_map/pallas_call | solution.py:330
  132.6 0.0 collective-permute-done.6.other_ref
  132.6 1.1 shard_map.173
  (3 shorter events, 0.1 us)
Async XLA Ops:
  4.8 16.8 %collective-permute-start = (f32[2,256,256]{2,1,0:T(8,128)}, f32[2,256,256]{2,1,0:T(8,128)S(1)}, u32[]{:S(2)}, u32[]{:S(2)}) collective-permute-start(f32[2,256,256]{2,1,0:T(8,128)} %get-tuple-element.28), channel_id=1, source_target_pairs={{0,1},{1,0},{2,3},{3,2},{4,5},{5,4},{6,7},{7,6},{8,9},{9,8},{10,11... | collective-permute-start | bytes 1572872 | tf_op jit(solution)/shard_map/ppermute | solution.py:293
  21.7 0.8 copy-start.1
  24.5 26.5 %all-to-all-start = ((bf16[32,96,128]{2,1,0:T(8,128)(2,1)}), bf16[32,96,128]{2,1,0:T(8,128)(2,1)S(1)}, u32[]{:S(2)}, u32[]{:S(2)}) async-start(bf16[32,96,128]{2,1,0:T(8,128)(2,1)} %shard_map.167), calls=%async_computation | async-start | bytes 1572864 | tf_op jit(solution)/shard_map/all_to_all | solution.py:277
  51.0 39.5 %all-to-all-start.1 = ((bf16[32,112,128]{2,1,0:T(8,128)(2,1)}), bf16[32,112,128]{2,1,0:T(8,128)(2,1)S(1)}, u32[]{:S(2)}, u32[]{:S(2)}) async-start(bf16[32,112,128]{2,1,0:T(8,128)(2,1)} %get-tuple-element.32), calls=%async_computation.1 | async-start | bytes 1835008 | tf_op jit(solution)/shard_map/all_to_all | solution.py:277
  56.1 5.3 %collective-permute-start.2 = (f32[32,128]{1,0:T(8,128)S(1)}, f32[32,128]{1,0:T(8,128)S(1)}, u32[]{:S(2)}, u32[]{:S(2)}) collective-permute-start(f32[32,128]{1,0:T(8,128)S(1)} %shard_map.168.refs_0_), channel_id=1, source_target_pairs={{2,0},{3,1},{4,2},{5,3},{0,4},{1,5},{8,6},{9,7},{10,8},{11,9},{6,1... | collective-permute-start | bytes 49160 | tf_op jit(solution)/shard_map/ppermute | solution.py:274
  58.2 5.7 %collective-permute-start.1 = (f32[32,128]{1,0:T(8,128)S(1)}, f32[32,128]{1,0:T(8,128)S(1)}, u32[]{:S(2)}, u32[]{:S(2)}) collective-permute-start(f32[32,128]{1,0:T(8,128)S(1)} %shard_map.168.refs_0_), channel_id=1, source_target_pairs={{4,0},{5,1},{0,2},{1,3},{2,4},{3,5},{10,6},{11,7},{6,8},{7,9},{8,1... | collective-permute-start | bytes 49160 | tf_op jit(solution)/shard_map/ppermute | solution.py:274
  63.9 24.5 %copy-start = (f32[32,128]{1,0:T(8,128)}, f32[32,128]{1,0:T(8,128)S(1)}, u32[]{:S(2)}) copy-start(f32[32,128]{1,0:T(8,128)S(1)} %shard_map.169.refs_0_) | copy-start | bytes 49156
  63.9 22.6 %collective-permute-start.5 = (f32[32,128]{1,0:T(8,128)S(1)}, f32[32,128]{1,0:T(8,128)S(1)}, u32[]{:S(2)}, u32[]{:S(2)}) collective-permute-start(f32[32,128]{1,0:T(8,128)S(1)} %shard_map.169.refs_0_), channel_id=1, source_target_pairs={{6,0},{7,1},{8,2},{9,3},{10,4},{11,5},{12,6},{13,7},{14,8},{15,9},... | collective-permute-start | bytes 49160 | tf_op jit(solution)/shard_map/ppermute | solution.py:274
  76.4 10.8 %collective-permute-start.4 = (f32[32,128]{1,0:T(8,128)S(1)}, f32[32,128]{1,0:T(8,128)S(1)}, u32[]{:S(2)}, u32[]{:S(2)}) collective-permute-start(f32[32,128]{1,0:T(8,128)S(1)} %shard_map.169.refs_0_), channel_id=1, source_target_pairs={{12,0},{13,1},{14,2},{15,3},{16,4},{17,5},{18,6},{19,7},{20,8},{21... | collective-permute-start | bytes 49160 | tf_op jit(solution)/shard_map/ppermute | solution.py:274
  80.7 7.7 %collective-permute-start.3 = (f32[32,128]{1,0:T(8,128)S(1)}, f32[32,128]{1,0:T(8,128)S(1)}, u32[]{:S(2)}, u32[]{:S(2)}) collective-permute-start(f32[32,128]{1,0:T(8,128)S(1)} %shard_map.169.refs_0_), channel_id=1, source_target_pairs={{18,0},{19,1},{20,2},{21,3},{22,4},{23,5},{0,6},{1,7},{2,8},{3,9},... | collective-permute-start | bytes 49160 | tf_op jit(solution)/shard_map/ppermute | solution.py:274
  86.5 1.9 %copy-start.2 = (f32[32,128]{1,0:T(8,128)}, f32[32,128]{1,0:T(8,128)S(1)}, u32[]{:S(2)}) copy-start(f32[32,128]{1,0:T(8,128)S(1)} %collective-permute-done.5.refs_3_) | copy-start | bytes 49156
  87.2 1.2 copy-start.3
  88.4 0.6 copy-start.4
  90.6 31.0 %all-to-all-start.2 = ((bf16[32,128,128]{2,1,0:T(8,128)(2,1)}), bf16[32,128,128]{2,1,0:T(8,128)(2,1)S(1)}, u32[]{:S(2)}, u32[]{:S(2)}) async-start(bf16[32,128,128]{2,1,0:T(8,128)(2,1)} %shard_map.170), calls=%async_computation.2 | async-start | bytes 2097152 | tf_op jit(solution)/shard_map/all_to_all | solution.py:277
  121.6 11.0 %collective-permute-start.6 = (bf16[32,32,128]{2,1,0:T(8,128)(2,1)S(1)}, bf16[32,32,128]{2,1,0:T(8,128)(2,1)S(1)}, u32[]{:S(2)}, u32[]{:S(2)}) collective-permute-start(bf16[32,32,128]{2,1,0:T(8,128)(2,1)S(1)} %slice.7), channel_id=1, source_target_pairs={{0,1},{1,0},{2,3},{3,2},{4,5},{5,4},{6,7},{7,6},{8,9},{9,8},{10,11... | collective-permute-start | bytes 786440 | tf_op jit(solution)/shard_map/ppermute | solution.py:337

commit v4 on v2

--- a/solution.py
+++ b/solution.py
@@ -1,3 +1,5 @@
+import functools
+
 import functools
 
 import jax
@@ -16,10 +18,10 @@
 BLK = 256
 OWNERS = 32
 TRASH = 32
+NEAR = 4
 VMEM = pl.BlockSpec(memory_space=pltpu.VMEM)
 SMEM = pl.BlockSpec(memory_space=pltpu.SMEM)
 HBM = pl.BlockSpec(memory_space=pltpu.HBM)
-ANY = pl.BlockSpec(memory_space=pl.ANY)
 PARAMS = pltpu.CompilerParams(vmem_limit_bytes=12 * 1024 * 1024)
 WIDE = pltpu.CompilerParams(vmem_limit_bytes=60 * 1024 * 1024)
 
@@ -101,56 +103,77 @@
         part = jnp.where(live, part, 0.0).astype(BF)
         for b in range(part.shape[0] // RB):
             j = t * (part.shape[0] // RB) + b
-            at = pl.multiple_of(rank_s[j] * 64, 64)
             block = part[b * RB : (b + 1) * RB, :]
-            out_ref[dest_ref[j], pl.ds(at, RB), :] = block[:, :HALF]
-            out_ref[dest_ref[j], pl.ds(at + RB, RB), :] = block[:, HALF:]
-
-
-def two_kernel(user_ref, count_ref, dest_ref, item_ref, adj_ref, dmsg_ref, a_ref, rank_s, seen_s, tab_s):
+            out_ref[rank_s[j], dest_ref[j], 0:32, :] = block[:, :HALF]
+            out_ref[rank_s[j], dest_ref[j], 32:64, :] = block[:, HALF:]
+
+
+def two_kernel(user_ref, count_ref, dest_ref, item_ref, adj_ref, dmsg_ref, slots_ref, index_ref, rank_s, seen_s, tab_s):
     rank_blocks(dest_ref, rank_s, seen_s)
     for i in range(2 * OWNERS):
         tab_s[i] = TRASH
     for j in range(dest_ref.shape[0]):
         tab_s[2 * dest_ref[j] + rank_s[j]] = item_ref[j]
-    a_ref[...] = jnp.zeros_like(a_ref)
+    slots_ref[...] = jnp.zeros_like(slots_ref)
     top = lax.broadcasted_iota(jnp.int32, (16, HALF), 0) < 8
     for o in range(OWNERS):
-        a_ref[o, 128:144, :] = jnp.where(top, tab_s[2 * o], tab_s[2 * o + 1]).astype(F32).astype(BF)
-    tile_terms(user_ref, count_ref, dest_ref, adj_ref, dmsg_ref, rank_s, a_ref)
-
-
-def one_kernel(user_ref, count_ref, dest_ref, adj_ref, dmsg_ref, b_ref, rank_s, seen_s):
+        index_ref[o] = jnp.where(top, tab_s[2 * o], tab_s[2 * o + 1]).astype(F32).astype(BF)
+    tile_terms(user_ref, count_ref, dest_ref, adj_ref, dmsg_ref, rank_s, slots_ref)
+
+
+def one_kernel(user_ref, count_ref, dest_ref, adj_ref, dmsg_ref, two_ref, index_ref, b_ref, rest_ref, slots_s, rank_s,
+               seen_s):
     rank_blocks(dest_ref, rank_s, seen_s)
-    b_ref[...] = jnp.zeros_like(b_ref)
-    tile_terms(user_ref, count_ref, dest_ref, adj_ref, dmsg_ref, rank_s, b_ref)
-
-
-def pack_kernel(keep_ref, got_ref, items_ref, a_ref, grads_s, sem):
+    slots_s[...] = jnp.zeros_like(slots_s)
+    tile_terms(user_ref, count_ref, dest_ref, adj_ref, dmsg_ref, rank_s, slots_s)
+    for o in range(OWNERS):
+        b_ref[o, 0:64, :] = two_ref[1, o]
+        b_ref[o, 64:80, :] = index_ref[o]
+        b_ref[o, 80:144, :] = slots_s[0, o]
+        b_ref[o, 144:176, :] = slots_s[1, o, 0:32, :]
+        rest_ref[o] = slots_s[1, o, 32:64, :]
+
+
+def pack_kernel(two_ref, keep_hbm, got_ref, a_ref, keep_ref, sem):
+    copy = pltpu.make_async_copy(keep_hbm, keep_ref, sem)
+    copy.start()
+    for o in range(OWNERS):
+        a_ref[o, 0:64, :] = two_ref[0, o]
+    copy.wait()
     for o in range(OWNERS):
         rows = slice(8 * o, 8 * o + 8)
         for at in range(2):
             total = keep_ref[at, rows, :] + got_ref[at, rows, :]
-            grads_s[o, 16 * at : 16 * at + 16, :] = jnp.concatenate([total[:, :HALF], total[:, HALF:]], axis=0).astype(BF)
-    copy = pltpu.make_async_copy(grads_s, a_ref.at[:, pl.ds(144, 32), :], sem)
-    copy.start()
-    copy.wait()
+            first = 64 + 16 * at
+            a_ref[o, first : first + 16, :] = jnp.concatenate([total[:, :HALF], total[:, HALF:]], axis=0).astype(BF)
 
 
 def chunk_kernel(a_ref, total_ref):
-    acc = a_ref[0, 144:176, :].astype(F32)
+    acc = a_ref[0, 64:96, :].astype(F32)
     for s in range(1, OWNERS):
-        acc = acc + a_ref[s, 144:176, :].astype(F32)
+        acc = acc + a_ref[s, 64:96, :].astype(F32)
     total_ref[...] = acc
 
 
-def collect_kernel(index_ref, in_ref, out_ref, acc_s):
+def last_kernel(own_ref, one_ref, two_ref, rest_ref, c_ref, slots_s):
+    group = lax.axis_index("rep") // (2 * NEAR)
+    for k, ref in enumerate((own_ref, one_ref, two_ref)):
+        slots_s[lax.rem(group + 3 - k, 3)] = ref[...]
+    total = (slots_s[0] + slots_s[1] + slots_s[2]).astype(BF)
+    for o in range(OWNERS):
+        c_ref[o, 0:32, :] = rest_ref[o]
+        c_ref[o, 32:64, :] = total
+
+
+def collect_kernel(cuts, index_ref, *refs):
+    *in_refs, out_ref, acc_s = refs
     acc_s[...] = jnp.zeros_like(acc_s)
 
     def body(s, carry):
-        for slot in range(2):
-            i = index_ref[2 * s + slot]
-            acc_s[i] += in_ref[s, 64 * slot : 64 * slot + 64, :].astype(F32)
+        for ref, pieces in zip(in_refs, cuts):
+            for slot, at, to, rows in pieces:
+                i = index_ref[2 * s + slot]
+                acc_s[i, to : to + rows, :] += ref[s, at : at + rows, :].astype(F32)
         return carry
 
     lax.fori_loop(0, OWNERS, body, 0, unroll=4)
@@ -162,7 +185,7 @@
 def unpack_kernel(mine_ref, other_ref, self_ref, inter_ref):
     even = lax.rem(lax.axis_index("rep"), 2) == 0
     for o in range(OWNERS):
-        mine = mine_ref[o].astype(F32)
+        mine = mine_ref[o, 32:64, :].astype(F32)
         other = other_ref[o].astype(F32)
         a = jnp.where(even, mine, other)
         b = jnp.where(even, other, mine)
@@ -174,15 +197,14 @@
             ref[0, rows, HALF:] = value[24:32]
 
 
-def call(kernel, outs, in_specs, scratch=(), aliases=(), params=PARAMS, out_spec=VMEM, **cost):
+def call(kernel, outs, in_specs, scratch=(), params=PARAMS, **cost):
     return pl.pallas_call(
         kernel,
         out_shape=[jax.ShapeDtypeStruct(s, d) for s, d in outs],
         in_specs=in_specs,
-        out_specs=[out_spec] * len(outs),
+        out_specs=[VMEM] * len(outs),
         scratch_shapes=list(scratch),
         compiler_params=params,
-        input_output_aliases=dict(aliases),
         cost_estimate=pl.CostEstimate(transcendentals=0, **cost),
     )
 
@@ -195,15 +217,21 @@
     swap = [(i, i ^ 1) for i in range(reps)]
     dest = dest.reshape(dest.shape[0])
 
-    def along_z(step):
-        return [(2 * z + c, 2 * step(z) + c) for z in range(z_chips) for c in range(2)]
+    def from_z(x, source):
+        return lax.ppermute(x, "rep", [(2 * source(z) + c, 2 * z + c) for z in range(z_chips) for c in range(2)])
 
     def to_owners(x):
         return lax.all_to_all(x, "owner", split_axis=0, concat_axis=0, tiled=True)
 
+    def rows(n):
+        return ((OWNERS, n, HALF), BF)
+
     user = ((users, FEAT), BF)
     both = ((2, FEAT, FEAT), F32)
+    chunk = ((32, HALF), F32)
     ranks = [pltpu.SMEM((OWNERS,), jnp.int32)] * 2
+    small = dict(flops=1_000_000, bytes_accessed=2 << 20)
+    tile = dict(flops=140_000_000, bytes_accessed=2 << 20)
     dmsg2, dmsg1, user_grad, keep, send = call(
         user_kernel,
         [user, user, user, both, both],
@@ -213,47 +241,43 @@
         params=WIDE, flops=900_000_000, bytes_accessed=6 << 20,
     )(cotangent, pre_two, pre_one, message_two, message_one, users_zero, w_self, w_inter)
     got = lax.ppermute(send, "rep", swap)
-    (items,) = call(
-        two_kernel, [((OWNERS, 176, HALF), BF)], [SMEM] * 4 + [VMEM] * 2,
-        ranks + [pltpu.SMEM((2 * OWNERS,), jnp.int32)], flops=140_000_000, bytes_accessed=2 << 20,
+    two, index_rows = call(
+        two_kernel, [((2, OWNERS, 64, HALF), BF), rows(16)], [SMEM] * 4 + [VMEM] * 2,
+        ranks + [pltpu.SMEM((2 * OWNERS,), jnp.int32)], **tile,
     )(tile_user, counts, dest, item_block, adjacency, dmsg2)
     (a,) = call(
-        pack_kernel, [((OWNERS, 176, HALF), BF)], [VMEM, VMEM, ANY],
-        [pltpu.VMEM((OWNERS, 32, HALF), BF), pltpu.SemaphoreType.DMA], aliases={2: 0}, out_spec=ANY,
-        flops=1_000_000, bytes_accessed=2 << 20,
-    )(keep, got, items)
+        pack_kernel, [rows(96)], [VMEM, HBM, VMEM], [pltpu.VMEM(both[0], F32), pltpu.SemaphoreType.DMA], **small
+    )(two, keep, got)
     got_a = to_owners(a)
 
-    (b,) = call(
-        one_kernel, [((OWNERS, 128, HALF), BF)], [SMEM] * 3 + [VMEM] * 2, ranks,
-        flops=140_000_000, bytes_accessed=2 << 20,
-    )(tile_user, counts, dest, adjacency, dmsg1)
+    b, rest = call(
+        one_kernel, [rows(176), rows(32)], [SMEM] * 3 + [VMEM] * 4,
+        [pltpu.VMEM((2, OWNERS, 64, HALF), BF)] + ranks, **tile,
+    )(tile_user, counts, dest, adjacency, dmsg1, two, index_rows)
     b, got_a = lax.optimization_barrier((b, got_a))
     got_b = to_owners(b)
 
-    (total,) = call(chunk_kernel, [((32, HALF), F32)], [VMEM], flops=1_000_000, bytes_accessed=1 << 18)(got_a)
-    total = total + lax.ppermute(total, "rep", along_z(lambda z: z ^ 1))
-    total = total + lax.ppermute(total, "rep", along_z(lambda z: z ^ 2))
-    total = (
-        total
-        + lax.ppermute(total, "rep", along_z(lambda z: (z + 4) % z_chips))
-        + lax.ppermute(total, "rep", along_z(lambda z: (z + 8) % z_chips))
-    )
-    index = got_a[:, 128:144:8, 0].astype(jnp.int32).reshape(2 * OWNERS)
-    acc = [pltpu.VMEM((TRASH + 1, 64, HALF), F32)]
-    item = [((OWNERS * RB, FEAT), BF)]
-
-    def collect(x):
-        return call(collect_kernel, item, [SMEM, VMEM], acc, flops=1_000_000, bytes_accessed=3 << 20)(index, x)[0]
-
-    item_one = collect(got_a)
-    got_b, total = lax.optimization_barrier((got_b, total))
-    mine = to_owners(jnp.broadcast_to(total.astype(BF)[None], (OWNERS, 32, HALF)))
-    item_zero = collect(got_b)
-    other = lax.ppermute(mine, "rep", swap)
-    self_grad, inter_grad = call(
-        unpack_kernel, [both] * 2, [VMEM] * 2, flops=1_000_000, bytes_accessed=2 << 20
-    )(mine, other)
+    (total,) = call(chunk_kernel, [chunk], [VMEM], **small)(got_a)
+    total = total + from_z(total, lambda z: z ^ 1)
+    total = total + from_z(total, lambda z: z ^ 2)
+    far = [from_z(total, lambda z, k=k: (z + z_chips - NEAR * k) % z_chips) for k in (1, 2)]
+    (c,) = call(last_kernel, [rows(64)], [VMEM] * 4, [pltpu.VMEM((3, 32, HALF), F32)], **small)(total, *far, rest)
+    c, got_b = lax.optimization_barrier((c, got_b))
+    got_c = to_owners(c)
+
+    index = got_b[:, 64:80:8, 0].astype(jnp.int32).reshape(2 * OWNERS)
+
+    def collect(cuts, *arrays):
+        return call(
+            functools.partial(collect_kernel, cuts), [((OWNERS * RB, FEAT), BF)], [SMEM] + [VMEM] * len(arrays),
+            [pltpu.VMEM((TRASH + 1, 64, HALF), F32)], **small,
+        )(index, *arrays)[0]
+
+    item_one = collect((((0, 0, 0, 64),), ((1, 0, 0, 64),)), got_a, got_b)
+    got_c, item_one = lax.optimization_barrier((got_c, item_one))
+    other = lax.ppermute(got_c[:, 32:64], "rep", swap)
+    item_zero = collect((((0, 80, 0, 64), (1, 144, 0, 32)), ((1, 0, 32, 32),)), got_b, got_c)
+    self_grad, inter_grad = call(unpack_kernel, [both] * 2, [VMEM] * 2, **small)(got_c, other)
     return user_grad, item_one, item_zero, self_grad, inter_grad
 
 

time: 128 us -> 119 us (0.930)
  blocking collectives: 19.4 us -> 0 us
  starting transfers between devices: 48.1 us -> 53.6 us
  waiting for transfers between devices: 43.7 us -> 46.5 us
  local copies, waits for them, and re-layouts: 1.31 us -> 3.44 us
    all_to_all x1 -> x0, blocking collectives: 19.4 us -> none  [to_owners(): return lax.all_to_all(x, 'owner', split_axis=0, concat_axis=0, tiled=True)]
    all_to_all x2 -> x3, starting transfers between devices: 10.5 us -> 15.7 us  [to_owners(): return lax.all_to_all(x, 'owner', split_axis=0, concat_axis=0, tiled=True)]
    unnamed x16 -> x18, local copies, waits for them, and re-layouts: 1.02 us -> 3.18 us
    ppermute x5, waiting for transfers between devices: 10.4 us -> 12.4 us  [the longest x4 12.4 us: from_z(): lax.ppermute(x, 'rep', [(2 * source(z) + c, 2 * z + c) for z in range(z_c...]
    all_to_all x2 -> x3, waiting for transfers between devices: 33.3 us -> 34.2 us  [to_owners(): return lax.all_to_all(x, 'owner', split_axis=0, concat_axis=0, tiled=True)]
    pallas_call x7 -> x8, Pallas kernels: 9.6 us -> 8.79 us  [the longest x2 3.67 us: collect(): call(functools.partial(collect_kernel, cuts), [((OWNERS * RB, FEAT), BF)]...]
  transfers between devices with their start and end apart: 8 -> 9, of which waited for: 4 -> 6; matrix products, arithmetic and copies ran while one was open for 1% -> 1% of each run, Pallas kernels for 6% -> 6%
where the time goes in v4:
time: 119 us; the launch traced here: 118 us
  starting transfers between devices  53.6 us (45%)
  waiting for transfers between devices  46.5 us (39%)
  Pallas kernels  13 us (11%)
  local copies, waits for them, and re-layouts  3.44 us (3%)
    all_to_all x3, waiting for transfers between devices, to_owners(): return lax.all_to_all(x, 'owner', split_axis=0, concat_axis=0, tiled=True)  34.2 us
    ppermute x4, starting transfers between devices, from_z(): lax.ppermute(x, 'rep', [(2 * source(z) + c, 2 * z + c) for z in range(z_c...  17 us
    all_to_all x3, starting transfers between devices, to_owners(): return lax.all_to_all(x, 'owner', split_axis=0, concat_axis=0, tiled=True)  15.7 us
    ppermute x1, starting transfers between devices, local(): got = lax.ppermute(send, 'rep', swap)  12.4 us
    ppermute x4, waiting for transfers between devices, from_z(): lax.ppermute(x, 'rep', [(2 * source(z) + c, 2 * z + c) for z in range(z_c...  12.4 us
    ppermute x1, starting transfers between devices, local(): other = lax.ppermute(got_c[:, 32:64], 'rep', swap)  8.42 us
    pallas_call x1, Pallas kernels, local(): call(user_kernel, [user, user, user, both, both], [HBM] * 8, [pltpu.VMEM(...  4.22 us
    pallas_call x2, Pallas kernels, collect(): call(functools.partial(collect_kernel, cuts), [((OWNERS * RB, FEAT), BF)]...  3.67 us
  transfers between devices with their start and end apart: 9, of which 6 were waited for; matrix products, arithmetic and copies ran while one was open for 1% of the time, Pallas kernels for 6%

profile of v4, /device:TPU:1, one launch (start us, length us, event | category | flops | bytes accessed | tf_op | source)
XLA Modules:
  0.0 118.1 jit_solution(7069732114407680450)
XLA Ops:
  0.6 0.0 copy-start.6
  0.6 0.0 copy-start.5
  0.7 0.0 copy-start
  0.7 0.0 copy-start.8
  0.7 0.0 copy-start.7
  0.7 4.2 %shard_map.164 = (bf16[768,256]{1,0:T(8,128)(2,1)}, bf16[768,256]{1,0:T(8,128)(2,1)}, bf16[768,256]{1,0:T(8,128)(2,1)}, f32[2,256,256]{2,1,0:T(8,128)}, f32[2,256,256]{2,1,0:T(8,128)}) custom-call(bf16[768,256]{1,0:T(8,128)(2,1)} %refs_0_.1, bf16[768,256]{1,0:T(8,128)(2,1)} %refs_1_.1, bf16[768,256]{1,0:T(8,128)(2,1)} %refs_2_.1, bf16[768,256]{1,0:T(8,128)(2,1)} %refs_3_.1, ...), custom_call_target="tpu_custom_call" | custom-call | flops 900000000 | bytes 6291456 | tf_op jit(solution)/shard_map/pallas_call | solution.py:235
  4.9 12.4 %collective-permute-start = (f32[2,256,256]{2,1,0:T(8,128)}, f32[2,256,256]{2,1,0:T(8,128)S(1)}, u32[]{:S(2)}, u32[]{:S(2)}) collective-permute-start(f32[2,256,256]{2,1,0:T(8,128)} %get-tuple-element.29), channel_id=1, source_target_pairs={{0,1},{1,0},{2,3},{3,2},{4,5},{5,4},{6,7},{7,6},{8,9},{9,8},{10,11... | collective-permute-start | bytes 1572872 | tf_op jit(solution)/shard_map/ppermute | solution.py:243
  17.4 0.0 copy-done.6
  17.4 0.0 copy-done.5
  17.4 0.0 copy-done
  17.4 0.0 copy-done.8
  17.4 0.0 copy-done.7
  17.4 0.0 copy-start.4
  17.4 1.0 copy-done.4
  18.4 1.1 shard_map.165
  19.5 0.0 collective-permute-done.got_ref
  19.5 0.0 copy-start.2
  19.5 1.0 copy-done.2
  20.5 1.0 shard_map.167
  21.5 0.0 copy-start.3
  21.6 4.1 %all-to-all-start = ((bf16[32,96,128]{2,1,0:T(8,128)(2,1)}), bf16[32,96,128]{2,1,0:T(8,128)(2,1)S(1)}, u32[]{:S(2)}, u32[]{:S(2)}) async-start(bf16[32,96,128]{2,1,0:T(8,128)(2,1)} %shard_map.167), calls=%async_computation | async-start | bytes 1572864 | tf_op jit(solution)/shard_map/all_to_all | solution.py:224
  25.6 0.0 copy-done.3
  25.6 1.1 shard_map.166
  26.7 0.0 copy-start.1
  26.7 1.1 copy-done.1
  27.8 20.4 %all-to-all-done.a_ref.refs_0_ = bf16[32,96,128]{2,1,0:T(8,128)(2,1)S(1)} async-done(((bf16[32,96,128]{2,1,0:T(8,128)(2,1)}), bf16[32,96,128]{2,1,0:T(8,128)(2,1)S(1)}, u32[]{:S(2)}, u32[]{:S(2)}) %all-to-all-start) | async-done | bytes 786464 | tf_op jit(solution)/shard_map/all_to_all | solution.py:224
  48.2 5.0 %all-to-all-start.1 = ((bf16[32,176,128]{2,1,0:T(8,128)(2,1)}), bf16[32,176,128]{2,1,0:T(8,128)(2,1)S(1)}, u32[]{:S(2)}, u32[]{:S(2)}) async-start(bf16[32,176,128]{2,1,0:T(8,128)(2,1)} %copy-done.1), calls=%async_computation.1 | async-start | bytes 2883584 | tf_op jit(solution)/shard_map/all_to_all | solution.py:224
  53.3 1.9 %collective-permute-start.1 = (f32[32,128]{1,0:T(8,128)S(1)}, f32[32,128]{1,0:T(8,128)S(1)}, u32[]{:S(2)}, u32[]{:S(2)}) collective-permute-start(f32[32,128]{1,0:T(8,128)S(1)} %shard_map.168), channel_id=1, source_target_pairs={{2,0},{3,1},{0,2},{1,3},{6,4},{7,5},{4,6},{5,7},{10,8},{11,9},{8,1... | collective-permute-start | bytes 49160 | tf_op jit(solution)/shard_map/ppermute | solution.py:221
  55.2 2.6 %collective-permute-done.1 = f32[32,128]{1,0:T(8,128)S(1)} collective-permute-done((f32[32,128]{1,0:T(8,128)S(1)}, f32[32,128]{1,0:T(8,128)S(1)}, u32[]{:S(2)}, u32[]{:S(2)}) %collective-permute-start.1) | collective-permute-done | bytes 16416 | tf_op jit(solution)/shard_map/ppermute | solution.py:221
  57.8 2.8 %collective-permute-start.2 = (f32[32,128]{1,0:T(8,128)S(1)}, f32[32,128]{1,0:T(8,128)S(1)}, u32[]{:S(2)}, u32[]{:S(2)}) collective-permute-start(f32[32,128]{1,0:T(8,128)S(1)} %add.6), channel_id=1, source_target_pairs={{4,0},{5,1},{6,2},{7,3},{0,4},{1,5},{2,6},{3,7},{12,8},{13,9},{14,... | collective-permute-start | bytes 49160 | tf_op jit(solution)/shard_map/ppermute | solution.py:221
  60.6 3.1 %collective-permute-done.2 = f32[32,128]{1,0:T(8,128)S(1)} collective-permute-done((f32[32,128]{1,0:T(8,128)S(1)}, f32[32,128]{1,0:T(8,128)S(1)}, u32[]{:S(2)}, u32[]{:S(2)}) %collective-permute-start.2) | collective-permute-done | bytes 16416 | tf_op jit(solution)/shard_map/ppermute | solution.py:221
  63.6 10.4 %collective-permute-start.4 = (f32[32,128]{1,0:T(8,128)S(1)}, f32[32,128]{1,0:T(8,128)S(1)}, u32[]{:S(2)}, u32[]{:S(2)}) collective-permute-start(f32[32,128]{1,0:T(8,128)S(1)} %add.7.own_ref), channel_id=1, source_target_pairs={{8,0},{9,1},{10,2},{11,3},{12,4},{13,5},{14,6},{15,7},{16,8},{17,9... | collective-permute-start | bytes 49160 | tf_op jit(solution)/shard_map/ppermute | solution.py:221
  74.1 1.9 %collective-permute-start.3 = (f32[32,128]{1,0:T(8,128)S(1)}, f32[32,128]{1,0:T(8,128)S(1)}, u32[]{:S(2)}, u32[]{:S(2)}) collective-permute-start(f32[32,128]{1,0:T(8,128)S(1)} %add.7.own_ref), channel_id=1, source_target_pairs={{16,0},{17,1},{18,2},{19,3},{20,4},{21,5},{22,6},{23,7},{0,8},{1,9... | collective-permute-start | bytes 49160 | tf_op jit(solution)/shard_map/ppermute | solution.py:221
  76.0 0.0 collective-permute-done.4.two_ref
  76.0 6.7 %collective-permute-done.3.one_ref = f32[32,128]{1,0:T(8,128)S(1)} collective-permute-done((f32[32,128]{1,0:T(8,128)S(1)}, f32[32,128]{1,0:T(8,128)S(1)}, u32[]{:S(2)}, u32[]{:S(2)}) %collective-permute-start.3) | collective-permute-done | bytes 16416 | tf_op jit(solution)/shard_map/ppermute | solution.py:221
  82.8 0.9 shard_map.169
  83.6 3.6 %all-to-all-done.1.refs_1_.refs_0_ = bf16[32,176,128]{2,1,0:T(8,128)(2,1)S(1)} async-done(((bf16[32,176,128]{2,1,0:T(8,128)(2,1)}), bf16[32,176,128]{2,1,0:T(8,128)(2,1)S(1)}, u32[]{:S(2)}, u32[]{:S(2)}) %all-to-all-start.1) | async-done | bytes 1441824 | tf_op jit(solution)/shard_map/all_to_all | solution.py:224
  87.3 6.6 %all-to-all-start.2 = ((bf16[32,64,128]{2,1,0:T(8,128)(2,1)}), bf16[32,64,128]{2,1,0:T(8,128)(2,1)S(1)}, u32[]{:S(2)}, u32[]{:S(2)}) async-start(bf16[32,64,128]{2,1,0:T(8,128)(2,1)} %shard_map.169), calls=%async_computation.2 | async-start | bytes 1048576 | tf_op jit(solution)/shard_map/all_to_all | solution.py:224
  93.9 0.1 slice.6
  94.0 0.6 convert_reduce_fusion
  94.6 0.1 reshape.18.index_ref
  94.7 1.8 %shard_map.170 = bf16[1024,256]{1,0:T(8,128)(2,1)} custom-call(s32[64]{0:T(128)S(1)} %reshape.18.index_ref, bf16[32,96,128]{2,1,0:T(8,128)(2,1)S(1)} %all-to-all-done.a_ref.refs_0_, bf16[32,176,128]{2,1,0:T(8,128)(2,1)S(1)} %all-to-all-done.1.refs_1_.refs_0_), custom_call_target="tpu_custom_call" | custom-call | flops 1000000 | bytes 2097152 | tf_op jit(solution)/shard_map/pallas_call | solution.py:271
  96.5 10.2 %all-to-all-done.2.refs_1_.mine_ref = bf16[32,64,128]{2,1,0:T(8,128)(2,1)S(1)} async-done(((bf16[32,64,128]{2,1,0:T(8,128)(2,1)}), bf16[32,64,128]{2,1,0:T(8,128)(2,1)S(1)}, u32[]{:S(2)}, u32[]{:S(2)}) %all-to-all-start.2) | async-done | bytes 524320 | tf_op jit(solution)/shard_map/all_to_all | solution.py:224
  106.7 8.4 %collective-permute-start.5 = (bf16[32,32,128]{2,1,0:T(8,128)(2,1)S(1)}, bf16[32,32,128]{2,1,0:T(8,128)(2,1)S(1)}, u32[]{:S(2)}, u32[]{:S(2)}) collective-permute-start(bf16[32,32,128]{2,1,0:T(8,128)(2,1)S(1)} %slice.7), channel_id=1, source_target_pairs={{0,1},{1,0},{2,3},{3,2},{4,5},{5,4},{6,7},{7,6},{8,9},{9,8},{10,11... | collective-permute-start | bytes 786440 | tf_op jit(solution)/shard_map/ppermute | solution.py:278
  115.1 1.9 %shard_map.171 = bf16[1024,256]{1,0:T(8,128)(2,1)} custom-call(s32[64]{0:T(128)S(1)} %reshape.18.index_ref, bf16[32,176,128]{2,1,0:T(8,128)(2,1)S(1)} %all-to-all-done.1.refs_1_.refs_0_, bf16[32,64,128]{2,1,0:T(8,128)(2,1)S(1)} %all-to-all-done.2.refs_1_.mine_ref), custom_call_target="tpu_custom_call" | custom-call | flops 1000000 | bytes 2097152 | tf_op jit(solution)/shard_map/pallas_call | solution.py:271
  117.0 0.0 collective-permute-done.5.other_ref
  117.0 1.1 shard_map.172
  (4 shorter events, 0.1 us)
Async XLA Ops:
  0.6 16.7 %copy-start.6 = (s32[4]{0:T(128)S(1)}, s32[4]{0:T(128)}, u32[]{:S(2)}) copy-start(s32[4]{0:T(128)} %count_ref.3) | copy-start | bytes 52
  0.6 16.7 %copy-start.5 = (s32[4]{0:T(128)S(1)}, s32[4]{0:T(128)}, u32[]{:S(2)}) copy-start(s32[4]{0:T(128)} %user_ref.3) | copy-start | bytes 52
  0.7 16.7 %copy-start = (bf16[4,256,256]{2,1,0:T(8,128)(2,1)S(1)}, bf16[4,256,256]{2,1,0:T(8,128)(2,1)}, u32[]{:S(2)}) copy-start(bf16[4,256,256]{2,1,0:T(8,128)(2,1)} %adj_ref.3) | copy-start | bytes 1572868
  0.7 16.7 %copy-start.8 = (s32[32]{0:T(128)S(1)}, s32[32]{0:T(128)}, u32[]{:S(2)}) copy-start(s32[32]{0:T(128)} %item_ref.1) | copy-start | bytes 388
  0.7 16.7 %copy-start.7 = (s32[32,1]{0,1:T(1,128)S(1)}, s32[32,1]{0,1:T(1,128)}, u32[]{:S(2)}) copy-start(s32[32,1]{0,1:T(1,128)} %param.24) | copy-start | bytes 388
  4.9 14.6 %collective-permute-start = (f32[2,256,256]{2,1,0:T(8,128)}, f32[2,256,256]{2,1,0:T(8,128)S(1)}, u32[]{:S(2)}, u32[]{:S(2)}) collective-permute-start(f32[2,256,256]{2,1,0:T(8,128)} %get-tuple-element.29), channel_id=1, source_target_pairs={{0,1},{1,0},{2,3},{3,2},{4,5},{5,4},{6,7},{7,6},{8,9},{9,8},{10,11... | collective-permute-start | bytes 1572872 | tf_op jit(solution)/shard_map/ppermute | solution.py:243
  17.4 1.0 copy-start.4
  19.5 1.0 copy-start.2
  21.5 4.1 %copy-start.3 = (bf16[768,256]{1,0:T(8,128)(2,1)S(1)}, bf16[768,256]{1,0:T(8,128)(2,1)}, u32[]{:S(2)}) copy-start(bf16[768,256]{1,0:T(8,128)(2,1)} %get-tuple-element.23.dmsg_ref) | copy-start | bytes 1179652
  21.6 26.7 %all-to-all-start = ((bf16[32,96,128]{2,1,0:T(8,128)(2,1)}), bf16[32,96,128]{2,1,0:T(8,128)(2,1)S(1)}, u32[]{:S(2)}, u32[]{:S(2)}) async-start(bf16[32,96,128]{2,1,0:T(8,128)(2,1)} %shard_map.167), calls=%async_computation | async-start | bytes 1572864 | tf_op jit(solution)/shard_map/all_to_all | solution.py:224
  26.7 1.1 copy-start.1
  48.2 39.0 %all-to-all-start.1 = ((bf16[32,176,128]{2,1,0:T(8,128)(2,1)}), bf16[32,176,128]{2,1,0:T(8,128)(2,1)S(1)}, u32[]{:S(2)}, u32[]{:S(2)}) async-start(bf16[32,176,128]{2,1,0:T(8,128)(2,1)} %copy-done.1), calls=%async_computation.1 | async-start | bytes 2883584 | tf_op jit(solution)/shard_map/all_to_all | solution.py:224
  53.3 4.5 %collective-permute-start.1 = (f32[32,128]{1,0:T(8,128)S(1)}, f32[32,128]{1,0:T(8,128)S(1)}, u32[]{:S(2)}, u32[]{:S(2)}) collective-permute-start(f32[32,128]{1,0:T(8,128)S(1)} %shard_map.168), channel_id=1, source_target_pairs={{2,0},{3,1},{0,2},{1,3},{6,4},{7,5},{4,6},{5,7},{10,8},{11,9},{8,1... | collective-permute-start | bytes 49160 | tf_op jit(solution)/shard_map/ppermute | solution.py:221
  57.8 5.8 %collective-permute-start.2 = (f32[32,128]{1,0:T(8,128)S(1)}, f32[32,128]{1,0:T(8,128)S(1)}, u32[]{:S(2)}, u32[]{:S(2)}) collective-permute-start(f32[32,128]{1,0:T(8,128)S(1)} %add.6), channel_id=1, source_target_pairs={{4,0},{5,1},{6,2},{7,3},{0,4},{1,5},{2,6},{3,7},{12,8},{13,9},{14,... | collective-permute-start | bytes 49160 | tf_op jit(solution)/shard_map/ppermute | solution.py:221
  63.6 12.4 %collective-permute-start.4 = (f32[32,128]{1,0:T(8,128)S(1)}, f32[32,128]{1,0:T(8,128)S(1)}, u32[]{:S(2)}, u32[]{:S(2)}) collective-permute-start(f32[32,128]{1,0:T(8,128)S(1)} %add.7.own_ref), channel_id=1, source_target_pairs={{8,0},{9,1},{10,2},{11,3},{12,4},{13,5},{14,6},{15,7},{16,8},{17,9... | collective-permute-start | bytes 49160 | tf_op jit(solution)/shard_map/ppermute | solution.py:221
  74.1 8.7 %collective-permute-start.3 = (f32[32,128]{1,0:T(8,128)S(1)}, f32[32,128]{1,0:T(8,128)S(1)}, u32[]{:S(2)}, u32[]{:S(2)}) collective-permute-start(f32[32,128]{1,0:T(8,128)S(1)} %add.7.own_ref), channel_id=1, source_target_pairs={{16,0},{17,1},{18,2},{19,3},{20,4},{21,5},{22,6},{23,7},{0,8},{1,9... | collective-permute-start | bytes 49160 | tf_op jit(solution)/shard_map/ppermute | solution.py:221
  87.3 19.4 %all-to-all-start.2 = ((bf16[32,64,128]{2,1,0:T(8,128)(2,1)}), bf16[32,64,128]{2,1,0:T(8,128)(2,1)S(1)}, u32[]{:S(2)}, u32[]{:S(2)}) async-start(bf16[32,64,128]{2,1,0:T(8,128)(2,1)} %shard_map.169), calls=%async_computation.2 | async-start | bytes 1048576 | tf_op jit(solution)/shard_map/all_to_all | solution.py:224
  106.7 10.3 %collective-permute-start.5 = (bf16[32,32,128]{2,1,0:T(8,128)(2,1)S(1)}, bf16[32,32,128]{2,1,0:T(8,128)(2,1)S(1)}, u32[]{:S(2)}, u32[]{:S(2)}) collective-permute-start(bf16[32,32,128]{2,1,0:T(8,128)(2,1)S(1)} %slice.7), channel_id=1, source_target_pairs={{0,1},{1,0},{2,3},{3,2},{4,5},{5,4},{6,7},{7,6},{8,9},{9,8},{10,11... | collective-permute-start | bytes 786440 | tf_op jit(solution)/shard_map/ppermute | solution.py:278

commit v5 on v4

--- a/solution.py
+++ b/solution.py
@@ -17,6 +17,10 @@
 HALF = 128
 BLK = 256
 OWNERS = 32
+XS = 4
+YS = 8
+INDEX = 128 * XS
+ONES = INDEX + 16 * XS
 TRASH = 32
 NEAR = 4
 VMEM = pl.BlockSpec(memory_space=pltpu.VMEM)
@@ -86,16 +90,18 @@
         send_ref[at] = jnp.where(even, grad_inter, grad_self)
 
 
-def rank_blocks(dest_ref, rank_s, seen_s):
+def place_blocks(dest_ref, rank_s, place_s, seen_s):
+    here = lax.rem(lax.axis_index("owner"), XS)
     for o in range(OWNERS):
         seen_s[o] = 0
     for j in range(dest_ref.shape[0]):
         o = dest_ref[j]
         rank_s[j] = seen_s[o]
         seen_s[o] = seen_s[o] + 1
-
-
-def tile_terms(user_ref, count_ref, dest_ref, adj_ref, dmsg_ref, rank_s, out_ref):
+        place_s[j] = lax.rem(lax.rem(o, XS) + XS - here, XS) * YS + o // XS
+
+
+def tile_terms(user_ref, count_ref, adj_ref, dmsg_ref, rank_s, place_s, out_ref):
     for t in range(adj_ref.shape[0]):
         start = pl.multiple_of(user_ref[t] * BLK, BLK)
         part = tdot(adj_ref[t], dmsg_ref[pl.ds(start, BLK), :])
@@ -104,79 +110,91 @@
         for b in range(part.shape[0] // RB):
             j = t * (part.shape[0] // RB) + b
             block = part[b * RB : (b + 1) * RB, :]
-            out_ref[rank_s[j], dest_ref[j], 0:32, :] = block[:, :HALF]
-            out_ref[rank_s[j], dest_ref[j], 32:64, :] = block[:, HALF:]
-
-
-def two_kernel(user_ref, count_ref, dest_ref, item_ref, adj_ref, dmsg_ref, slots_ref, index_ref, rank_s, seen_s, tab_s):
-    rank_blocks(dest_ref, rank_s, seen_s)
+            out_ref[rank_s[j], place_s[j], 0:32, :] = block[:, :HALF]
+            out_ref[rank_s[j], place_s[j], 32:64, :] = block[:, HALF:]
+
+
+def two_kernel(user_ref, count_ref, dest_ref, item_ref, adj_ref, dmsg_ref, *refs):
+    *out_refs, slots_s, rank_s, place_s, seen_s, tab_s = refs
+    place_blocks(dest_ref, rank_s, place_s, seen_s)
     for i in range(2 * OWNERS):
         tab_s[i] = TRASH
     for j in range(dest_ref.shape[0]):
-        tab_s[2 * dest_ref[j] + rank_s[j]] = item_ref[j]
-    slots_ref[...] = jnp.zeros_like(slots_ref)
+        tab_s[2 * place_s[j] + rank_s[j]] = item_ref[j]
+    slots_s[...] = jnp.zeros_like(slots_s)
+    tile_terms(user_ref, count_ref, adj_ref, dmsg_ref, rank_s, place_s, slots_s)
     top = lax.broadcasted_iota(jnp.int32, (16, HALF), 0) < 8
-    for o in range(OWNERS):
-        index_ref[o] = jnp.where(top, tab_s[2 * o], tab_s[2 * o + 1]).astype(F32).astype(BF)
-    tile_terms(user_ref, count_ref, dest_ref, adj_ref, dmsg_ref, rank_s, slots_ref)
-
-
-def one_kernel(user_ref, count_ref, dest_ref, adj_ref, dmsg_ref, two_ref, index_ref, b_ref, rest_ref, slots_s, rank_s,
-               seen_s):
-    rank_blocks(dest_ref, rank_s, seen_s)
+    for k, out_ref in enumerate(out_refs):
+        for y in range(YS):
+            p = k * YS + y
+            out_ref[y, 0:64, :] = slots_s[0, p]
+            out_ref[y, 64:128, :] = slots_s[1, p]
+            out_ref[y, 128:144, :] = jnp.where(top, tab_s[2 * p], tab_s[2 * p + 1]).astype(F32).astype(BF)
+
+
+def one_kernel(user_ref, count_ref, dest_ref, adj_ref, dmsg_ref, out_ref, slots_s, rank_s, place_s, seen_s):
+    place_blocks(dest_ref, rank_s, place_s, seen_s)
     slots_s[...] = jnp.zeros_like(slots_s)
-    tile_terms(user_ref, count_ref, dest_ref, adj_ref, dmsg_ref, rank_s, slots_s)
-    for o in range(OWNERS):
-        b_ref[o, 0:64, :] = two_ref[1, o]
-        b_ref[o, 64:80, :] = index_ref[o]
-        b_ref[o, 80:144, :] = slots_s[0, o]
-        b_ref[o, 144:176, :] = slots_s[1, o, 0:32, :]
-        rest_ref[o] = slots_s[1, o, 32:64, :]
-
-
-def pack_kernel(two_ref, keep_hbm, got_ref, a_ref, keep_ref, sem):
-    copy = pltpu.make_async_copy(keep_hbm, keep_ref, sem)
-    copy.start()
-    for o in range(OWNERS):
-        a_ref[o, 0:64, :] = two_ref[0, o]
-    copy.wait()
+    tile_terms(user_ref, count_ref, adj_ref, dmsg_ref, rank_s, place_s, slots_s)
+    for k in range(XS):
+        for y in range(YS):
+            out_ref[y, 128 * k : 128 * k + 64, :] = slots_s[0, k * YS + y]
+            out_ref[y, 128 * k + 64 : 128 * k + 128, :] = slots_s[1, k * YS + y]
+
+
+def join_kernel(*refs):
+    *two_refs, one_ref, out_ref = refs
+    for y in range(YS):
+        for k, ref in enumerate(two_refs):
+            out_ref[y, 128 * k : 128 * k + 128, :] = ref[y, 0:128, :]
+            out_ref[y, INDEX + 16 * k : INDEX + 16 * k + 16, :] = ref[y, 128:144, :]
+        out_ref[y, ONES:, :] = one_ref[y]
+
+
+def split_kernel(in_ref, *out_refs):
+    for y in range(YS):
+        for k, ref in enumerate(out_refs):
+            at = ONES + 128 * (k + 1)
+            ref[y] = in_ref[y, at : at + 128, :]
+
+
+def pack_kernel(keep_ref, got_ref, a_ref):
     for o in range(OWNERS):
         rows = slice(8 * o, 8 * o + 8)
         for at in range(2):
             total = keep_ref[at, rows, :] + got_ref[at, rows, :]
-            first = 64 + 16 * at
-            a_ref[o, first : first + 16, :] = jnp.concatenate([total[:, :HALF], total[:, HALF:]], axis=0).astype(BF)
+            a_ref[o, 16 * at : 16 * at + 16, :] = jnp.concatenate([total[:, :HALF], total[:, HALF:]], axis=0).astype(BF)
 
 
 def chunk_kernel(a_ref, total_ref):
-    acc = a_ref[0, 64:96, :].astype(F32)
+    acc = a_ref[0].astype(F32)
     for s in range(1, OWNERS):
-        acc = acc + a_ref[s, 64:96, :].astype(F32)
+        acc = acc + a_ref[s].astype(F32)
     total_ref[...] = acc
 
 
-def last_kernel(own_ref, one_ref, two_ref, rest_ref, c_ref, slots_s):
+def last_kernel(own_ref, one_ref, two_ref, c_ref, slots_s):
     group = lax.axis_index("rep") // (2 * NEAR)
     for k, ref in enumerate((own_ref, one_ref, two_ref)):
         slots_s[lax.rem(group + 3 - k, 3)] = ref[...]
     total = (slots_s[0] + slots_s[1] + slots_s[2]).astype(BF)
     for o in range(OWNERS):
-        c_ref[o, 0:32, :] = rest_ref[o]
-        c_ref[o, 32:64, :] = total
+        c_ref[o] = total
 
 
 def collect_kernel(cuts, index_ref, *refs):
     *in_refs, out_ref, acc_s = refs
     acc_s[...] = jnp.zeros_like(acc_s)
 
-    def body(s, carry):
+    def body(y, carry):
         for ref, pieces in zip(in_refs, cuts):
-            for slot, at, to, rows in pieces:
-                i = index_ref[2 * s + slot]
-                acc_s[i, to : to + rows, :] += ref[s, at : at + rows, :].astype(F32)
+            for k, at in pieces:
+                for slot in range(2):
+                    i = index_ref[2 * (XS * y + k) + slot]
+                    acc_s[i] += ref[y, at + 64 * slot : at + 64 * slot + 64, :].astype(F32)
         return carry
 
-    lax.fori_loop(0, OWNERS, body, 0, unroll=4)
+    lax.fori_loop(0, YS, body, 0)
     for i in range(TRASH):
         out_ref[RB * i : RB * i + RB, :HALF] = acc_s[i, 0:32, :].astype(BF)
         out_ref[RB * i : RB * i + RB, HALF:] = acc_s[i, 32:64, :].astype(BF)
@@ -185,7 +203,7 @@
 def unpack_kernel(mine_ref, other_ref, self_ref, inter_ref):
     even = lax.rem(lax.axis_index("rep"), 2) == 0
     for o in range(OWNERS):
-        mine = mine_ref[o, 32:64, :].astype(F32)
+        mine = mine_ref[o].astype(F32)
         other = other_ref[o].astype(F32)
         a = jnp.where(even, mine, other)
         b = jnp.where(even, other, mine)
@@ -223,13 +241,16 @@
     def to_owners(x):
         return lax.all_to_all(x, "owner", split_axis=0, concat_axis=0, tiled=True)
 
-    def rows(n):
-        return ((OWNERS, n, HALF), BF)
+    def along_x(x, k):
+        return lax.ppermute(x, "owner", [(o, o - o % XS + (o + k) % XS) for o in range(OWNERS)])
+
+    def rows(n, lead=OWNERS):
+        return ((lead, n, HALF), BF)
 
     user = ((users, FEAT), BF)
     both = ((2, FEAT, FEAT), F32)
     chunk = ((32, HALF), F32)
-    ranks = [pltpu.SMEM((OWNERS,), jnp.int32)] * 2
+    slots = [pltpu.VMEM((2, OWNERS, 64, HALF), BF)] + [pltpu.SMEM((OWNERS,), jnp.int32)] * 3
     small = dict(flops=1_000_000, bytes_accessed=2 << 20)
     tile = dict(flops=140_000_000, bytes_accessed=2 << 20)
     dmsg2, dmsg1, user_grad, keep, send = call(
@@ -241,31 +262,33 @@
         params=WIDE, flops=900_000_000, bytes_accessed=6 << 20,
     )(cotangent, pre_two, pre_one, message_two, message_one, users_zero, w_self, w_inter)
     got = lax.ppermute(send, "rep", swap)
-    two, index_rows = call(
-        two_kernel, [((2, OWNERS, 64, HALF), BF), rows(16)], [SMEM] * 4 + [VMEM] * 2,
-        ranks + [pltpu.SMEM((2 * OWNERS,), jnp.int32)], **tile,
+    two = call(
+        two_kernel, [rows(144, YS)] * XS, [SMEM] * 4 + [VMEM] * 2, slots + [pltpu.SMEM((2 * OWNERS,), jnp.int32)], **tile
     )(tile_user, counts, dest, item_block, adjacency, dmsg2)
-    (a,) = call(
-        pack_kernel, [rows(96)], [VMEM, HBM, VMEM], [pltpu.VMEM(both[0], F32), pltpu.SemaphoreType.DMA], **small
-    )(two, keep, got)
+    keep, *two = lax.optimization_barrier((keep, *two))
+    (a,) = call(pack_kernel, [rows(32)], [VMEM] * 2, **small)(keep, got)
     got_a = to_owners(a)
 
-    b, rest = call(
-        one_kernel, [rows(176), rows(32)], [SMEM] * 3 + [VMEM] * 4,
-        [pltpu.VMEM((2, OWNERS, 64, HALF), BF)] + ranks, **tile,
-    )(tile_user, counts, dest, adjacency, dmsg1, two, index_rows)
+    two = [two[0]] + [along_x(two[k], k) for k in range(1, XS)]
+    (one,) = call(one_kernel, [rows(128 * XS, YS)], [SMEM] * 3 + [VMEM] * 2, slots, **tile)(
+        tile_user, counts, dest, adjacency, dmsg1
+    )
+    (b,) = call(join_kernel, [rows(272 * XS, YS)], [VMEM] * 5, **small)(*two, one)
     b, got_a = lax.optimization_barrier((b, got_a))
-    got_b = to_owners(b)
+    got_b = lax.all_to_all(
+        b, "owner", split_axis=0, concat_axis=0, tiled=True,
+        axis_index_groups=[[XS * y + x for y in range(YS)] for x in range(XS)],
+    )
 
     (total,) = call(chunk_kernel, [chunk], [VMEM], **small)(got_a)
     total = total + from_z(total, lambda z: z ^ 1)
     total = total + from_z(total, lambda z: z ^ 2)
     far = [from_z(total, lambda z, k=k: (z + z_chips - NEAR * k) % z_chips) for k in (1, 2)]
-    (c,) = call(last_kernel, [rows(64)], [VMEM] * 4, [pltpu.VMEM((3, 32, HALF), F32)], **small)(total, *far, rest)
+    (c,) = call(last_kernel, [rows(32)], [VMEM] * 3, [pltpu.VMEM((3, 32, HALF), F32)], **small)(total, *far)
     c, got_b = lax.optimization_barrier((c, got_b))
     got_c = to_owners(c)
 
-    index = got_b[:, 64:80:8, 0].astype(jnp.int32).reshape(2 * OWNERS)
+    index = got_b[:, INDEX:ONES:8, 0].astype(jnp.int32).reshape(2 * OWNERS)
 
     def collect(cuts, *arrays):
         return call(
@@ -273,10 +296,12 @@
             [pltpu.VMEM((TRASH + 1, 64, HALF), F32)], **small,
         )(index, *arrays)[0]
 
-    item_one = collect((((0, 0, 0, 64),), ((1, 0, 0, 64),)), got_a, got_b)
-    got_c, item_one = lax.optimization_barrier((got_c, item_one))
-    other = lax.ppermute(got_c[:, 32:64], "rep", swap)
-    item_zero = collect((((0, 80, 0, 64), (1, 144, 0, 32)), ((1, 0, 32, 32),)), got_b, got_c)
+    ones = call(split_kernel, [rows(128, YS)] * (XS - 1), [VMEM], **small)(got_b)
+    ones = [along_x(ones[k - 1], k) for k in range(1, XS)]
+    item_one = collect((tuple((k, 128 * k) for k in range(XS)),), got_b)
+    item_zero = collect((((0, ONES),),) + tuple(((k, 0),) for k in range(1, XS)), got_b, *ones)
+    got_c, item_one, item_zero = lax.optimization_barrier((got_c, item_one, item_zero))
+    other = lax.ppermute(got_c, "rep", swap)
     self_grad, inter_grad = call(unpack_kernel, [both] * 2, [VMEM] * 2, **small)(got_c, other)
     return user_grad, item_one, item_zero, self_grad, inter_grad
 

time: 119 us -> 140 us (1.18)
  starting transfers between devices: 53.6 us -> 68.9 us
  waiting for transfers between devices: 46.5 us -> 51.1 us
    all_to_all x3 -> x2, waiting for transfers between devices: 34.2 us -> 0.01 us  [to_owners(): return lax.all_to_all(x, 'owner', split_axis=0, concat_axis=0, tiled=True)]
    all_to_all x0 -> x1, waiting for transfers between devices: none -> 24 us  [local(): lax.all_to_all(b, 'owner', split_axis=0, concat_axis=0, tiled=True, axis_...]
    ppermute x1 -> x7, starting transfers between devices: 8.42 us -> 24.5 us  [the longest x6 20.9 us: along_x(): lax.ppermute(x, 'owner', [(o, o - o % XS + (o + k) % XS) for o in range(O...]
    ppermute x1 -> x7, waiting for transfers between devices: 0.01 us -> 15.7 us  [the longest x6 14.6 us: along_x(): lax.ppermute(x, 'owner', [(o, o - o % XS + (o + k) % XS) for o in range(O...]
    all_to_all x3 -> x2, starting transfers between devices: 15.7 us -> 8.62 us  [to_owners(): return lax.all_to_all(x, 'owner', split_axis=0, concat_axis=0, tiled=True)]
    all_to_all x0 -> x1, starting transfers between devices: none -> 5.31 us  [local(): lax.all_to_all(b, 'owner', split_axis=0, concat_axis=0, tiled=True, axis_...]
    pallas_call x4 -> x6, Pallas kernels: 4 us -> 4.82 us  [the longest x1 1.24 us: local(): call(two_kernel, [rows(144, YS)] * XS, [SMEM] * 4 + [VMEM] * 2, slots + [...]
  transfers between devices with their start and end apart: 9 -> 15, of which waited for: 6 -> 9; matrix products, arithmetic and copies ran while one was open for 1% -> 1% of each run, Pallas kernels for 6% -> 5%
where the time goes in v5:
time: 140 us
  starting transfers between devices  68.9 us (49%)
  waiting for transfers between devices  51.1 us (36%)
  Pallas kernels  13.7 us (10%)
  local copies, waits for them, and re-layouts  4.24 us (3%)
    all_to_all x1, waiting for transfers between devices, local(): lax.all_to_all(b, 'owner', split_axis=0, concat_axis=0, tiled=True, axis_...  24 us
    ppermute x6, starting transfers between devices, along_x(): lax.ppermute(x, 'owner', [(o, o - o % XS + (o + k) % XS) for o in range(O...  20.9 us
    ppermute x4, starting transfers between devices, from_z(): lax.ppermute(x, 'rep', [(2 * source(z) + c, 2 * z + c) for z in range(z_c...  18 us
    ppermute x6, waiting for transfers between devices, along_x(): lax.ppermute(x, 'owner', [(o, o - o % XS + (o + k) % XS) for o in range(O...  14.6 us
    ppermute x1, starting transfers between devices, local(): got = lax.ppermute(send, 'rep', swap)  12.4 us
    ppermute x4, waiting for transfers between devices, from_z(): lax.ppermute(x, 'rep', [(2 * source(z) + c, 2 * z + c) for z in range(z_c...  11.5 us
    all_to_all x2, starting transfers between devices, to_owners(): return lax.all_to_all(x, 'owner', split_axis=0, concat_axis=0, tiled=True)  8.62 us
    all_to_all x1, starting transfers between devices, local(): lax.all_to_all(b, 'owner', split_axis=0, concat_axis=0, tiled=True, axis_...  5.31 us
  transfers between devices with their start and end apart: 15, of which 9 were waited for; matrix products, arithmetic and copies ran while one was open for 1% of the time, Pallas kernels for 5%

profile of v5, /device:TPU:1, one launch (start us, length us, event | category | flops | bytes accessed | tf_op | source)
XLA Modules:
  0.0 139.7 jit_solution(14362680563121767706)
XLA Ops:
  0.6 0.0 copy-start.6
  0.6 0.0 copy-start.5
  0.7 0.0 copy-start.1
  0.7 0.0 copy-start.8
  0.7 0.0 copy-start.7
  0.7 4.2 %shard_map.164 = (bf16[768,256]{1,0:T(8,128)(2,1)}, bf16[768,256]{1,0:T(8,128)(2,1)}, bf16[768,256]{1,0:T(8,128)(2,1)}, f32[2,256,256]{2,1,0:T(8,128)}, f32[2,256,256]{2,1,0:T(8,128)}) custom-call(bf16[768,256]{1,0:T(8,128)(2,1)} %refs_0_.1, bf16[768,256]{1,0:T(8,128)(2,1)} %refs_1_.1, bf16[768,256]{1,0:T(8,128)(2,1)} %refs_2_.1, bf16[768,256]{1,0:T(8,128)(2,1)} %refs_3_.1, ...), custom_call_target="tpu_custom_call" | custom-call | flops 900000000 | bytes 6291456 | tf_op jit(solution)/shard_map/pallas_call | solution.py:256
  4.9 12.4 %collective-permute-start.3 = (f32[2,256,256]{2,1,0:T(8,128)}, f32[2,256,256]{2,1,0:T(8,128)S(1)}, u32[]{:S(2)}, u32[]{:S(2)}) collective-permute-start(f32[2,256,256]{2,1,0:T(8,128)} %get-tuple-element.44), channel_id=1, source_target_pairs={{0,1},{1,0},{2,3},{3,2},{4,5},{5,4},{6,7},{7,6},{8,9},{9,8},{10,11... | collective-permute-start | bytes 1572872 | tf_op jit(solution)/shard_map/ppermute | solution.py:264
  17.4 0.0 copy-done.6
  17.4 0.0 copy-done.5
  17.4 0.0 copy-done.1
  17.4 0.0 copy-done.8
  17.4 0.0 copy-done.7
  17.4 0.0 copy-start.3
  17.4 1.0 copy-done.3
  18.4 0.0 copy-start.4
  18.4 1.2 shard_map.165
  19.7 0.0 collective-permute-done.3.got_ref
  19.7 0.0 copy-start.2
  19.7 1.0 copy-done.2
  20.7 0.8 shard_map.168
  21.5 3.9 %all-to-all-start = ((bf16[32,32,128]{2,1,0:T(8,128)(2,1)}), bf16[32,32,128]{2,1,0:T(8,128)(2,1)S(1)}, u32[]{:S(2)}, u32[]{:S(2)}) async-start(bf16[32,32,128]{2,1,0:T(8,128)(2,1)} %shard_map.168), calls=%async_computation | async-start | bytes 524288 | tf_op jit(solution)/shard_map/all_to_all | solution.py:242
  25.3 3.0 %collective-permute-start = (bf16[8,144,128]{2,1,0:T(8,128)(2,1)S(1)}, bf16[8,144,128]{2,1,0:T(8,128)(2,1)S(1)}, u32[]{:S(2)}, u32[]{:S(2)}) collective-permute-start(bf16[8,144,128]{2,1,0:T(8,128)(2,1)S(1)} %get-tuple-element.39), channel_id=1, source_target_pairs={{0,24},{24,48},{48,72},{72,0},{96,120},{120,144},{144,168},{168,96... | collective-permute-start | bytes 884744 | tf_op jit(solution)/shard_map/ppermute | solution.py:245
  28.4 4.3 %collective-permute-start.1 = (bf16[8,144,128]{2,1,0:T(8,128)(2,1)S(1)}, bf16[8,144,128]{2,1,0:T(8,128)(2,1)S(1)}, u32[]{:S(2)}, u32[]{:S(2)}) collective-permute-start(bf16[8,144,128]{2,1,0:T(8,128)(2,1)S(1)} %get-tuple-element.40), channel_id=1, source_target_pairs={{0,48},{24,72},{48,0},{72,24},{96,144},{120,168},{144,96},{168,120... | collective-permute-start | bytes 884744 | tf_op jit(solution)/shard_map/ppermute | solution.py:245
  32.7 3.1 %collective-permute-start.2 = (bf16[8,144,128]{2,1,0:T(8,128)(2,1)S(1)}, bf16[8,144,128]{2,1,0:T(8,128)(2,1)S(1)}, u32[]{:S(2)}, u32[]{:S(2)}) collective-permute-start(bf16[8,144,128]{2,1,0:T(8,128)(2,1)S(1)} %get-tuple-element.41), channel_id=1, source_target_pairs={{0,72},{24,0},{48,24},{72,48},{96,168},{120,96},{144,120},{168,144... | collective-permute-start | bytes 884744 | tf_op jit(solution)/shard_map/ppermute | solution.py:245
  35.8 0.0 copy-done.4
  35.8 1.1 shard_map.166.refs_4_
  36.9 2.6 %collective-permute-done.refs_1_ = bf16[8,144,128]{2,1,0:T(8,128)(2,1)S(1)} collective-permute-done((bf16[8,144,128]{2,1,0:T(8,128)(2,1)S(1)}, bf16[8,144,128]{2,1,0:T(8,128)(2,1)S(1)}, u32[]{:S(2)}, u32[]{:S(2)}) %collective-permute-start) | collective-permute-done | bytes 294944 | tf_op jit(solution)/shard_map/ppermute | solution.py:245
  39.5 6.8 %collective-permute-done.1.refs_2_ = bf16[8,144,128]{2,1,0:T(8,128)(2,1)S(1)} collective-permute-done((bf16[8,144,128]{2,1,0:T(8,128)(2,1)S(1)}, bf16[8,144,128]{2,1,0:T(8,128)(2,1)S(1)}, u32[]{:S(2)}, u32[]{:S(2)}) %collective-permute-start.1) | collective-permute-done | bytes 294944 | tf_op jit(solution)/shard_map/ppermute | solution.py:245
  46.2 0.4 collective-permute-done.2.refs_3_
  46.6 0.1 shard_map.167
  46.8 0.0 copy-start
  46.8 1.4 copy-done
  48.1 0.0 all-to-all-done.a_ref
  48.2 5.3 %all-to-all-start.1 = ((bf16[8,1088,128]{2,1,0:T(8,128)(2,1)}), bf16[8,1088,128]{2,1,0:T(8,128)(2,1)S(1)}, u32[]{:S(2)}, u32[]{:S(2)}) async-start(bf16[8,1088,128]{2,1,0:T(8,128)(2,1)} %copy-done), calls=%async_computation.1 | async-start | bytes 4456448 | tf_op jit(solution)/shard_map/all_to_all | solution.py:278
  53.5 1.9 %collective-permute-start.4 = (f32[32,128]{1,0:T(8,128)S(1)}, f32[32,128]{1,0:T(8,128)S(1)}, u32[]{:S(2)}, u32[]{:S(2)}) collective-permute-start(f32[32,128]{1,0:T(8,128)S(1)} %shard_map.169), channel_id=1, source_target_pairs={{2,0},{3,1},{0,2},{1,3},{6,4},{7,5},{4,6},{5,7},{10,8},{11,9},{8,1... | collective-permute-start | bytes 49160 | tf_op jit(solution)/shard_map/ppermute | solution.py:239
  55.4 2.6 %collective-permute-done.4 = f32[32,128]{1,0:T(8,128)S(1)} collective-permute-done((f32[32,128]{1,0:T(8,128)S(1)}, f32[32,128]{1,0:T(8,128)S(1)}, u32[]{:S(2)}, u32[]{:S(2)}) %collective-permute-start.4) | collective-permute-done | bytes 16416 | tf_op jit(solution)/shard_map/ppermute | solution.py:239
  58.0 3.4 %collective-permute-start.5 = (f32[32,128]{1,0:T(8,128)S(1)}, f32[32,128]{1,0:T(8,128)S(1)}, u32[]{:S(2)}, u32[]{:S(2)}) collective-permute-start(f32[32,128]{1,0:T(8,128)S(1)} %add.6), channel_id=1, source_target_pairs={{4,0},{5,1},{6,2},{7,3},{0,4},{1,5},{2,6},{3,7},{12,8},{13,9},{14,... | collective-permute-start | bytes 49160 | tf_op jit(solution)/shard_map/ppermute | solution.py:239
  61.4 2.4 %collective-permute-done.5 = f32[32,128]{1,0:T(8,128)S(1)} collective-permute-done((f32[32,128]{1,0:T(8,128)S(1)}, f32[32,128]{1,0:T(8,128)S(1)}, u32[]{:S(2)}, u32[]{:S(2)}) %collective-permute-start.5) | collective-permute-done | bytes 16416 | tf_op jit(solution)/shard_map/ppermute | solution.py:239
  63.8 10.8 %collective-permute-start.7 = (f32[32,128]{1,0:T(8,128)S(1)}, f32[32,128]{1,0:T(8,128)S(1)}, u32[]{:S(2)}, u32[]{:S(2)}) collective-permute-start(f32[32,128]{1,0:T(8,128)S(1)} %add.7.own_ref), channel_id=1, source_target_pairs={{8,0},{9,1},{10,2},{11,3},{12,4},{13,5},{14,6},{15,7},{16,8},{17,9... | collective-permute-start | bytes 49160 | tf_op jit(solution)/shard_map/ppermute | solution.py:239
  74.6 1.9 %collective-permute-start.6 = (f32[32,128]{1,0:T(8,128)S(1)}, f32[32,128]{1,0:T(8,128)S(1)}, u32[]{:S(2)}, u32[]{:S(2)}) collective-permute-start(f32[32,128]{1,0:T(8,128)S(1)} %add.7.own_ref), channel_id=1, source_target_pairs={{16,0},{17,1},{18,2},{19,3},{20,4},{21,5},{22,6},{23,7},{0,8},{1,9... | collective-permute-start | bytes 49160 | tf_op jit(solution)/shard_map/ppermute | solution.py:239
  76.5 0.0 collective-permute-done.7.two_ref
  76.5 6.5 %collective-permute-done.6.one_ref = f32[32,128]{1,0:T(8,128)S(1)} collective-permute-done((f32[32,128]{1,0:T(8,128)S(1)}, f32[32,128]{1,0:T(8,128)S(1)}, u32[]{:S(2)}, u32[]{:S(2)}) %collective-permute-start.6) | collective-permute-done | bytes 16416 | tf_op jit(solution)/shard_map/ppermute | solution.py:239
  83.0 0.7 shard_map.170
  83.8 24.0 %all-to-all-done.1.refs_0_.in_ref = bf16[8,1088,128]{2,1,0:T(8,128)(2,1)S(1)} async-done(((bf16[8,1088,128]{2,1,0:T(8,128)(2,1)}), bf16[8,1088,128]{2,1,0:T(8,128)(2,1)S(1)}, u32[]{:S(2)}, u32[]{:S(2)}) %all-to-all-start.1) | async-done | bytes 2228256 | tf_op jit(solution)/shard_map/all_to_all | solution.py:278
  107.7 4.7 %all-to-all-start.2 = ((bf16[32,32,128]{2,1,0:T(8,128)(2,1)}), bf16[32,32,128]{2,1,0:T(8,128)(2,1)S(1)}, u32[]{:S(2)}, u32[]{:S(2)}) async-start(bf16[32,32,128]{2,1,0:T(8,128)(2,1)} %shard_map.170), calls=%async_computation.2 | async-start | bytes 524288 | tf_op jit(solution)/shard_map/all_to_all | solution.py:242
  112.5 0.8 shard_map.172
  113.3 3.1 %collective-permute-start.8 = (bf16[8,128,128]{2,1,0:T(8,128)(2,1)}, bf16[8,128,128]{2,1,0:T(8,128)(2,1)S(1)}, u32[]{:S(2)}, u32[]{:S(2)}) collective-permute-start(bf16[8,128,128]{2,1,0:T(8,128)(2,1)} %get-tuple-element.49), channel_id=1, source_target_pairs={{0,24},{24,48},{48,72},{72,0},{96,120},{120,144},{144,168},{168,96... | collective-permute-start | bytes 786440 | tf_op jit(solution)/shard_map/ppermute | solution.py:245
  116.5 4.3 %collective-permute-start.9 = (bf16[8,128,128]{2,1,0:T(8,128)(2,1)}, bf16[8,128,128]{2,1,0:T(8,128)(2,1)S(1)}, u32[]{:S(2)}, u32[]{:S(2)}) collective-permute-start(bf16[8,128,128]{2,1,0:T(8,128)(2,1)} %get-tuple-element.50), channel_id=1, source_target_pairs={{0,48},{24,72},{48,0},{72,24},{96,144},{120,168},{144,96},{168,120... | collective-permute-start | bytes 786440 | tf_op jit(solution)/shard_map/ppermute | solution.py:245
  120.8 3.1 %collective-permute-start.10 = (bf16[8,128,128]{2,1,0:T(8,128)(2,1)S(1)}, bf16[8,128,128]{2,1,0:T(8,128)(2,1)S(1)}, u32[]{:S(2)}, u32[]{:S(2)}) collective-permute-start(bf16[8,128,128]{2,1,0:T(8,128)(2,1)S(1)} %get-tuple-element.51), channel_id=1, source_target_pairs={{0,72},{24,0},{48,24},{72,48},{96,168},{120,96},{144,120},{168,144... | collective-permute-start | bytes 786440 | tf_op jit(solution)/shard_map/ppermute | solution.py:245
  123.9 0.1 slice.3
  123.9 0.8 convert_reduce_fusion
  124.7 0.8 reshape.18.index_ref
  125.5 1.8 %shard_map.171 = bf16[1024,256]{1,0:T(8,128)(2,1)} custom-call(s32[64]{0:T(128)S(1)} %reshape.18.index_ref, bf16[8,1088,128]{2,1,0:T(8,128)(2,1)S(1)} %all-to-all-done.1.refs_0_.in_ref), custom_call_target="tpu_custom_call" | custom-call | flops 1000000 | bytes 2097152 | tf_op jit(solution)/shard_map/pallas_call | solution.py:294
  127.3 0.0 collective-permute-done.8.refs_1_
  127.3 4.9 %collective-permute-done.9.refs_2_ = bf16[8,128,128]{2,1,0:T(8,128)(2,1)S(1)} collective-permute-done((bf16[8,128,128]{2,1,0:T(8,128)(2,1)}, bf16[8,128,128]{2,1,0:T(8,128)(2,1)S(1)}, u32[]{:S(2)}, u32[]{:S(2)}) %collective-permute-start.9) | collective-permute-done | bytes 262176 | tf_op jit(solution)/shard_map/ppermute | solution.py:245
  132.1 0.0 collective-permute-done.10.refs_3_
  132.1 1.8 %shard_map.173 = bf16[1024,256]{1,0:T(8,128)(2,1)} custom-call(s32[64]{0:T(128)S(1)} %reshape.18.index_ref, bf16[8,1088,128]{2,1,0:T(8,128)(2,1)S(1)} %all-to-all-done.1.refs_0_.in_ref, bf16[8,128,128]{2,1,0:T(8,128)(2,1)S(1)} %collective-permute-done.8.refs_1_, bf16[8,128,128]{2,1,0:T(8,128)(2,1)S(1)} %collective-permute-done.9.refs_2_, ...), custom_call_target="tpu_custom_call" | custom-call | flops 1000000 | bytes 2097152 | tf_op jit(solution)/shard_map/pallas_call | solution.py:294
  133.9 0.0 all-to-all-done.2.mine_ref
  133.9 3.6 %collective-permute-start.11 = (bf16[32,32,128]{2,1,0:T(8,128)(2,1)S(1)}, bf16[32,32,128]{2,1,0:T(8,128)(2,1)S(1)}, u32[]{:S(2)}, u32[]{:S(2)}) collective-permute-start(bf16[32,32,128]{2,1,0:T(8,128)(2,1)S(1)} %all-to-all-done.2.mine_ref), channel_id=1, source_target_pairs={{0,1},{1,0},{2,3},{3,2},{4,5},{5,4},{6,7},{7,6},{8,9},{9,8},{10,11... | collective-permute-start | bytes 786440 | tf_op jit(solution)/shard_map/ppermute | solution.py:304
  137.5 1.1 collective-permute-done.11.other_ref
  138.6 1.1 shard_map.174
  (3 shorter events, 0.1 us)
Async XLA Ops:
  0.6 16.7 %copy-start.6 = (s32[4]{0:T(128)S(1)}, s32[4]{0:T(128)}, u32[]{:S(2)}) copy-start(s32[4]{0:T(128)} %count_ref.3) | copy-start | bytes 52
  0.6 16.7 %copy-start.5 = (s32[4]{0:T(128)S(1)}, s32[4]{0:T(128)}, u32[]{:S(2)}) copy-start(s32[4]{0:T(128)} %user_ref.3) | copy-start | bytes 52
  0.7 16.7 %copy-start.1 = (bf16[4,256,256]{2,1,0:T(8,128)(2,1)S(1)}, bf16[4,256,256]{2,1,0:T(8,128)(2,1)}, u32[]{:S(2)}) copy-start(bf16[4,256,256]{2,1,0:T(8,128)(2,1)} %adj_ref.3) | copy-start | bytes 1572868
  0.7 16.7 %copy-start.8 = (s32[32]{0:T(128)S(1)}, s32[32]{0:T(128)}, u32[]{:S(2)}) copy-start(s32[32]{0:T(128)} %item_ref.1) | copy-start | bytes 388
  0.7 16.7 %copy-start.7 = (s32[32,1]{0,1:T(1,128)S(1)}, s32[32,1]{0,1:T(1,128)}, u32[]{:S(2)}) copy-start(s32[32,1]{0,1:T(1,128)} %param.24) | copy-start | bytes 388
  4.9 14.7 %collective-permute-start.3 = (f32[2,256,256]{2,1,0:T(8,128)}, f32[2,256,256]{2,1,0:T(8,128)S(1)}, u32[]{:S(2)}, u32[]{:S(2)}) collective-permute-start(f32[2,256,256]{2,1,0:T(8,128)} %get-tuple-element.44), channel_id=1, source_target_pairs={{0,1},{1,0},{2,3},{3,2},{4,5},{5,4},{6,7},{7,6},{8,9},{9,8},{10,11... | collective-permute-start | bytes 1572872 | tf_op jit(solution)/shard_map/ppermute | solution.py:264
  17.4 1.0 copy-start.3
  18.4 17.4 %copy-start.4 = (bf16[768,256]{1,0:T(8,128)(2,1)S(1)}, bf16[768,256]{1,0:T(8,128)(2,1)}, u32[]{:S(2)}) copy-start(bf16[768,256]{1,0:T(8,128)(2,1)} %get-tuple-element.42.dmsg_ref) | copy-start | bytes 1179652
  19.7 1.0 copy-start.2
  21.5 26.7 %all-to-all-start = ((bf16[32,32,128]{2,1,0:T(8,128)(2,1)}), bf16[32,32,128]{2,1,0:T(8,128)(2,1)S(1)}, u32[]{:S(2)}, u32[]{:S(2)}) async-start(bf16[32,32,128]{2,1,0:T(8,128)(2,1)} %shard_map.168), calls=%async_computation | async-start | bytes 524288 | tf_op jit(solution)/shard_map/all_to_all | solution.py:242
  25.3 14.1 %collective-permute-start = (bf16[8,144,128]{2,1,0:T(8,128)(2,1)S(1)}, bf16[8,144,128]{2,1,0:T(8,128)(2,1)S(1)}, u32[]{:S(2)}, u32[]{:S(2)}) collective-permute-start(bf16[8,144,128]{2,1,0:T(8,128)(2,1)S(1)} %get-tuple-element.39), channel_id=1, source_target_pairs={{0,24},{24,48},{48,72},{72,0},{96,120},{120,144},{144,168},{168,96... | collective-permute-start | bytes 884744 | tf_op jit(solution)/shard_map/ppermute | solution.py:245
  28.4 17.9 %collective-permute-start.1 = (bf16[8,144,128]{2,1,0:T(8,128)(2,1)S(1)}, bf16[8,144,128]{2,1,0:T(8,128)(2,1)S(1)}, u32[]{:S(2)}, u32[]{:S(2)}) collective-permute-start(bf16[8,144,128]{2,1,0:T(8,128)(2,1)S(1)} %get-tuple-element.40), channel_id=1, source_target_pairs={{0,48},{24,72},{48,0},{72,24},{96,144},{120,168},{144,96},{168,120... | collective-permute-start | bytes 884744 | tf_op jit(solution)/shard_map/ppermute | solution.py:245
  32.7 13.9 %collective-permute-start.2 = (bf16[8,144,128]{2,1,0:T(8,128)(2,1)S(1)}, bf16[8,144,128]{2,1,0:T(8,128)(2,1)S(1)}, u32[]{:S(2)}, u32[]{:S(2)}) collective-permute-start(bf16[8,144,128]{2,1,0:T(8,128)(2,1)S(1)} %get-tuple-element.41), channel_id=1, source_target_pairs={{0,72},{24,0},{48,24},{72,48},{96,168},{120,96},{144,120},{168,144... | collective-permute-start | bytes 884744 | tf_op jit(solution)/shard_map/ppermute | solution.py:245
  46.8 1.4 copy-start
  48.2 59.6 %all-to-all-start.1 = ((bf16[8,1088,128]{2,1,0:T(8,128)(2,1)}), bf16[8,1088,128]{2,1,0:T(8,128)(2,1)S(1)}, u32[]{:S(2)}, u32[]{:S(2)}) async-start(bf16[8,1088,128]{2,1,0:T(8,128)(2,1)} %copy-done), calls=%async_computation.1 | async-start | bytes 4456448 | tf_op jit(solution)/shard_map/all_to_all | solution.py:278
  53.5 4.5 %collective-permute-start.4 = (f32[32,128]{1,0:T(8,128)S(1)}, f32[32,128]{1,0:T(8,128)S(1)}, u32[]{:S(2)}, u32[]{:S(2)}) collective-permute-start(f32[32,128]{1,0:T(8,128)S(1)} %shard_map.169), channel_id=1, source_target_pairs={{2,0},{3,1},{0,2},{1,3},{6,4},{7,5},{4,6},{5,7},{10,8},{11,9},{8,1... | collective-permute-start | bytes 49160 | tf_op jit(solution)/shard_map/ppermute | solution.py:239
  58.0 5.8 %collective-permute-start.5 = (f32[32,128]{1,0:T(8,128)S(1)}, f32[32,128]{1,0:T(8,128)S(1)}, u32[]{:S(2)}, u32[]{:S(2)}) collective-permute-start(f32[32,128]{1,0:T(8,128)S(1)} %add.6), channel_id=1, source_target_pairs={{4,0},{5,1},{6,2},{7,3},{0,4},{1,5},{2,6},{3,7},{12,8},{13,9},{14,... | collective-permute-start | bytes 49160 | tf_op jit(solution)/shard_map/ppermute | solution.py:239
  63.8 12.7 %collective-permute-start.7 = (f32[32,128]{1,0:T(8,128)S(1)}, f32[32,128]{1,0:T(8,128)S(1)}, u32[]{:S(2)}, u32[]{:S(2)}) collective-permute-start(f32[32,128]{1,0:T(8,128)S(1)} %add.7.own_ref), channel_id=1, source_target_pairs={{8,0},{9,1},{10,2},{11,3},{12,4},{13,5},{14,6},{15,7},{16,8},{17,9... | collective-permute-start | bytes 49160 | tf_op jit(solution)/shard_map/ppermute | solution.py:239
  74.6 8.4 %collective-permute-start.6 = (f32[32,128]{1,0:T(8,128)S(1)}, f32[32,128]{1,0:T(8,128)S(1)}, u32[]{:S(2)}, u32[]{:S(2)}) collective-permute-start(f32[32,128]{1,0:T(8,128)S(1)} %add.7.own_ref), channel_id=1, source_target_pairs={{16,0},{17,1},{18,2},{19,3},{20,4},{21,5},{22,6},{23,7},{0,8},{1,9... | collective-permute-start | bytes 49160 | tf_op jit(solution)/shard_map/ppermute | solution.py:239
  107.7 26.2 %all-to-all-start.2 = ((bf16[32,32,128]{2,1,0:T(8,128)(2,1)}), bf16[32,32,128]{2,1,0:T(8,128)(2,1)S(1)}, u32[]{:S(2)}, u32[]{:S(2)}) async-start(bf16[32,32,128]{2,1,0:T(8,128)(2,1)} %shard_map.170), calls=%async_computation.2 | async-start | bytes 524288 | tf_op jit(solution)/shard_map/all_to_all | solution.py:242
  113.3 14.0 %collective-permute-start.8 = (bf16[8,128,128]{2,1,0:T(8,128)(2,1)}, bf16[8,128,128]{2,1,0:T(8,128)(2,1)S(1)}, u32[]{:S(2)}, u32[]{:S(2)}) collective-permute-start(bf16[8,128,128]{2,1,0:T(8,128)(2,1)} %get-tuple-element.49), channel_id=1, source_target_pairs={{0,24},{24,48},{48,72},{72,0},{96,120},{120,144},{144,168},{168,96... | collective-permute-start | bytes 786440 | tf_op jit(solution)/shard_map/ppermute | solution.py:245
  116.5 15.7 %collective-permute-start.9 = (bf16[8,128,128]{2,1,0:T(8,128)(2,1)}, bf16[8,128,128]{2,1,0:T(8,128)(2,1)S(1)}, u32[]{:S(2)}, u32[]{:S(2)}) collective-permute-start(bf16[8,128,128]{2,1,0:T(8,128)(2,1)} %get-tuple-element.50), channel_id=1, source_target_pairs={{0,48},{24,72},{48,0},{72,24},{96,144},{120,168},{144,96},{168,120... | collective-permute-start | bytes 786440 | tf_op jit(solution)/shard_map/ppermute | solution.py:245
  120.8 11.4 %collective-permute-start.10 = (bf16[8,128,128]{2,1,0:T(8,128)(2,1)S(1)}, bf16[8,128,128]{2,1,0:T(8,128)(2,1)S(1)}, u32[]{:S(2)}, u32[]{:S(2)}) collective-permute-start(bf16[8,128,128]{2,1,0:T(8,128)(2,1)S(1)} %get-tuple-element.51), channel_id=1, source_target_pairs={{0,72},{24,0},{48,24},{72,48},{96,168},{120,96},{144,120},{168,144... | collective-permute-start | bytes 786440 | tf_op jit(solution)/shard_map/ppermute | solution.py:245
  133.9 4.7 %collective-permute-start.11 = (bf16[32,32,128]{2,1,0:T(8,128)(2,1)S(1)}, bf16[32,32,128]{2,1,0:T(8,128)(2,1)S(1)}, u32[]{:S(2)}, u32[]{:S(2)}) collective-permute-start(bf16[32,32,128]{2,1,0:T(8,128)(2,1)S(1)} %all-to-all-done.2.mine_ref), channel_id=1, source_target_pairs={{0,1},{1,0},{2,3},{3,2},{4,5},{5,4},{6,7},{7,6},{8,9},{9,8},{10,11... | collective-permute-start | bytes 786440 | tf_op jit(solution)/shard_map/ppermute | solution.py:304

commit v6 on v4

--- a/solution.py
+++ b/solution.py
@@ -83,7 +83,7 @@
         grad_self = tdot(sum_s[...], delta_s[...])
         grad_inter = tdot(prod_s[...], delta_s[...])
         keep_ref[at] = jnp.where(even, grad_self, grad_inter)
-        send_ref[at] = jnp.where(even, grad_inter, grad_self)
+        send_ref[at] = jnp.where(even, grad_inter, grad_self).astype(BF)
 
 
 def rank_blocks(dest_ref, rank_s, seen_s):
@@ -115,7 +115,7 @@
     for j in range(dest_ref.shape[0]):
         tab_s[2 * dest_ref[j] + rank_s[j]] = item_ref[j]
     slots_ref[...] = jnp.zeros_like(slots_ref)
-    top = lax.broadcasted_iota(jnp.int32, (16, HALF), 0) < 8
+    top = lax.broadcasted_iota(jnp.int32, (8, HALF), 0) < 4
     for o in range(OWNERS):
         index_ref[o] = jnp.where(top, tab_s[2 * o], tab_s[2 * o + 1]).astype(F32).astype(BF)
     tile_terms(user_ref, count_ref, dest_ref, adj_ref, dmsg_ref, rank_s, slots_ref)
@@ -127,31 +127,28 @@
     slots_s[...] = jnp.zeros_like(slots_s)
     tile_terms(user_ref, count_ref, dest_ref, adj_ref, dmsg_ref, rank_s, slots_s)
     for o in range(OWNERS):
-        b_ref[o, 0:64, :] = two_ref[1, o]
-        b_ref[o, 64:80, :] = index_ref[o]
-        b_ref[o, 80:144, :] = slots_s[0, o]
-        b_ref[o, 144:176, :] = slots_s[1, o, 0:32, :]
+        b_ref[o, 0:32, :] = two_ref[0, o, 32:64, :]
+        b_ref[o, 32:96, :] = two_ref[1, o]
+        b_ref[o, 96:160, :] = slots_s[0, o]
+        b_ref[o, 160:192, :] = slots_s[1, o, 0:32, :]
+        b_ref[o, 192:200, :] = index_ref[o]
         rest_ref[o] = slots_s[1, o, 32:64, :]
 
 
-def pack_kernel(two_ref, keep_hbm, got_ref, a_ref, keep_ref, sem):
-    copy = pltpu.make_async_copy(keep_hbm, keep_ref, sem)
-    copy.start()
-    for o in range(OWNERS):
-        a_ref[o, 0:64, :] = two_ref[0, o]
-    copy.wait()
-    for o in range(OWNERS):
+def pack_kernel(two_ref, keep_ref, got_ref, a_ref):
+    for o in range(OWNERS):
+        a_ref[o, 0:32, :] = two_ref[0, o, 0:32, :]
         rows = slice(8 * o, 8 * o + 8)
         for at in range(2):
-            total = keep_ref[at, rows, :] + got_ref[at, rows, :]
-            first = 64 + 16 * at
+            total = keep_ref[at, rows, :] + got_ref[at, rows, :].astype(F32)
+            first = 32 + 16 * at
             a_ref[o, first : first + 16, :] = jnp.concatenate([total[:, :HALF], total[:, HALF:]], axis=0).astype(BF)
 
 
 def chunk_kernel(a_ref, total_ref):
-    acc = a_ref[0, 64:96, :].astype(F32)
+    acc = a_ref[0, 32:64, :].astype(F32)
     for s in range(1, OWNERS):
-        acc = acc + a_ref[s, 64:96, :].astype(F32)
+        acc = acc + a_ref[s, 32:64, :].astype(F32)
     total_ref[...] = acc
 
 
@@ -234,7 +231,7 @@
     tile = dict(flops=140_000_000, bytes_accessed=2 << 20)
     dmsg2, dmsg1, user_grad, keep, send = call(
         user_kernel,
-        [user, user, user, both, both],
+        [user, user, user, both, (both[0], BF)],
         [HBM] * 8,
         [pltpu.VMEM((users, FEAT), BF)] * 6 + [pltpu.VMEM((2, FEAT, FEAT), BF)] * 2
         + [pltpu.VMEM((users, FEAT), BF)] * 6 + [pltpu.SemaphoreType.DMA((8 + 6 * (users // BLK),))],
@@ -242,16 +239,14 @@
     )(cotangent, pre_two, pre_one, message_two, message_one, users_zero, w_self, w_inter)
     got = lax.ppermute(send, "rep", swap)
     two, index_rows = call(
-        two_kernel, [((2, OWNERS, 64, HALF), BF), rows(16)], [SMEM] * 4 + [VMEM] * 2,
+        two_kernel, [((2, OWNERS, 64, HALF), BF), rows(8)], [SMEM] * 4 + [VMEM] * 2,
         ranks + [pltpu.SMEM((2 * OWNERS,), jnp.int32)], **tile,
     )(tile_user, counts, dest, item_block, adjacency, dmsg2)
-    (a,) = call(
-        pack_kernel, [rows(96)], [VMEM, HBM, VMEM], [pltpu.VMEM(both[0], F32), pltpu.SemaphoreType.DMA], **small
-    )(two, keep, got)
+    (a,) = call(pack_kernel, [rows(64)], [VMEM] * 3, **small)(two, keep, got)
     got_a = to_owners(a)
 
     b, rest = call(
-        one_kernel, [rows(176), rows(32)], [SMEM] * 3 + [VMEM] * 4,
+        one_kernel, [rows(200), rows(32)], [SMEM] * 3 + [VMEM] * 4,
         [pltpu.VMEM((2, OWNERS, 64, HALF), BF)] + ranks, **tile,
     )(tile_user, counts, dest, adjacency, dmsg1, two, index_rows)
     b, got_a = lax.optimization_barrier((b, got_a))
@@ -265,7 +260,7 @@
     c, got_b = lax.optimization_barrier((c, got_b))
     got_c = to_owners(c)
 
-    index = got_b[:, 64:80:8, 0].astype(jnp.int32).reshape(2 * OWNERS)
+    index = got_b[:, 192:200:4, 0].astype(jnp.int32).reshape(2 * OWNERS)
 
     def collect(cuts, *arrays):
         return call(
@@ -273,10 +268,10 @@
             [pltpu.VMEM((TRASH + 1, 64, HALF), F32)], **small,
         )(index, *arrays)[0]
 
-    item_one = collect((((0, 0, 0, 64),), ((1, 0, 0, 64),)), got_a, got_b)
+    item_one = collect((((0, 0, 0, 32),), ((0, 0, 32, 32), (1, 32, 0, 64))), got_a, got_b)
     got_c, item_one = lax.optimization_barrier((got_c, item_one))
     other = lax.ppermute(got_c[:, 32:64], "rep", swap)
-    item_zero = collect((((0, 80, 0, 64), (1, 144, 0, 32)), ((1, 0, 32, 32),)), got_b, got_c)
+    item_zero = collect((((0, 96, 0, 64), (1, 160, 0, 32)), ((1, 0, 32, 32),)), got_b, got_c)
     self_grad, inter_grad = call(unpack_kernel, [both] * 2, [VMEM] * 2, **small)(got_c, other)
     return user_grad, item_one, item_zero, self_grad, inter_grad
 

time: 119 us -> 116 us (0.975)
  starting transfers between devices: 53.6 us -> 51.9 us
    ppermute x1, starting transfers between devices: 8.42 us -> 6.29 us  [local(): other = lax.ppermute(got_c[:, 32:64], 'rep', swap)]
where the time goes in v6:
time: 116 us
  starting transfers between devices  51.9 us (45%)
  waiting for transfers between devices  45.9 us (40%)
  Pallas kernels  12.8 us (11%)
  local copies, waits for them, and re-layouts  3.5 us (3%)
    all_to_all x3, waiting for transfers between devices, to_owners(): return lax.all_to_all(x, 'owner', split_axis=0, concat_axis=0, tiled=True)  34.2 us
    ppermute x4, starting transfers between devices, from_z(): lax.ppermute(x, 'rep', [(2 * source(z) + c, 2 * z + c) for z in range(z_c...  18 us
    all_to_all x3, starting transfers between devices, to_owners(): return lax.all_to_all(x, 'owner', split_axis=0, concat_axis=0, tiled=True)  15.2 us
    ppermute x1, starting transfers between devices, local(): got = lax.ppermute(send, 'rep', swap)  12.4 us
    ppermute x4, waiting for transfers between devices, from_z(): lax.ppermute(x, 'rep', [(2 * source(z) + c, 2 * z + c) for z in range(z_c...  11.7 us
    ppermute x1, starting transfers between devices, local(): other = lax.ppermute(got_c[:, 32:64], 'rep', swap)  6.29 us
    pallas_call x1, Pallas kernels, local(): call(user_kernel, [user, user, user, both, (both[0], BF)], [HBM] * 8, [pl...  4.13 us
    pallas_call x2, Pallas kernels, collect(): call(functools.partial(collect_kernel, cuts), [((OWNERS * RB, FEAT), BF)]...  3.73 us
  transfers between devices with their start and end apart: 9, of which 6 were waited for; matrix products, arithmetic and copies ran while one was open for 1% of the time, Pallas kernels for 6%

profile of v6, /device:TPU:1, one launch (start us, length us, event | category | flops | bytes accessed | tf_op | source)
XLA Modules:
  0.0 115.7 jit_solution(4232823243603338069)
XLA Ops:
  0.6 0.0 copy-start.6
  0.6 0.0 copy-start.5
  0.7 0.0 copy-start
  0.7 0.0 copy-start.8
  0.7 0.0 copy-start.7
  0.7 4.1 %shard_map.164 = (bf16[768,256]{1,0:T(8,128)(2,1)}, bf16[768,256]{1,0:T(8,128)(2,1)}, bf16[768,256]{1,0:T(8,128)(2,1)}, f32[2,256,256]{2,1,0:T(8,128)}, bf16[2,256,256]{2,1,0:T(8,128)(2,1)}) custom-call(bf16[768,256]{1,0:T(8,128)(2,1)} %refs_0_.1, bf16[768,256]{1,0:T(8,128)(2,1)} %refs_1_.1, bf16[768,256]{1,0:T(8,128)(2,1)} %refs_2_.1, ...), custom_call_target="tpu_custom_call" | custom-call | flops 900000000 | bytes 6291456 | tf_op jit(solution)/shard_map/pallas_call | solution.py:232
  4.8 12.4 %collective-permute-start = (bf16[2,256,256]{2,1,0:T(8,128)(2,1)}, bf16[2,256,256]{2,1,0:T(8,128)(2,1)S(1)}, u32[]{:S(2)}, u32[]{:S(2)}) collective-permute-start(bf16[2,256,256]{2,1,0:T(8,128)(2,1)} %get-tuple-element.29), channel_id=1, source_target_pairs={{0,1},{1,0},{2,3},{3,2},{4,5},{5,4},{6,7},{7,6},{8,9},{9,8},{10,11... | collective-permute-start | bytes 786440 | tf_op jit(solution)/shard_map/ppermute | solution.py:240
  17.3 0.0 copy-done.6
  17.3 0.0 copy-done.5
  17.3 0.0 copy-done
  17.3 0.0 copy-done.8
  17.3 0.0 copy-done.7
  17.3 0.0 copy-start.4
  17.3 1.0 copy-done.4
  18.3 1.1 shard_map.165
  19.4 0.0 collective-permute-done.got_ref
  19.4 0.0 copy-start.2
  19.4 1.0 copy-done.2
  20.4 0.0 copy-start.3
  20.4 0.8 shard_map.167
  21.3 3.9 %all-to-all-start = ((bf16[32,64,128]{2,1,0:T(8,128)(2,1)}), bf16[32,64,128]{2,1,0:T(8,128)(2,1)S(1)}, u32[]{:S(2)}, u32[]{:S(2)}) async-start(bf16[32,64,128]{2,1,0:T(8,128)(2,1)} %shard_map.167), calls=%async_computation | async-start | bytes 1048576 | tf_op jit(solution)/shard_map/all_to_all | solution.py:221
  25.2 0.0 copy-done.3
  25.2 1.1 shard_map.166
  26.3 0.0 copy-start.1
  26.3 1.2 %copy-done.1 = bf16[32,200,128]{2,1,0:T(8,128)(2,1)} copy-done((bf16[32,200,128]{2,1,0:T(8,128)(2,1)}, bf16[32,200,128]{2,1,0:T(8,128)(2,1)S(1)}, u32[]{:S(2)}) %copy-start.1) | copy-done | bytes 1638424
  27.5 14.9 %all-to-all-done.a_ref.refs_0_ = bf16[32,64,128]{2,1,0:T(8,128)(2,1)S(1)} async-done(((bf16[32,64,128]{2,1,0:T(8,128)(2,1)}), bf16[32,64,128]{2,1,0:T(8,128)(2,1)S(1)}, u32[]{:S(2)}, u32[]{:S(2)}) %all-to-all-start) | async-done | bytes 524320 | tf_op jit(solution)/shard_map/all_to_all | solution.py:221
  42.4 4.7 %all-to-all-start.1 = ((bf16[32,200,128]{2,1,0:T(8,128)(2,1)}), bf16[32,200,128]{2,1,0:T(8,128)(2,1)S(1)}, u32[]{:S(2)}, u32[]{:S(2)}) async-start(bf16[32,200,128]{2,1,0:T(8,128)(2,1)} %copy-done.1), calls=%async_computation.1 | async-start | bytes 3276800 | tf_op jit(solution)/shard_map/all_to_all | solution.py:221
  47.1 1.9 %collective-permute-start.1 = (f32[32,128]{1,0:T(8,128)S(1)}, f32[32,128]{1,0:T(8,128)S(1)}, u32[]{:S(2)}, u32[]{:S(2)}) collective-permute-start(f32[32,128]{1,0:T(8,128)S(1)} %shard_map.168), channel_id=1, source_target_pairs={{2,0},{3,1},{0,2},{1,3},{6,4},{7,5},{4,6},{5,7},{10,8},{11,9},{8,1... | collective-permute-start | bytes 49160 | tf_op jit(solution)/shard_map/ppermute | solution.py:218
  49.0 2.6 %collective-permute-done.1 = f32[32,128]{1,0:T(8,128)S(1)} collective-permute-done((f32[32,128]{1,0:T(8,128)S(1)}, f32[32,128]{1,0:T(8,128)S(1)}, u32[]{:S(2)}, u32[]{:S(2)}) %collective-permute-start.1) | collective-permute-done | bytes 16416 | tf_op jit(solution)/shard_map/ppermute | solution.py:218
  51.6 3.4 %collective-permute-start.2 = (f32[32,128]{1,0:T(8,128)S(1)}, f32[32,128]{1,0:T(8,128)S(1)}, u32[]{:S(2)}, u32[]{:S(2)}) collective-permute-start(f32[32,128]{1,0:T(8,128)S(1)} %add.6), channel_id=1, source_target_pairs={{4,0},{5,1},{6,2},{7,3},{0,4},{1,5},{2,6},{3,7},{12,8},{13,9},{14,... | collective-permute-start | bytes 49160 | tf_op jit(solution)/shard_map/ppermute | solution.py:218
  55.0 2.4 %collective-permute-done.2 = f32[32,128]{1,0:T(8,128)S(1)} collective-permute-done((f32[32,128]{1,0:T(8,128)S(1)}, f32[32,128]{1,0:T(8,128)S(1)}, u32[]{:S(2)}, u32[]{:S(2)}) %collective-permute-start.2) | collective-permute-done | bytes 16416 | tf_op jit(solution)/shard_map/ppermute | solution.py:218
  57.4 10.7 %collective-permute-start.4 = (f32[32,128]{1,0:T(8,128)S(1)}, f32[32,128]{1,0:T(8,128)S(1)}, u32[]{:S(2)}, u32[]{:S(2)}) collective-permute-start(f32[32,128]{1,0:T(8,128)S(1)} %add.7.own_ref), channel_id=1, source_target_pairs={{8,0},{9,1},{10,2},{11,3},{12,4},{13,5},{14,6},{15,7},{16,8},{17,9... | collective-permute-start | bytes 49160 | tf_op jit(solution)/shard_map/ppermute | solution.py:218
  68.2 1.9 %collective-permute-start.3 = (f32[32,128]{1,0:T(8,128)S(1)}, f32[32,128]{1,0:T(8,128)S(1)}, u32[]{:S(2)}, u32[]{:S(2)}) collective-permute-start(f32[32,128]{1,0:T(8,128)S(1)} %add.7.own_ref), channel_id=1, source_target_pairs={{16,0},{17,1},{18,2},{19,3},{20,4},{21,5},{22,6},{23,7},{0,8},{1,9... | collective-permute-start | bytes 49160 | tf_op jit(solution)/shard_map/ppermute | solution.py:218
  70.1 0.0 collective-permute-done.4.two_ref
  70.1 6.7 %collective-permute-done.3.one_ref = f32[32,128]{1,0:T(8,128)S(1)} collective-permute-done((f32[32,128]{1,0:T(8,128)S(1)}, f32[32,128]{1,0:T(8,128)S(1)}, u32[]{:S(2)}, u32[]{:S(2)}) %collective-permute-start.3) | collective-permute-done | bytes 16416 | tf_op jit(solution)/shard_map/ppermute | solution.py:218
  76.9 0.9 shard_map.169
  77.7 7.5 %all-to-all-done.1.refs_1_.refs_0_ = bf16[32,200,128]{2,1,0:T(8,128)(2,1)S(1)} async-done(((bf16[32,200,128]{2,1,0:T(8,128)(2,1)}), bf16[32,200,128]{2,1,0:T(8,128)(2,1)S(1)}, u32[]{:S(2)}, u32[]{:S(2)}) %all-to-all-start.1) | async-done | bytes 1638432 | tf_op jit(solution)/shard_map/all_to_all | solution.py:221
  85.2 6.7 %all-to-all-start.2 = ((bf16[32,64,128]{2,1,0:T(8,128)(2,1)}), bf16[32,64,128]{2,1,0:T(8,128)(2,1)S(1)}, u32[]{:S(2)}, u32[]{:S(2)}) async-start(bf16[32,64,128]{2,1,0:T(8,128)(2,1)} %shard_map.169), calls=%async_computation.2 | async-start | bytes 1048576 | tf_op jit(solution)/shard_map/all_to_all | solution.py:221
  91.9 0.1 slice.6
  92.0 0.6 convert_reduce_fusion
  92.7 0.1 reshape.18.index_ref
  92.8 1.9 %shard_map.170 = bf16[1024,256]{1,0:T(8,128)(2,1)} custom-call(s32[64]{0:T(128)S(1)} %reshape.18.index_ref, bf16[32,64,128]{2,1,0:T(8,128)(2,1)S(1)} %all-to-all-done.a_ref.refs_0_, bf16[32,200,128]{2,1,0:T(8,128)(2,1)S(1)} %all-to-all-done.1.refs_1_.refs_0_), custom_call_target="tpu_custom_call" | custom-call | flops 1000000 | bytes 2097152 | tf_op jit(solution)/shard_map/pallas_call | solution.py:266
  94.6 11.8 %all-to-all-done.2.refs_1_.mine_ref = bf16[32,64,128]{2,1,0:T(8,128)(2,1)S(1)} async-done(((bf16[32,64,128]{2,1,0:T(8,128)(2,1)}), bf16[32,64,128]{2,1,0:T(8,128)(2,1)S(1)}, u32[]{:S(2)}, u32[]{:S(2)}) %all-to-all-start.2) | async-done | bytes 524320 | tf_op jit(solution)/shard_map/all_to_all | solution.py:221
  106.5 6.3 %collective-permute-start.5 = (bf16[32,32,128]{2,1,0:T(8,128)(2,1)S(1)}, bf16[32,32,128]{2,1,0:T(8,128)(2,1)S(1)}, u32[]{:S(2)}, u32[]{:S(2)}) collective-permute-start(bf16[32,32,128]{2,1,0:T(8,128)(2,1)S(1)} %slice.7), channel_id=1, source_target_pairs={{0,1},{1,0},{2,3},{3,2},{4,5},{5,4},{6,7},{7,6},{8,9},{9,8},{10,11... | collective-permute-start | bytes 786440 | tf_op jit(solution)/shard_map/ppermute | solution.py:273
  112.8 1.9 %shard_map.171 = bf16[1024,256]{1,0:T(8,128)(2,1)} custom-call(s32[64]{0:T(128)S(1)} %reshape.18.index_ref, bf16[32,200,128]{2,1,0:T(8,128)(2,1)S(1)} %all-to-all-done.1.refs_1_.refs_0_, bf16[32,64,128]{2,1,0:T(8,128)(2,1)S(1)} %all-to-all-done.2.refs_1_.mine_ref), custom_call_target="tpu_custom_call" | custom-call | flops 1000000 | bytes 2097152 | tf_op jit(solution)/shard_map/pallas_call | solution.py:266
  114.6 0.0 collective-permute-done.5.other_ref
  114.6 1.1 shard_map.172
  (4 shorter events, 0.1 us)
Async XLA Ops:
  0.6 16.6 %copy-start.6 = (s32[4]{0:T(128)S(1)}, s32[4]{0:T(128)}, u32[]{:S(2)}) copy-start(s32[4]{0:T(128)} %count_ref.3) | copy-start | bytes 52
  0.6 16.6 %copy-start.5 = (s32[4]{0:T(128)S(1)}, s32[4]{0:T(128)}, u32[]{:S(2)}) copy-start(s32[4]{0:T(128)} %user_ref.3) | copy-start | bytes 52
  0.7 16.6 %copy-start = (bf16[4,256,256]{2,1,0:T(8,128)(2,1)S(1)}, bf16[4,256,256]{2,1,0:T(8,128)(2,1)}, u32[]{:S(2)}) copy-start(bf16[4,256,256]{2,1,0:T(8,128)(2,1)} %adj_ref.3) | copy-start | bytes 1572868
  0.7 16.6 %copy-start.8 = (s32[32]{0:T(128)S(1)}, s32[32]{0:T(128)}, u32[]{:S(2)}) copy-start(s32[32]{0:T(128)} %item_ref.1) | copy-start | bytes 388
  0.7 16.6 %copy-start.7 = (s32[32,1]{0,1:T(1,128)S(1)}, s32[32,1]{0,1:T(1,128)}, u32[]{:S(2)}) copy-start(s32[32,1]{0,1:T(1,128)} %param.24) | copy-start | bytes 388
  4.8 14.6 %collective-permute-start = (bf16[2,256,256]{2,1,0:T(8,128)(2,1)}, bf16[2,256,256]{2,1,0:T(8,128)(2,1)S(1)}, u32[]{:S(2)}, u32[]{:S(2)}) collective-permute-start(bf16[2,256,256]{2,1,0:T(8,128)(2,1)} %get-tuple-element.29), channel_id=1, source_target_pairs={{0,1},{1,0},{2,3},{3,2},{4,5},{5,4},{6,7},{7,6},{8,9},{9,8},{10,11... | collective-permute-start | bytes 786440 | tf_op jit(solution)/shard_map/ppermute | solution.py:240
  17.3 1.0 copy-start.4
  19.4 1.0 copy-start.2
  20.4 4.8 %copy-start.3 = (bf16[768,256]{1,0:T(8,128)(2,1)S(1)}, bf16[768,256]{1,0:T(8,128)(2,1)}, u32[]{:S(2)}) copy-start(bf16[768,256]{1,0:T(8,128)(2,1)} %get-tuple-element.23.dmsg_ref) | copy-start | bytes 1179652
  21.3 21.1 %all-to-all-start = ((bf16[32,64,128]{2,1,0:T(8,128)(2,1)}), bf16[32,64,128]{2,1,0:T(8,128)(2,1)S(1)}, u32[]{:S(2)}, u32[]{:S(2)}) async-start(bf16[32,64,128]{2,1,0:T(8,128)(2,1)} %shard_map.167), calls=%async_computation | async-start | bytes 1048576 | tf_op jit(solution)/shard_map/all_to_all | solution.py:221
  26.3 1.2 %copy-start.1 = (bf16[32,200,128]{2,1,0:T(8,128)(2,1)}, bf16[32,200,128]{2,1,0:T(8,128)(2,1)S(1)}, u32[]{:S(2)}) copy-start(bf16[32,200,128]{2,1,0:T(8,128)(2,1)S(1)} %get-tuple-element.32) | copy-start | bytes 4915204
  42.4 42.9 %all-to-all-start.1 = ((bf16[32,200,128]{2,1,0:T(8,128)(2,1)}), bf16[32,200,128]{2,1,0:T(8,128)(2,1)S(1)}, u32[]{:S(2)}, u32[]{:S(2)}) async-start(bf16[32,200,128]{2,1,0:T(8,128)(2,1)} %copy-done.1), calls=%async_computation.1 | async-start | bytes 3276800 | tf_op jit(solution)/shard_map/all_to_all | solution.py:221
  47.1 4.5 %collective-permute-start.1 = (f32[32,128]{1,0:T(8,128)S(1)}, f32[32,128]{1,0:T(8,128)S(1)}, u32[]{:S(2)}, u32[]{:S(2)}) collective-permute-start(f32[32,128]{1,0:T(8,128)S(1)} %shard_map.168), channel_id=1, source_target_pairs={{2,0},{3,1},{0,2},{1,3},{6,4},{7,5},{4,6},{5,7},{10,8},{11,9},{8,1... | collective-permute-start | bytes 49160 | tf_op jit(solution)/shard_map/ppermute | solution.py:218
  51.6 5.8 %collective-permute-start.2 = (f32[32,128]{1,0:T(8,128)S(1)}, f32[32,128]{1,0:T(8,128)S(1)}, u32[]{:S(2)}, u32[]{:S(2)}) collective-permute-start(f32[32,128]{1,0:T(8,128)S(1)} %add.6), channel_id=1, source_target_pairs={{4,0},{5,1},{6,2},{7,3},{0,4},{1,5},{2,6},{3,7},{12,8},{13,9},{14,... | collective-permute-start | bytes 49160 | tf_op jit(solution)/shard_map/ppermute | solution.py:218
  57.4 12.7 %collective-permute-start.4 = (f32[32,128]{1,0:T(8,128)S(1)}, f32[32,128]{1,0:T(8,128)S(1)}, u32[]{:S(2)}, u32[]{:S(2)}) collective-permute-start(f32[32,128]{1,0:T(8,128)S(1)} %add.7.own_ref), channel_id=1, source_target_pairs={{8,0},{9,1},{10,2},{11,3},{12,4},{13,5},{14,6},{15,7},{16,8},{17,9... | collective-permute-start | bytes 49160 | tf_op jit(solution)/shard_map/ppermute | solution.py:218
  68.2 8.7 %collective-permute-start.3 = (f32[32,128]{1,0:T(8,128)S(1)}, f32[32,128]{1,0:T(8,128)S(1)}, u32[]{:S(2)}, u32[]{:S(2)}) collective-permute-start(f32[32,128]{1,0:T(8,128)S(1)} %add.7.own_ref), channel_id=1, source_target_pairs={{16,0},{17,1},{18,2},{19,3},{20,4},{21,5},{22,6},{23,7},{0,8},{1,9... | collective-permute-start | bytes 49160 | tf_op jit(solution)/shard_map/ppermute | solution.py:218
  85.2 21.2 %all-to-all-start.2 = ((bf16[32,64,128]{2,1,0:T(8,128)(2,1)}), bf16[32,64,128]{2,1,0:T(8,128)(2,1)S(1)}, u32[]{:S(2)}, u32[]{:S(2)}) async-start(bf16[32,64,128]{2,1,0:T(8,128)(2,1)} %shard_map.169), calls=%async_computation.2 | async-start | bytes 1048576 | tf_op jit(solution)/shard_map/all_to_all | solution.py:221
  106.5 8.2 %collective-permute-start.5 = (bf16[32,32,128]{2,1,0:T(8,128)(2,1)S(1)}, bf16[32,32,128]{2,1,0:T(8,128)(2,1)S(1)}, u32[]{:S(2)}, u32[]{:S(2)}) collective-permute-start(bf16[32,32,128]{2,1,0:T(8,128)(2,1)S(1)} %slice.7), channel_id=1, source_target_pairs={{0,1},{1,0},{2,3},{3,2},{4,5},{5,4},{6,7},{7,6},{8,9},{9,8},{10,11... | collective-permute-start | bytes 786440 | tf_op jit(solution)/shard_map/ppermute | solution.py:273

commit v7 on v6

--- a/solution.py
+++ b/solution.py
@@ -17,6 +17,9 @@
 HALF = 128
 BLK = 256
 OWNERS = 32
+XS = 4
+YS = 8
+INDEX = 256
 TRASH = 32
 NEAR = 4
 VMEM = pl.BlockSpec(memory_space=pltpu.VMEM)
@@ -121,45 +124,40 @@
     tile_terms(user_ref, count_ref, dest_ref, adj_ref, dmsg_ref, rank_s, slots_ref)
 
 
-def one_kernel(user_ref, count_ref, dest_ref, adj_ref, dmsg_ref, two_ref, index_ref, b_ref, rest_ref, slots_s, rank_s,
-               seen_s):
+def one_kernel(user_ref, count_ref, dest_ref, adj_ref, dmsg_ref, two_ref, index_ref, b_ref, slots_s, rank_s, seen_s):
     rank_blocks(dest_ref, rank_s, seen_s)
     slots_s[...] = jnp.zeros_like(slots_s)
     tile_terms(user_ref, count_ref, dest_ref, adj_ref, dmsg_ref, rank_s, slots_s)
     for o in range(OWNERS):
-        b_ref[o, 0:32, :] = two_ref[0, o, 32:64, :]
-        b_ref[o, 32:96, :] = two_ref[1, o]
-        b_ref[o, 96:160, :] = slots_s[0, o]
-        b_ref[o, 160:192, :] = slots_s[1, o, 0:32, :]
-        b_ref[o, 192:200, :] = index_ref[o]
-        rest_ref[o] = slots_s[1, o, 32:64, :]
-
-
-def pack_kernel(two_ref, keep_ref, got_ref, a_ref):
-    for o in range(OWNERS):
-        a_ref[o, 0:32, :] = two_ref[0, o, 0:32, :]
-        rows = slice(8 * o, 8 * o + 8)
+        for slot in range(2):
+            b_ref[o, 64 * slot : 64 * slot + 64, :] = two_ref[slot, o]
+            b_ref[o, 128 + 64 * slot : 192 + 64 * slot, :] = slots_s[slot, o]
+        b_ref[o, INDEX : INDEX + 8, :] = index_ref[o]
+
+
+def pack_kernel(keep_ref, got_ref, a_ref):
+    for y in range(YS):
         for at in range(2):
+            rows = slice(32 * y, 32 * y + 32)
             total = keep_ref[at, rows, :] + got_ref[at, rows, :].astype(F32)
-            first = 32 + 16 * at
-            a_ref[o, first : first + 16, :] = jnp.concatenate([total[:, :HALF], total[:, HALF:]], axis=0).astype(BF)
+            a_ref[y, 64 * at : 64 * at + 32, :] = total[:, :HALF].astype(BF)
+            a_ref[y, 64 * at + 32 : 64 * at + 64, :] = total[:, HALF:].astype(BF)
 
 
 def chunk_kernel(a_ref, total_ref):
-    acc = a_ref[0, 32:64, :].astype(F32)
-    for s in range(1, OWNERS):
-        acc = acc + a_ref[s, 32:64, :].astype(F32)
+    acc = a_ref[0].astype(F32)
+    for y in range(1, YS):
+        acc = acc + a_ref[y].astype(F32)
     total_ref[...] = acc
 
 
-def last_kernel(own_ref, one_ref, two_ref, rest_ref, c_ref, slots_s):
+def last_kernel(own_ref, one_ref, two_ref, c_ref, slots_s):
     group = lax.axis_index("rep") // (2 * NEAR)
     for k, ref in enumerate((own_ref, one_ref, two_ref)):
         slots_s[lax.rem(group + 3 - k, 3)] = ref[...]
     total = (slots_s[0] + slots_s[1] + slots_s[2]).astype(BF)
-    for o in range(OWNERS):
-        c_ref[o, 0:32, :] = rest_ref[o]
-        c_ref[o, 32:64, :] = total
+    for y in range(YS):
+        c_ref[y] = total
 
 
 def collect_kernel(cuts, index_ref, *refs):
@@ -181,17 +179,14 @@
 
 def unpack_kernel(mine_ref, other_ref, self_ref, inter_ref):
     even = lax.rem(lax.axis_index("rep"), 2) == 0
-    for o in range(OWNERS):
-        mine = mine_ref[o, 32:64, :].astype(F32)
-        other = other_ref[o].astype(F32)
-        a = jnp.where(even, mine, other)
-        b = jnp.where(even, other, mine)
-        rows = slice(8 * o, 8 * o + 8)
-        for ref, value in ((self_ref, a), (inter_ref, b)):
-            ref[1, rows, :HALF] = value[0:8]
-            ref[1, rows, HALF:] = value[8:16]
-            ref[0, rows, :HALF] = value[16:24]
-            ref[0, rows, HALF:] = value[24:32]
+    for y in range(YS):
+        mine = mine_ref[y].astype(F32)
+        other = other_ref[y].astype(F32)
+        rows = slice(32 * y, 32 * y + 32)
+        for ref, value in ((self_ref, jnp.where(even, mine, other)), (inter_ref, jnp.where(even, other, mine))):
+            for at, layer in ((0, 1), (64, 0)):
+                ref[layer, rows, :HALF] = value[at : at + 32]
+                ref[layer, rows, HALF:] = value[at + 32 : at + 64]
 
 
 def call(kernel, outs, in_specs, scratch=(), params=PARAMS, **cost):
@@ -220,12 +215,19 @@
     def to_owners(x):
         return lax.all_to_all(x, "owner", split_axis=0, concat_axis=0, tiled=True)
 
-    def rows(n):
-        return ((OWNERS, n, HALF), BF)
+    def to_column(x):
+        columns = [[XS * y + x for y in range(YS)] for x in range(XS)]
+        return lax.all_to_all(x, "owner", split_axis=0, concat_axis=0, tiled=True, axis_index_groups=columns)
+
+    def add_x(x, bit):
+        return x + lax.ppermute(x, "owner", [(o, o ^ bit) for o in range(OWNERS)])
+
+    def rows(n, lead=OWNERS):
+        return ((lead, n, HALF), BF)
 
     user = ((users, FEAT), BF)
     both = ((2, FEAT, FEAT), F32)
-    chunk = ((32, HALF), F32)
+    chunk = ((128, HALF), F32)
     ranks = [pltpu.SMEM((OWNERS,), jnp.int32)] * 2
     small = dict(flops=1_000_000, bytes_accessed=2 << 20)
     tile = dict(flops=140_000_000, bytes_accessed=2 << 20)
@@ -242,25 +244,26 @@
         two_kernel, [((2, OWNERS, 64, HALF), BF), rows(8)], [SMEM] * 4 + [VMEM] * 2,
         ranks + [pltpu.SMEM((2 * OWNERS,), jnp.int32)], **tile,
     )(tile_user, counts, dest, item_block, adjacency, dmsg2)
-    (a,) = call(pack_kernel, [rows(64)], [VMEM] * 3, **small)(two, keep, got)
-    got_a = to_owners(a)
-
-    b, rest = call(
-        one_kernel, [rows(200), rows(32)], [SMEM] * 3 + [VMEM] * 4,
+    (a,) = call(pack_kernel, [rows(128, YS)], [VMEM] * 2, **small)(keep, got)
+    got_a = to_column(a)
+
+    (b,) = call(
+        one_kernel, [rows(INDEX + 8)], [SMEM] * 3 + [VMEM] * 4,
         [pltpu.VMEM((2, OWNERS, 64, HALF), BF)] + ranks, **tile,
     )(tile_user, counts, dest, adjacency, dmsg1, two, index_rows)
     b, got_a = lax.optimization_barrier((b, got_a))
     got_b = to_owners(b)
 
     (total,) = call(chunk_kernel, [chunk], [VMEM], **small)(got_a)
+    total = add_x(add_x(total, 1), 2)
     total = total + from_z(total, lambda z: z ^ 1)
     total = total + from_z(total, lambda z: z ^ 2)
     far = [from_z(total, lambda z, k=k: (z + z_chips - NEAR * k) % z_chips) for k in (1, 2)]
-    (c,) = call(last_kernel, [rows(64)], [VMEM] * 4, [pltpu.VMEM((3, 32, HALF), F32)], **small)(total, *far, rest)
+    (c,) = call(last_kernel, [rows(128, YS)], [VMEM] * 3, [pltpu.VMEM((3, 128, HALF), F32)], **small)(total, *far)
     c, got_b = lax.optimization_barrier((c, got_b))
-    got_c = to_owners(c)
-
-    index = got_b[:, 192:200:4, 0].astype(jnp.int32).reshape(2 * OWNERS)
+    got_c = to_column(c)
+
+    index = got_b[:, INDEX : INDEX + 8 : 4, 0].astype(jnp.int32).reshape(2 * OWNERS)
 
     def collect(cuts, *arrays):
         return call(
@@ -268,10 +271,10 @@
             [pltpu.VMEM((TRASH + 1, 64, HALF), F32)], **small,
         )(index, *arrays)[0]
 
-    item_one = collect((((0, 0, 0, 32),), ((0, 0, 32, 32), (1, 32, 0, 64))), got_a, got_b)
-    got_c, item_one = lax.optimization_barrier((got_c, item_one))
-    other = lax.ppermute(got_c[:, 32:64], "rep", swap)
-    item_zero = collect((((0, 96, 0, 64), (1, 160, 0, 32)), ((1, 0, 32, 32),)), got_b, got_c)
+    item_one = collect((((0, 0, 0, 64), (1, 64, 0, 64)),), got_b)
+    item_zero = collect((((0, 128, 0, 64), (1, 192, 0, 64)),), got_b)
+    got_c, item_one, item_zero = lax.optimization_barrier((got_c, item_one, item_zero))
+    other = lax.ppermute(got_c, "rep", swap)
     self_grad, inter_grad = call(unpack_kernel, [both] * 2, [VMEM] * 2, **small)(got_c, other)
     return user_grad, item_one, item_zero, self_grad, inter_grad
 

time: 116 us -> 121 us (1.043)
  starting transfers between devices: 51.9 us -> 62.4 us
  waiting for transfers between devices: 45.9 us -> 39.9 us
    all_to_all x3 -> x1, waiting for transfers between devices: 34.2 us -> 4.29 us  [to_owners(): return lax.all_to_all(x, 'owner', split_axis=0, concat_axis=0, tiled=True)]
    ppermute x1 -> x3, starting transfers between devices: 6.29 us -> 20.5 us  [the longest x1 13.4 us: local(): other = lax.ppermute(got_c, 'rep', swap)]
    all_to_all x0 -> x2, waiting for transfers between devices: none -> 12.6 us  [to_column(): lax.all_to_all(x, 'owner', split_axis=0, concat_axis=0, tiled=True, axis_...]
    all_to_all x3 -> x1, starting transfers between devices: 15.2 us -> 4.05 us  [to_owners(): return lax.all_to_all(x, 'owner', split_axis=0, concat_axis=0, tiled=True)]
    all_to_all x0 -> x2, starting transfers between devices: none -> 8.4 us  [to_column(): lax.all_to_all(x, 'owner', split_axis=0, concat_axis=0, tiled=True, axis_...]
    ppermute x1 -> x3, waiting for transfers between devices: 0.01 us -> 7.21 us  [the longest x2 6.07 us: add_x(): return x + lax.ppermute(x, 'owner', [(o, o ^ bit) for o in range(OWNERS)])]
    ppermute x4, waiting for transfers between devices: 11.7 us -> 14.5 us  [from_z(): lax.ppermute(x, 'rep', [(2 * source(z) + c, 2 * z + c) for z in range(z_c...]
    ppermute x1, waiting for transfers between devices: 0.01 us -> 1.35 us  [local(): got = lax.ppermute(send, 'rep', swap)]
  transfers between devices with their start and end apart: 9 -> 11, of which waited for: 6 -> 10; matrix products, arithmetic and copies ran while one was open for 1% -> 1% of each run, Pallas kernels for 6% -> 5%
where the time goes in v7:
time: 121 us; the launch traced here: 120 us
  starting transfers between devices  62.4 us (52%)
  waiting for transfers between devices  39.9 us (33%)
  Pallas kernels  12.5 us (10%)
  local copies, waits for them, and re-layouts  3.63 us (3%)
    ppermute x4, starting transfers between devices, from_z(): lax.ppermute(x, 'rep', [(2 * source(z) + c, 2 * z + c) for z in range(z_c...  17.1 us
    ppermute x4, waiting for transfers between devices, from_z(): lax.ppermute(x, 'rep', [(2 * source(z) + c, 2 * z + c) for z in range(z_c...  14.5 us
    ppermute x1, starting transfers between devices, local(): other = lax.ppermute(got_c, 'rep', swap)  13.4 us
    all_to_all x2, waiting for transfers between devices, to_column(): lax.all_to_all(x, 'owner', split_axis=0, concat_axis=0, tiled=True, axis_...  12.6 us
    ppermute x1, starting transfers between devices, local(): got = lax.ppermute(send, 'rep', swap)  12.4 us
    all_to_all x2, starting transfers between devices, to_column(): lax.all_to_all(x, 'owner', split_axis=0, concat_axis=0, tiled=True, axis_...  8.4 us
    ppermute x2, starting transfers between devices, add_x(): return x + lax.ppermute(x, 'owner', [(o, o ^ bit) for o in range(OWNERS)])  7.02 us
    ppermute x2, waiting for transfers between devices, add_x(): return x + lax.ppermute(x, 'owner', [(o, o ^ bit) for o in range(OWNERS)])  6.07 us
  transfers between devices with their start and end apart: 11, of which 10 were waited for; matrix products, arithmetic and copies ran while one was open for 1% of the time, Pallas kernels for 5%

profile of v7, /device:TPU:1, one launch (start us, length us, event | category | flops | bytes accessed | tf_op | source)
XLA Modules:
  0.0 120.0 jit_solution(12562558265545548131)
XLA Ops:
  0.6 0.0 copy-start.6
  0.6 0.0 copy-start.5
  0.7 0.0 copy-start.1
  0.7 0.0 copy-start.8
  0.7 0.0 copy-start.7
  0.7 4.1 %shard_map.164 = (bf16[768,256]{1,0:T(8,128)(2,1)}, bf16[768,256]{1,0:T(8,128)(2,1)}, bf16[768,256]{1,0:T(8,128)(2,1)}, f32[2,256,256]{2,1,0:T(8,128)}, bf16[2,256,256]{2,1,0:T(8,128)(2,1)}) custom-call(bf16[768,256]{1,0:T(8,128)(2,1)} %refs_0_.1, bf16[768,256]{1,0:T(8,128)(2,1)} %refs_1_.1, bf16[768,256]{1,0:T(8,128)(2,1)} %refs_2_.1, ...), custom_call_target="tpu_custom_call" | custom-call | flops 900000000 | bytes 6291456 | tf_op jit(solution)/shard_map/pallas_call | solution.py:234
  4.8 12.4 %collective-permute-start = (bf16[2,256,256]{2,1,0:T(8,128)(2,1)}, bf16[2,256,256]{2,1,0:T(8,128)(2,1)S(1)}, u32[]{:S(2)}, u32[]{:S(2)}) collective-permute-start(bf16[2,256,256]{2,1,0:T(8,128)(2,1)} %get-tuple-element.27), channel_id=1, source_target_pairs={{0,1},{1,0},{2,3},{3,2},{4,5},{5,4},{6,7},{7,6},{8,9},{9,8},{10,11... | collective-permute-start | bytes 786440 | tf_op jit(solution)/shard_map/ppermute | solution.py:242
  17.3 1.4 %collective-permute-done.got_ref = bf16[2,256,256]{2,1,0:T(8,128)(2,1)S(1)} collective-permute-done((bf16[2,256,256]{2,1,0:T(8,128)(2,1)}, bf16[2,256,256]{2,1,0:T(8,128)(2,1)S(1)}, u32[]{:S(2)}, u32[]{:S(2)}) %collective-permute-start) | collective-permute-done | bytes 262176 | tf_op jit(solution)/shard_map/ppermute | solution.py:242
  18.6 0.0 copy-start.2
  18.6 1.0 copy-done.2
  19.7 0.0 copy-start.3
  19.7 0.7 shard_map.167
  20.4 3.4 %all-to-all-start = ((bf16[8,128,128]{2,1,0:T(8,128)(2,1)}), bf16[8,128,128]{2,1,0:T(8,128)(2,1)S(1)}, u32[]{:S(2)}, u32[]{:S(2)}) async-start(bf16[8,128,128]{2,1,0:T(8,128)(2,1)} %shard_map.167), calls=%async_computation | async-start | bytes 524288 | tf_op jit(solution)/shard_map/all_to_all | solution.py:220
  23.8 0.0 copy-done.6
  23.8 0.0 copy-done.5
  23.8 0.0 copy-done.1
  23.9 0.0 copy-done.8
  23.9 0.0 copy-done.7
  23.9 0.0 copy-start.4
  23.9 1.0 copy-done.4
  24.9 1.1 shard_map.165
  25.9 0.0 copy-done.3
  26.0 1.1 shard_map.166
  27.1 0.0 copy-start
  27.1 1.3 %copy-done = bf16[32,264,128]{2,1,0:T(8,128)(2,1)} copy-done((bf16[32,264,128]{2,1,0:T(8,128)(2,1)}, bf16[32,264,128]{2,1,0:T(8,128)(2,1)S(1)}, u32[]{:S(2)}) %copy-start) | copy-done | bytes 2162712
  28.4 7.7 %all-to-all-done.a_ref = bf16[8,128,128]{2,1,0:T(8,128)(2,1)S(1)} async-done(((bf16[8,128,128]{2,1,0:T(8,128)(2,1)}), bf16[8,128,128]{2,1,0:T(8,128)(2,1)S(1)}, u32[]{:S(2)}, u32[]{:S(2)}) %all-to-all-start) | async-done | bytes 262176 | tf_op jit(solution)/shard_map/all_to_all | solution.py:220
  36.1 4.1 %all-to-all-start.1 = ((bf16[32,264,128]{2,1,0:T(8,128)(2,1)}), bf16[32,264,128]{2,1,0:T(8,128)(2,1)S(1)}, u32[]{:S(2)}, u32[]{:S(2)}) async-start(bf16[32,264,128]{2,1,0:T(8,128)(2,1)} %copy-done), calls=%async_computation.1 | async-start | bytes 4325376 | tf_op jit(solution)/shard_map/all_to_all | solution.py:216
  40.2 3.0 %collective-permute-start.1 = (f32[128,128]{1,0:T(8,128)S(1)}, f32[128,128]{1,0:T(8,128)S(1)}, u32[]{:S(2)}, u32[]{:S(2)}) collective-permute-start(f32[128,128]{1,0:T(8,128)S(1)} %shard_map.168), channel_id=1, source_target_pairs={{0,24},{24,0},{48,72},{72,48},{96,120},{120,96},{144,168},{168,144... | collective-permute-start | bytes 196616 | tf_op jit(solution)/shard_map/ppermute | solution.py:223
  43.2 3.3 %collective-permute-done.1 = f32[128,128]{1,0:T(8,128)S(1)} collective-permute-done((f32[128,128]{1,0:T(8,128)S(1)}, f32[128,128]{1,0:T(8,128)S(1)}, u32[]{:S(2)}, u32[]{:S(2)}) %collective-permute-start.1) | collective-permute-done | bytes 65568 | tf_op jit(solution)/shard_map/ppermute | solution.py:223
  46.5 4.0 %collective-permute-start.2 = (f32[128,128]{1,0:T(8,128)S(1)}, f32[128,128]{1,0:T(8,128)S(1)}, u32[]{:S(2)}, u32[]{:S(2)}) collective-permute-start(f32[128,128]{1,0:T(8,128)S(1)} %add.12), channel_id=1, source_target_pairs={{0,48},{24,72},{48,0},{72,24},{96,144},{120,168},{144,96},{168,120... | collective-permute-start | bytes 196616 | tf_op jit(solution)/shard_map/ppermute | solution.py:223
  50.6 2.8 %collective-permute-done.2 = f32[128,128]{1,0:T(8,128)S(1)} collective-permute-done((f32[128,128]{1,0:T(8,128)S(1)}, f32[128,128]{1,0:T(8,128)S(1)}, u32[]{:S(2)}, u32[]{:S(2)}) %collective-permute-start.2) | collective-permute-done | bytes 65568 | tf_op jit(solution)/shard_map/ppermute | solution.py:223
  53.3 1.9 %collective-permute-start.3 = (f32[128,128]{1,0:T(8,128)S(1)}, f32[128,128]{1,0:T(8,128)S(1)}, u32[]{:S(2)}, u32[]{:S(2)}) collective-permute-start(f32[128,128]{1,0:T(8,128)S(1)} %add.13), channel_id=1, source_target_pairs={{2,0},{3,1},{0,2},{1,3},{6,4},{7,5},{4,6},{5,7},{10,8},{11,9},{8,1... | collective-permute-start | bytes 196616 | tf_op jit(solution)/shard_map/ppermute | solution.py:213
  55.3 3.4 %collective-permute-done.3 = f32[128,128]{1,0:T(8,128)S(1)} collective-permute-done((f32[128,128]{1,0:T(8,128)S(1)}, f32[128,128]{1,0:T(8,128)S(1)}, u32[]{:S(2)}, u32[]{:S(2)}) %collective-permute-start.3) | collective-permute-done | bytes 65568 | tf_op jit(solution)/shard_map/ppermute | solution.py:213
  58.7 3.0 %collective-permute-start.4 = (f32[128,128]{1,0:T(8,128)S(1)}, f32[128,128]{1,0:T(8,128)S(1)}, u32[]{:S(2)}, u32[]{:S(2)}) collective-permute-start(f32[128,128]{1,0:T(8,128)S(1)} %add.14), channel_id=1, source_target_pairs={{4,0},{5,1},{6,2},{7,3},{0,4},{1,5},{2,6},{3,7},{12,8},{13,9},{14,... | collective-permute-start | bytes 196616 | tf_op jit(solution)/shard_map/ppermute | solution.py:213
  61.7 3.8 %collective-permute-done.4 = f32[128,128]{1,0:T(8,128)S(1)} collective-permute-done((f32[128,128]{1,0:T(8,128)S(1)}, f32[128,128]{1,0:T(8,128)S(1)}, u32[]{:S(2)}, u32[]{:S(2)}) %collective-permute-start.4) | collective-permute-done | bytes 65568 | tf_op jit(solution)/shard_map/ppermute | solution.py:213
  65.5 10.2 %collective-permute-start.6 = (f32[128,128]{1,0:T(8,128)S(1)}, f32[128,128]{1,0:T(8,128)S(1)}, u32[]{:S(2)}, u32[]{:S(2)}) collective-permute-start(f32[128,128]{1,0:T(8,128)S(1)} %add.15.own_ref), channel_id=1, source_target_pairs={{8,0},{9,1},{10,2},{11,3},{12,4},{13,5},{14,6},{15,7},{16,8},{17,9... | collective-permute-start | bytes 196616 | tf_op jit(solution)/shard_map/ppermute | solution.py:213
  75.8 1.9 %collective-permute-start.5 = (f32[128,128]{1,0:T(8,128)S(1)}, f32[128,128]{1,0:T(8,128)S(1)}, u32[]{:S(2)}, u32[]{:S(2)}) collective-permute-start(f32[128,128]{1,0:T(8,128)S(1)} %add.15.own_ref), channel_id=1, source_target_pairs={{16,0},{17,1},{18,2},{19,3},{20,4},{21,5},{22,6},{23,7},{0,8},{1,9... | collective-permute-start | bytes 196616 | tf_op jit(solution)/shard_map/ppermute | solution.py:213
  77.7 0.0 collective-permute-done.6.two_ref
  77.7 7.3 %collective-permute-done.5.one_ref = f32[128,128]{1,0:T(8,128)S(1)} collective-permute-done((f32[128,128]{1,0:T(8,128)S(1)}, f32[128,128]{1,0:T(8,128)S(1)}, u32[]{:S(2)}, u32[]{:S(2)}) %collective-permute-start.5) | collective-permute-done | bytes 65568 | tf_op jit(solution)/shard_map/ppermute | solution.py:213
  85.0 0.8 shard_map.169
  85.7 4.3 %all-to-all-done.1.refs_0_ = bf16[32,264,128]{2,1,0:T(8,128)(2,1)S(1)} async-done(((bf16[32,264,128]{2,1,0:T(8,128)(2,1)}), bf16[32,264,128]{2,1,0:T(8,128)(2,1)S(1)}, u32[]{:S(2)}, u32[]{:S(2)}) %all-to-all-start.1) | async-done | bytes 2162720 | tf_op jit(solution)/shard_map/all_to_all | solution.py:216
  90.0 5.0 %all-to-all-start.2 = ((bf16[8,128,128]{2,1,0:T(8,128)(2,1)}), bf16[8,128,128]{2,1,0:T(8,128)(2,1)S(1)}, u32[]{:S(2)}, u32[]{:S(2)}) async-start(bf16[8,128,128]{2,1,0:T(8,128)(2,1)} %shard_map.169), calls=%async_computation.2 | async-start | bytes 524288 | tf_op jit(solution)/shard_map/all_to_all | solution.py:220
  95.0 0.1 slice.3
  95.1 0.6 convert_reduce_fusion
  95.8 0.1 reshape.18.index_ref
  95.9 1.8 %shard_map.171 = bf16[1024,256]{1,0:T(8,128)(2,1)} custom-call(s32[64]{0:T(128)S(1)} %reshape.18.index_ref, bf16[32,264,128]{2,1,0:T(8,128)(2,1)S(1)} %all-to-all-done.1.refs_0_), custom_call_target="tpu_custom_call" | custom-call | flops 1000000 | bytes 2097152 | tf_op jit(solution)/shard_map/pallas_call | solution.py:269
  97.7 1.8 %shard_map.170 = bf16[1024,256]{1,0:T(8,128)(2,1)} custom-call(s32[64]{0:T(128)S(1)} %reshape.18.index_ref, bf16[32,264,128]{2,1,0:T(8,128)(2,1)S(1)} %all-to-all-done.1.refs_0_), custom_call_target="tpu_custom_call" | custom-call | flops 1000000 | bytes 2097152 | tf_op jit(solution)/shard_map/pallas_call | solution.py:269
  99.5 4.9 %all-to-all-done.2.mine_ref = bf16[8,128,128]{2,1,0:T(8,128)(2,1)S(1)} async-done(((bf16[8,128,128]{2,1,0:T(8,128)(2,1)}), bf16[8,128,128]{2,1,0:T(8,128)(2,1)S(1)}, u32[]{:S(2)}, u32[]{:S(2)}) %all-to-all-start.2) | async-done | bytes 262176 | tf_op jit(solution)/shard_map/all_to_all | solution.py:220
  104.3 13.4 %collective-permute-start.7 = (bf16[8,128,128]{2,1,0:T(8,128)(2,1)S(1)}, bf16[8,128,128]{2,1,0:T(8,128)(2,1)S(1)}, u32[]{:S(2)}, u32[]{:S(2)}) collective-permute-start(bf16[8,128,128]{2,1,0:T(8,128)(2,1)S(1)} %all-to-all-done.2.mine_ref), channel_id=1, source_target_pairs={{0,1},{1,0},{2,3},{3,2},{4,5},{5,4},{6,7},{7,6},{8,9},{9,8},{10,11... | collective-permute-start | bytes 786440 | tf_op jit(solution)/shard_map/ppermute | solution.py:277
  117.8 1.1 collective-permute-done.7.other_ref
  118.9 1.1 shard_map.172
  (5 shorter events, 0.1 us)
Async XLA Ops:
  0.6 23.2 %copy-start.6 = (s32[4]{0:T(128)S(1)}, s32[4]{0:T(128)}, u32[]{:S(2)}) copy-start(s32[4]{0:T(128)} %count_ref.3) | copy-start | bytes 52
  0.6 23.2 %copy-start.5 = (s32[4]{0:T(128)S(1)}, s32[4]{0:T(128)}, u32[]{:S(2)}) copy-start(s32[4]{0:T(128)} %user_ref.3) | copy-start | bytes 52
  0.7 23.2 %copy-start.1 = (bf16[4,256,256]{2,1,0:T(8,128)(2,1)S(1)}, bf16[4,256,256]{2,1,0:T(8,128)(2,1)}, u32[]{:S(2)}) copy-start(bf16[4,256,256]{2,1,0:T(8,128)(2,1)} %adj_ref.3) | copy-start | bytes 1572868
  0.7 23.2 %copy-start.8 = (s32[32]{0:T(128)S(1)}, s32[32]{0:T(128)}, u32[]{:S(2)}) copy-start(s32[32]{0:T(128)} %item_ref.1) | copy-start | bytes 388
  0.7 23.2 %copy-start.7 = (s32[32,1]{0,1:T(1,128)S(1)}, s32[32,1]{0,1:T(1,128)}, u32[]{:S(2)}) copy-start(s32[32,1]{0,1:T(1,128)} %param.24) | copy-start | bytes 388
  4.8 13.8 %collective-permute-start = (bf16[2,256,256]{2,1,0:T(8,128)(2,1)}, bf16[2,256,256]{2,1,0:T(8,128)(2,1)S(1)}, u32[]{:S(2)}, u32[]{:S(2)}) collective-permute-start(bf16[2,256,256]{2,1,0:T(8,128)(2,1)} %get-tuple-element.27), channel_id=1, source_target_pairs={{0,1},{1,0},{2,3},{3,2},{4,5},{5,4},{6,7},{7,6},{8,9},{9,8},{10,11... | collective-permute-start | bytes 786440 | tf_op jit(solution)/shard_map/ppermute | solution.py:242
  18.6 1.0 copy-start.2
  19.7 6.3 %copy-start.3 = (bf16[768,256]{1,0:T(8,128)(2,1)S(1)}, bf16[768,256]{1,0:T(8,128)(2,1)}, u32[]{:S(2)}) copy-start(bf16[768,256]{1,0:T(8,128)(2,1)} %get-tuple-element.22.dmsg_ref) | copy-start | bytes 1179652
  20.4 15.7 %all-to-all-start = ((bf16[8,128,128]{2,1,0:T(8,128)(2,1)}), bf16[8,128,128]{2,1,0:T(8,128)(2,1)S(1)}, u32[]{:S(2)}, u32[]{:S(2)}) async-start(bf16[8,128,128]{2,1,0:T(8,128)(2,1)} %shard_map.167), calls=%async_computation | async-start | bytes 524288 | tf_op jit(solution)/shard_map/all_to_all | solution.py:220
  23.9 1.0 copy-start.4
  27.1 1.4 %copy-start = (bf16[32,264,128]{2,1,0:T(8,128)(2,1)}, bf16[32,264,128]{2,1,0:T(8,128)(2,1)S(1)}, u32[]{:S(2)}) copy-start(bf16[32,264,128]{2,1,0:T(8,128)(2,1)S(1)} %shard_map.166) | copy-start | bytes 6488068
  36.1 53.9 %all-to-all-start.1 = ((bf16[32,264,128]{2,1,0:T(8,128)(2,1)}), bf16[32,264,128]{2,1,0:T(8,128)(2,1)S(1)}, u32[]{:S(2)}, u32[]{:S(2)}) async-start(bf16[32,264,128]{2,1,0:T(8,128)(2,1)} %copy-done), calls=%async_computation.1 | async-start | bytes 4325376 | tf_op jit(solution)/shard_map/all_to_all | solution.py:216
  40.2 6.3 %collective-permute-start.1 = (f32[128,128]{1,0:T(8,128)S(1)}, f32[128,128]{1,0:T(8,128)S(1)}, u32[]{:S(2)}, u32[]{:S(2)}) collective-permute-start(f32[128,128]{1,0:T(8,128)S(1)} %shard_map.168), channel_id=1, source_target_pairs={{0,24},{24,0},{48,72},{72,48},{96,120},{120,96},{144,168},{168,144... | collective-permute-start | bytes 196616 | tf_op jit(solution)/shard_map/ppermute | solution.py:223
  46.5 6.8 %collective-permute-start.2 = (f32[128,128]{1,0:T(8,128)S(1)}, f32[128,128]{1,0:T(8,128)S(1)}, u32[]{:S(2)}, u32[]{:S(2)}) collective-permute-start(f32[128,128]{1,0:T(8,128)S(1)} %add.12), channel_id=1, source_target_pairs={{0,48},{24,72},{48,0},{72,24},{96,144},{120,168},{144,96},{168,120... | collective-permute-start | bytes 196616 | tf_op jit(solution)/shard_map/ppermute | solution.py:223
  53.3 5.3 %collective-permute-start.3 = (f32[128,128]{1,0:T(8,128)S(1)}, f32[128,128]{1,0:T(8,128)S(1)}, u32[]{:S(2)}, u32[]{:S(2)}) collective-permute-start(f32[128,128]{1,0:T(8,128)S(1)} %add.13), channel_id=1, source_target_pairs={{2,0},{3,1},{0,2},{1,3},{6,4},{7,5},{4,6},{5,7},{10,8},{11,9},{8,1... | collective-permute-start | bytes 196616 | tf_op jit(solution)/shard_map/ppermute | solution.py:213
  58.7 6.9 %collective-permute-start.4 = (f32[128,128]{1,0:T(8,128)S(1)}, f32[128,128]{1,0:T(8,128)S(1)}, u32[]{:S(2)}, u32[]{:S(2)}) collective-permute-start(f32[128,128]{1,0:T(8,128)S(1)} %add.14), channel_id=1, source_target_pairs={{4,0},{5,1},{6,2},{7,3},{0,4},{1,5},{2,6},{3,7},{12,8},{13,9},{14,... | collective-permute-start | bytes 196616 | tf_op jit(solution)/shard_map/ppermute | solution.py:213
  65.5 12.2 %collective-permute-start.6 = (f32[128,128]{1,0:T(8,128)S(1)}, f32[128,128]{1,0:T(8,128)S(1)}, u32[]{:S(2)}, u32[]{:S(2)}) collective-permute-start(f32[128,128]{1,0:T(8,128)S(1)} %add.15.own_ref), channel_id=1, source_target_pairs={{8,0},{9,1},{10,2},{11,3},{12,4},{13,5},{14,6},{15,7},{16,8},{17,9... | collective-permute-start | bytes 196616 | tf_op jit(solution)/shard_map/ppermute | solution.py:213
  75.8 9.2 %collective-permute-start.5 = (f32[128,128]{1,0:T(8,128)S(1)}, f32[128,128]{1,0:T(8,128)S(1)}, u32[]{:S(2)}, u32[]{:S(2)}) collective-permute-start(f32[128,128]{1,0:T(8,128)S(1)} %add.15.own_ref), channel_id=1, source_target_pairs={{16,0},{17,1},{18,2},{19,3},{20,4},{21,5},{22,6},{23,7},{0,8},{1,9... | collective-permute-start | bytes 196616 | tf_op jit(solution)/shard_map/ppermute | solution.py:213
  90.0 14.3 %all-to-all-start.2 = ((bf16[8,128,128]{2,1,0:T(8,128)(2,1)}), bf16[8,128,128]{2,1,0:T(8,128)(2,1)S(1)}, u32[]{:S(2)}, u32[]{:S(2)}) async-start(bf16[8,128,128]{2,1,0:T(8,128)(2,1)} %shard_map.169), calls=%async_computation.2 | async-start | bytes 524288 | tf_op jit(solution)/shard_map/all_to_all | solution.py:220
  104.3 14.6 %collective-permute-start.7 = (bf16[8,128,128]{2,1,0:T(8,128)(2,1)S(1)}, bf16[8,128,128]{2,1,0:T(8,128)(2,1)S(1)}, u32[]{:S(2)}, u32[]{:S(2)}) collective-permute-start(bf16[8,128,128]{2,1,0:T(8,128)(2,1)S(1)} %all-to-all-done.2.mine_ref), channel_id=1, source_target_pairs={{0,1},{1,0},{2,3},{3,2},{4,5},{5,4},{6,7},{7,6},{8,9},{9,8},{10,11... | collective-permute-start | bytes 786440 | tf_op jit(solution)/shard_map/ppermute | solution.py:277

commit v8 on v6

--- a/solution.py
+++ b/solution.py
@@ -36,9 +36,10 @@
 
 def user_kernel(*refs):
     ins, rest = refs[:8], refs[8:]
-    dmsg2_ref, dmsg1_ref, user_grad_ref, keep_ref, send_ref = rest[:5]
-    bufs, sum2_s, prod2_s, delta2_s, sum1_s, prod1_s, delta1_s, sems = rest[5:13], *rest[13:]
-    blocks = ins[0].shape[0] // BLK
+    near_ref, dmsg1_ref, user_grad_ref, send_ref = rest[:4]
+    bufs, sum2_s, prod2_s, delta2_s, sum1_s, prod1_s, delta1_s, sems = rest[4:12], *rest[12:]
+    users = ins[0].shape[0]
+    blocks = users // BLK
     weights = [pltpu.make_async_copy(ins[i], bufs[i], sems.at[i]) for i in (6, 7)]
     for copy in weights:
         copy.start()
@@ -66,7 +67,7 @@
         prod2_s[rows, :] = (msg * prev).astype(BF)
         back_self = dot_t(deltas, ws[1])
         back_inter = dot_t(deltas, wi[1])
-        dmsg2_ref[rows, :] = (back_self + back_inter * prev).astype(BF)
+        near_ref[rows, :] = (back_self + back_inter * prev).astype(BF)
         dprev = back_self + back_inter * msg
         deltas = (dprev * jnp.where(one > 0, 1.0, SLOPE)).astype(BF)
         msg = msg1[rows, :].astype(F32)
@@ -82,7 +83,7 @@
     for at, (sum_s, prod_s, delta_s) in enumerate(((sum2_s, prod2_s, delta2_s), (sum1_s, prod1_s, delta1_s))):
         grad_self = tdot(sum_s[...], delta_s[...])
         grad_inter = tdot(prod_s[...], delta_s[...])
-        keep_ref[at] = jnp.where(even, grad_self, grad_inter)
+        near_ref[users + at * FEAT : users + (at + 1) * FEAT, :] = jnp.where(even, grad_self, grad_inter).astype(BF)
         send_ref[at] = jnp.where(even, grad_inter, grad_self).astype(BF)
 
 
@@ -135,14 +136,18 @@
         rest_ref[o] = slots_s[1, o, 32:64, :]
 
 
-def pack_kernel(two_ref, keep_ref, got_ref, a_ref):
-    for o in range(OWNERS):
-        a_ref[o, 0:32, :] = two_ref[0, o, 0:32, :]
-        rows = slice(8 * o, 8 * o + 8)
+def pack_kernel(two_ref, near_ref, got_ref, a_ref):
+    kept = near_ref.shape[0] - got_ref.shape[0] * FEAT
+    for o in range(0, OWNERS, 2):
+        for p in range(2):
+            a_ref[o + p, 0:32, :] = two_ref[0, o + p, 0:32, :]
         for at in range(2):
-            total = keep_ref[at, rows, :] + got_ref[at, rows, :].astype(F32)
-            first = 32 + 16 * at
-            a_ref[o, first : first + 16, :] = jnp.concatenate([total[:, :HALF], total[:, HALF:]], axis=0).astype(BF)
+            first = kept + at * FEAT + 8 * o
+            total = near_ref[first : first + 16, :].astype(F32) + got_ref[at, 8 * o : 8 * o + 16, :].astype(F32)
+            for p in range(2):
+                part = total[8 * p : 8 * p + 8, :]
+                part = jnp.concatenate([part[:, :HALF], part[:, HALF:]], axis=0)
+                a_ref[o + p, 32 + 16 * at : 48 + 16 * at, :] = part.astype(BF)
 
 
 def chunk_kernel(a_ref, total_ref):
@@ -229,9 +234,9 @@
     ranks = [pltpu.SMEM((OWNERS,), jnp.int32)] * 2
     small = dict(flops=1_000_000, bytes_accessed=2 << 20)
     tile = dict(flops=140_000_000, bytes_accessed=2 << 20)
-    dmsg2, dmsg1, user_grad, keep, send = call(
+    near, dmsg1, user_grad, send = call(
         user_kernel,
-        [user, user, user, both, (both[0], BF)],
+        [((users + 2 * FEAT, FEAT), BF), user, user, (both[0], BF)],
         [HBM] * 8,
         [pltpu.VMEM((users, FEAT), BF)] * 6 + [pltpu.VMEM((2, FEAT, FEAT), BF)] * 2
         + [pltpu.VMEM((users, FEAT), BF)] * 6 + [pltpu.SemaphoreType.DMA((8 + 6 * (users // BLK),))],
@@ -241,8 +246,8 @@
     two, index_rows = call(
         two_kernel, [((2, OWNERS, 64, HALF), BF), rows(8)], [SMEM] * 4 + [VMEM] * 2,
         ranks + [pltpu.SMEM((2 * OWNERS,), jnp.int32)], **tile,
-    )(tile_user, counts, dest, item_block, adjacency, dmsg2)
-    (a,) = call(pack_kernel, [rows(64)], [VMEM] * 3, **small)(two, keep, got)
+    )(tile_user, counts, dest, item_block, adjacency, near)
+    (a,) = call(pack_kernel, [rows(64)], [VMEM] * 3, **small)(two, near, got)
     got_a = to_owners(a)
 
     b, rest = call(

time: 116 us -> 115 us (level)
    unnamed x18 -> x16, local copies, waits for them, and re-layouts: 3.25 us -> 2.29 us
where the time goes in v8:
time: 115 us
  starting transfers between devices  51.9 us (45%)
  waiting for transfers between devices  45.9 us (40%)
  Pallas kernels  12.9 us (11%)
  local copies, waits for them, and re-layouts  2.55 us (2%)
    all_to_all x3, waiting for transfers between devices, to_owners(): return lax.all_to_all(x, 'owner', split_axis=0, concat_axis=0, tiled=True)  34.2 us
    ppermute x4, starting transfers between devices, from_z(): lax.ppermute(x, 'rep', [(2 * source(z) + c, 2 * z + c) for z in range(z_c...  18 us
    all_to_all x3, starting transfers between devices, to_owners(): return lax.all_to_all(x, 'owner', split_axis=0, concat_axis=0, tiled=True)  15.2 us
    ppermute x1, starting transfers between devices, local(): got = lax.ppermute(send, 'rep', swap)  12.4 us
    ppermute x4, waiting for transfers between devices, from_z(): lax.ppermute(x, 'rep', [(2 * source(z) + c, 2 * z + c) for z in range(z_c...  11.7 us
    ppermute x1, starting transfers between devices, local(): other = lax.ppermute(got_c[:, 32:64], 'rep', swap)  6.29 us
    pallas_call x1, Pallas kernels, local(): call(user_kernel, [((users + 2 * FEAT, FEAT), BF), user, user, (both[0],...  4.18 us
    pallas_call x2, Pallas kernels, collect(): call(functools.partial(collect_kernel, cuts), [((OWNERS * RB, FEAT), BF)]...  3.72 us
  transfers between devices with their start and end apart: 9, of which 6 were waited for; matrix products, arithmetic and copies ran while one was open for 1% of the time, Pallas kernels for 6%

profile of v8, /device:TPU:1, one launch (start us, length us, event | category | flops | bytes accessed | tf_op | source)
XLA Modules:
  0.0 114.8 jit_solution(10150944686224559453)
XLA Ops:
  0.6 0.0 copy-start.5
  0.6 0.0 copy-start.4
  0.7 0.0 copy-start.1
  0.7 0.0 copy-start.7
  0.7 0.0 copy-start.6
  0.7 4.2 %shard_map.164 = (bf16[1280,256]{1,0:T(8,128)(2,1)}, bf16[768,256]{1,0:T(8,128)(2,1)}, bf16[768,256]{1,0:T(8,128)(2,1)}, bf16[2,256,256]{2,1,0:T(8,128)(2,1)}) custom-call(bf16[768,256]{1,0:T(8,128)(2,1)} %refs_0_.1, bf16[768,256]{1,0:T(8,128)(2,1)} %refs_1_.1, bf16[768,256]{1,0:T(8,128)(2,1)} %refs_2_.1, bf16[768,256]{1,0:T(8,128)(2,1)} %refs_3_.1, ...), custom_call_target="tpu_custom_call" | custom-call | flops 900000000 | bytes 6291456 | tf_op jit(solution)/shard_map/pallas_call | solution.py:237
  4.9 12.4 %collective-permute-start = (bf16[2,256,256]{2,1,0:T(8,128)(2,1)}, bf16[2,256,256]{2,1,0:T(8,128)(2,1)S(1)}, u32[]{:S(2)}, u32[]{:S(2)}) collective-permute-start(bf16[2,256,256]{2,1,0:T(8,128)(2,1)} %get-tuple-element.27), channel_id=1, source_target_pairs={{0,1},{1,0},{2,3},{3,2},{4,5},{5,4},{6,7},{7,6},{8,9},{9,8},{10,11... | collective-permute-start | bytes 786440 | tf_op jit(solution)/shard_map/ppermute | solution.py:245
  17.3 0.0 copy-done.5
  17.3 0.0 copy-done.4
  17.3 0.0 copy-done.1
  17.3 0.0 copy-done.7
  17.3 0.0 copy-done.6
  17.4 0.0 copy-start
  17.4 1.1 copy-done
  18.4 1.1 shard_map.165
  19.5 0.0 collective-permute-done.got_ref
  19.5 0.0 copy-start.3
  19.5 0.9 shard_map.167
  20.4 3.9 %all-to-all-start = ((bf16[32,64,128]{2,1,0:T(8,128)(2,1)}), bf16[32,64,128]{2,1,0:T(8,128)(2,1)S(1)}, u32[]{:S(2)}, u32[]{:S(2)}) async-start(bf16[32,64,128]{2,1,0:T(8,128)(2,1)} %shard_map.167), calls=%async_computation | async-start | bytes 1048576 | tf_op jit(solution)/shard_map/all_to_all | solution.py:226
  24.3 0.0 copy-done.3
  24.3 1.1 shard_map.166
  25.4 0.0 copy-start.2
  25.4 1.2 %copy-done.2 = bf16[32,200,128]{2,1,0:T(8,128)(2,1)} copy-done((bf16[32,200,128]{2,1,0:T(8,128)(2,1)}, bf16[32,200,128]{2,1,0:T(8,128)(2,1)S(1)}, u32[]{:S(2)}) %copy-start.2) | copy-done | bytes 1638424
  26.6 14.9 %all-to-all-done.a_ref.refs_0_ = bf16[32,64,128]{2,1,0:T(8,128)(2,1)S(1)} async-done(((bf16[32,64,128]{2,1,0:T(8,128)(2,1)}), bf16[32,64,128]{2,1,0:T(8,128)(2,1)S(1)}, u32[]{:S(2)}, u32[]{:S(2)}) %all-to-all-start) | async-done | bytes 524320 | tf_op jit(solution)/shard_map/all_to_all | solution.py:226
  41.5 4.7 %all-to-all-start.1 = ((bf16[32,200,128]{2,1,0:T(8,128)(2,1)}), bf16[32,200,128]{2,1,0:T(8,128)(2,1)S(1)}, u32[]{:S(2)}, u32[]{:S(2)}) async-start(bf16[32,200,128]{2,1,0:T(8,128)(2,1)} %copy-done.2), calls=%async_computation.1 | async-start | bytes 3276800 | tf_op jit(solution)/shard_map/all_to_all | solution.py:226
  46.2 1.9 %collective-permute-start.1 = (f32[32,128]{1,0:T(8,128)S(1)}, f32[32,128]{1,0:T(8,128)S(1)}, u32[]{:S(2)}, u32[]{:S(2)}) collective-permute-start(f32[32,128]{1,0:T(8,128)S(1)} %shard_map.168), channel_id=1, source_target_pairs={{2,0},{3,1},{0,2},{1,3},{6,4},{7,5},{4,6},{5,7},{10,8},{11,9},{8,1... | collective-permute-start | bytes 49160 | tf_op jit(solution)/shard_map/ppermute | solution.py:223
  48.1 2.6 %collective-permute-done.1 = f32[32,128]{1,0:T(8,128)S(1)} collective-permute-done((f32[32,128]{1,0:T(8,128)S(1)}, f32[32,128]{1,0:T(8,128)S(1)}, u32[]{:S(2)}, u32[]{:S(2)}) %collective-permute-start.1) | collective-permute-done | bytes 16416 | tf_op jit(solution)/shard_map/ppermute | solution.py:223
  50.7 3.4 %collective-permute-start.2 = (f32[32,128]{1,0:T(8,128)S(1)}, f32[32,128]{1,0:T(8,128)S(1)}, u32[]{:S(2)}, u32[]{:S(2)}) collective-permute-start(f32[32,128]{1,0:T(8,128)S(1)} %add.6), channel_id=1, source_target_pairs={{4,0},{5,1},{6,2},{7,3},{0,4},{1,5},{2,6},{3,7},{12,8},{13,9},{14,... | collective-permute-start | bytes 49160 | tf_op jit(solution)/shard_map/ppermute | solution.py:223
  54.1 2.4 %collective-permute-done.2 = f32[32,128]{1,0:T(8,128)S(1)} collective-permute-done((f32[32,128]{1,0:T(8,128)S(1)}, f32[32,128]{1,0:T(8,128)S(1)}, u32[]{:S(2)}, u32[]{:S(2)}) %collective-permute-start.2) | collective-permute-done | bytes 16416 | tf_op jit(solution)/shard_map/ppermute | solution.py:223
  56.5 10.7 %collective-permute-start.4 = (f32[32,128]{1,0:T(8,128)S(1)}, f32[32,128]{1,0:T(8,128)S(1)}, u32[]{:S(2)}, u32[]{:S(2)}) collective-permute-start(f32[32,128]{1,0:T(8,128)S(1)} %add.7.own_ref), channel_id=1, source_target_pairs={{8,0},{9,1},{10,2},{11,3},{12,4},{13,5},{14,6},{15,7},{16,8},{17,9... | collective-permute-start | bytes 49160 | tf_op jit(solution)/shard_map/ppermute | solution.py:223
  67.3 1.9 %collective-permute-start.3 = (f32[32,128]{1,0:T(8,128)S(1)}, f32[32,128]{1,0:T(8,128)S(1)}, u32[]{:S(2)}, u32[]{:S(2)}) collective-permute-start(f32[32,128]{1,0:T(8,128)S(1)} %add.7.own_ref), channel_id=1, source_target_pairs={{16,0},{17,1},{18,2},{19,3},{20,4},{21,5},{22,6},{23,7},{0,8},{1,9... | collective-permute-start | bytes 49160 | tf_op jit(solution)/shard_map/ppermute | solution.py:223
  69.2 0.0 collective-permute-done.4.two_ref
  69.2 6.7 %collective-permute-done.3.one_ref = f32[32,128]{1,0:T(8,128)S(1)} collective-permute-done((f32[32,128]{1,0:T(8,128)S(1)}, f32[32,128]{1,0:T(8,128)S(1)}, u32[]{:S(2)}, u32[]{:S(2)}) %collective-permute-start.3) | collective-permute-done | bytes 16416 | tf_op jit(solution)/shard_map/ppermute | solution.py:223
  76.0 0.9 shard_map.169
  76.8 7.5 %all-to-all-done.1.refs_1_.refs_0_ = bf16[32,200,128]{2,1,0:T(8,128)(2,1)S(1)} async-done(((bf16[32,200,128]{2,1,0:T(8,128)(2,1)}), bf16[32,200,128]{2,1,0:T(8,128)(2,1)S(1)}, u32[]{:S(2)}, u32[]{:S(2)}) %all-to-all-start.1) | async-done | bytes 1638432 | tf_op jit(solution)/shard_map/all_to_all | solution.py:226
  84.3 6.7 %all-to-all-start.2 = ((bf16[32,64,128]{2,1,0:T(8,128)(2,1)}), bf16[32,64,128]{2,1,0:T(8,128)(2,1)S(1)}, u32[]{:S(2)}, u32[]{:S(2)}) async-start(bf16[32,64,128]{2,1,0:T(8,128)(2,1)} %shard_map.169), calls=%async_computation.2 | async-start | bytes 1048576 | tf_op jit(solution)/shard_map/all_to_all | solution.py:226
  91.0 0.1 slice.6
  91.1 0.6 convert_reduce_fusion
  91.8 0.1 reshape.18.index_ref
  91.9 1.9 %shard_map.170 = bf16[1024,256]{1,0:T(8,128)(2,1)} custom-call(s32[64]{0:T(128)S(1)} %reshape.18.index_ref, bf16[32,64,128]{2,1,0:T(8,128)(2,1)S(1)} %all-to-all-done.a_ref.refs_0_, bf16[32,200,128]{2,1,0:T(8,128)(2,1)S(1)} %all-to-all-done.1.refs_1_.refs_0_), custom_call_target="tpu_custom_call" | custom-call | flops 1000000 | bytes 2097152 | tf_op jit(solution)/shard_map/pallas_call | solution.py:271
  93.7 11.8 %all-to-all-done.2.refs_1_.mine_ref = bf16[32,64,128]{2,1,0:T(8,128)(2,1)S(1)} async-done(((bf16[32,64,128]{2,1,0:T(8,128)(2,1)}), bf16[32,64,128]{2,1,0:T(8,128)(2,1)S(1)}, u32[]{:S(2)}, u32[]{:S(2)}) %all-to-all-start.2) | async-done | bytes 524320 | tf_op jit(solution)/shard_map/all_to_all | solution.py:226
  105.6 6.3 %collective-permute-start.5 = (bf16[32,32,128]{2,1,0:T(8,128)(2,1)S(1)}, bf16[32,32,128]{2,1,0:T(8,128)(2,1)S(1)}, u32[]{:S(2)}, u32[]{:S(2)}) collective-permute-start(bf16[32,32,128]{2,1,0:T(8,128)(2,1)S(1)} %slice.7), channel_id=1, source_target_pairs={{0,1},{1,0},{2,3},{3,2},{4,5},{5,4},{6,7},{7,6},{8,9},{9,8},{10,11... | collective-permute-start | bytes 786440 | tf_op jit(solution)/shard_map/ppermute | solution.py:278
  111.9 1.9 %shard_map.171 = bf16[1024,256]{1,0:T(8,128)(2,1)} custom-call(s32[64]{0:T(128)S(1)} %reshape.18.index_ref, bf16[32,200,128]{2,1,0:T(8,128)(2,1)S(1)} %all-to-all-done.1.refs_1_.refs_0_, bf16[32,64,128]{2,1,0:T(8,128)(2,1)S(1)} %all-to-all-done.2.refs_1_.mine_ref), custom_call_target="tpu_custom_call" | custom-call | flops 1000000 | bytes 2097152 | tf_op jit(solution)/shard_map/pallas_call | solution.py:271
  113.7 0.0 collective-permute-done.5.other_ref
  113.7 1.1 shard_map.172
  (4 shorter events, 0.1 us)
Async XLA Ops:
  0.6 16.7 %copy-start.5 = (s32[4]{0:T(128)S(1)}, s32[4]{0:T(128)}, u32[]{:S(2)}) copy-start(s32[4]{0:T(128)} %count_ref.3) | copy-start | bytes 52
  0.6 16.7 %copy-start.4 = (s32[4]{0:T(128)S(1)}, s32[4]{0:T(128)}, u32[]{:S(2)}) copy-start(s32[4]{0:T(128)} %user_ref.3) | copy-start | bytes 52
  0.7 16.7 %copy-start.1 = (bf16[4,256,256]{2,1,0:T(8,128)(2,1)S(1)}, bf16[4,256,256]{2,1,0:T(8,128)(2,1)}, u32[]{:S(2)}) copy-start(bf16[4,256,256]{2,1,0:T(8,128)(2,1)} %adj_ref.3) | copy-start | bytes 1572868
  0.7 16.7 %copy-start.7 = (s32[32]{0:T(128)S(1)}, s32[32]{0:T(128)}, u32[]{:S(2)}) copy-start(s32[32]{0:T(128)} %item_ref.1) | copy-start | bytes 388
  0.7 16.7 %copy-start.6 = (s32[32,1]{0,1:T(1,128)S(1)}, s32[32,1]{0,1:T(1,128)}, u32[]{:S(2)}) copy-start(s32[32,1]{0,1:T(1,128)} %param.24) | copy-start | bytes 388
  4.9 14.6 %collective-permute-start = (bf16[2,256,256]{2,1,0:T(8,128)(2,1)}, bf16[2,256,256]{2,1,0:T(8,128)(2,1)S(1)}, u32[]{:S(2)}, u32[]{:S(2)}) collective-permute-start(bf16[2,256,256]{2,1,0:T(8,128)(2,1)} %get-tuple-element.27), channel_id=1, source_target_pairs={{0,1},{1,0},{2,3},{3,2},{4,5},{5,4},{6,7},{7,6},{8,9},{9,8},{10,11... | collective-permute-start | bytes 786440 | tf_op jit(solution)/shard_map/ppermute | solution.py:245
  17.4 1.1 copy-start
  19.5 4.8 %copy-start.3 = (bf16[768,256]{1,0:T(8,128)(2,1)S(1)}, bf16[768,256]{1,0:T(8,128)(2,1)}, u32[]{:S(2)}) copy-start(bf16[768,256]{1,0:T(8,128)(2,1)} %get-tuple-element.22.dmsg_ref) | copy-start | bytes 1179652
  20.4 21.1 %all-to-all-start = ((bf16[32,64,128]{2,1,0:T(8,128)(2,1)}), bf16[32,64,128]{2,1,0:T(8,128)(2,1)S(1)}, u32[]{:S(2)}, u32[]{:S(2)}) async-start(bf16[32,64,128]{2,1,0:T(8,128)(2,1)} %shard_map.167), calls=%async_computation | async-start | bytes 1048576 | tf_op jit(solution)/shard_map/all_to_all | solution.py:226
  25.4 1.2 %copy-start.2 = (bf16[32,200,128]{2,1,0:T(8,128)(2,1)}, bf16[32,200,128]{2,1,0:T(8,128)(2,1)S(1)}, u32[]{:S(2)}) copy-start(bf16[32,200,128]{2,1,0:T(8,128)(2,1)S(1)} %get-tuple-element.30) | copy-start | bytes 4915204
  41.5 42.9 %all-to-all-start.1 = ((bf16[32,200,128]{2,1,0:T(8,128)(2,1)}), bf16[32,200,128]{2,1,0:T(8,128)(2,1)S(1)}, u32[]{:S(2)}, u32[]{:S(2)}) async-start(bf16[32,200,128]{2,1,0:T(8,128)(2,1)} %copy-done.2), calls=%async_computation.1 | async-start | bytes 3276800 | tf_op jit(solution)/shard_map/all_to_all | solution.py:226
  46.2 4.5 %collective-permute-start.1 = (f32[32,128]{1,0:T(8,128)S(1)}, f32[32,128]{1,0:T(8,128)S(1)}, u32[]{:S(2)}, u32[]{:S(2)}) collective-permute-start(f32[32,128]{1,0:T(8,128)S(1)} %shard_map.168), channel_id=1, source_target_pairs={{2,0},{3,1},{0,2},{1,3},{6,4},{7,5},{4,6},{5,7},{10,8},{11,9},{8,1... | collective-permute-start | bytes 49160 | tf_op jit(solution)/shard_map/ppermute | solution.py:223
  50.7 5.8 %collective-permute-start.2 = (f32[32,128]{1,0:T(8,128)S(1)}, f32[32,128]{1,0:T(8,128)S(1)}, u32[]{:S(2)}, u32[]{:S(2)}) collective-permute-start(f32[32,128]{1,0:T(8,128)S(1)} %add.6), channel_id=1, source_target_pairs={{4,0},{5,1},{6,2},{7,3},{0,4},{1,5},{2,6},{3,7},{12,8},{13,9},{14,... | collective-permute-start | bytes 49160 | tf_op jit(solution)/shard_map/ppermute | solution.py:223
  56.5 12.7 %collective-permute-start.4 = (f32[32,128]{1,0:T(8,128)S(1)}, f32[32,128]{1,0:T(8,128)S(1)}, u32[]{:S(2)}, u32[]{:S(2)}) collective-permute-start(f32[32,128]{1,0:T(8,128)S(1)} %add.7.own_ref), channel_id=1, source_target_pairs={{8,0},{9,1},{10,2},{11,3},{12,4},{13,5},{14,6},{15,7},{16,8},{17,9... | collective-permute-start | bytes 49160 | tf_op jit(solution)/shard_map/ppermute | solution.py:223
  67.3 8.7 %collective-permute-start.3 = (f32[32,128]{1,0:T(8,128)S(1)}, f32[32,128]{1,0:T(8,128)S(1)}, u32[]{:S(2)}, u32[]{:S(2)}) collective-permute-start(f32[32,128]{1,0:T(8,128)S(1)} %add.7.own_ref), channel_id=1, source_target_pairs={{16,0},{17,1},{18,2},{19,3},{20,4},{21,5},{22,6},{23,7},{0,8},{1,9... | collective-permute-start | bytes 49160 | tf_op jit(solution)/shard_map/ppermute | solution.py:223
  84.3 21.2 %all-to-all-start.2 = ((bf16[32,64,128]{2,1,0:T(8,128)(2,1)}), bf16[32,64,128]{2,1,0:T(8,128)(2,1)S(1)}, u32[]{:S(2)}, u32[]{:S(2)}) async-start(bf16[32,64,128]{2,1,0:T(8,128)(2,1)} %shard_map.169), calls=%async_computation.2 | async-start | bytes 1048576 | tf_op jit(solution)/shard_map/all_to_all | solution.py:226
  105.6 8.2 %collective-permute-start.5 = (bf16[32,32,128]{2,1,0:T(8,128)(2,1)S(1)}, bf16[32,32,128]{2,1,0:T(8,128)(2,1)S(1)}, u32[]{:S(2)}, u32[]{:S(2)}) collective-permute-start(bf16[32,32,128]{2,1,0:T(8,128)(2,1)S(1)} %slice.7), channel_id=1, source_target_pairs={{0,1},{1,0},{2,3},{3,2},{4,5},{5,4},{6,7},{7,6},{8,9},{9,8},{10,11... | collective-permute-start | bytes 786440 | tf_op jit(solution)/shard_map/ppermute | solution.py:278

commit v9 on v6

--- a/solution.py
+++ b/solution.py
@@ -36,9 +36,10 @@
 
 def user_kernel(*refs):
     ins, rest = refs[:8], refs[8:]
-    dmsg2_ref, dmsg1_ref, user_grad_ref, keep_ref, send_ref = rest[:5]
-    bufs, sum2_s, prod2_s, delta2_s, sum1_s, prod1_s, delta1_s, sems = rest[5:13], *rest[13:]
-    blocks = ins[0].shape[0] // BLK
+    dmsg2_ref, dmsg1_ref, user_grad_ref, a_ref = rest[:4]
+    bufs, sum2_s, prod2_s, delta2_s, sum1_s, prod1_s, delta1_s, sems = rest[4:12], *rest[12:]
+    users = ins[0].shape[0]
+    blocks = users // BLK
     weights = [pltpu.make_async_copy(ins[i], bufs[i], sems.at[i]) for i in (6, 7)]
     for copy in weights:
         copy.start()
@@ -78,12 +79,14 @@
         back_inter = dot_t(deltas, wi[0])
         dmsg1_ref[rows, :] = (back_self + back_inter * prev).astype(BF)
         user_grad_ref[rows, :] = (back_self + back_inter * msg).astype(BF)
-    even = lax.rem(lax.axis_index("rep"), 2) == 0
     for at, (sum_s, prod_s, delta_s) in enumerate(((sum2_s, prod2_s, delta2_s), (sum1_s, prod1_s, delta1_s))):
-        grad_self = tdot(sum_s[...], delta_s[...])
-        grad_inter = tdot(prod_s[...], delta_s[...])
-        keep_ref[at] = jnp.where(even, grad_self, grad_inter)
-        send_ref[at] = jnp.where(even, grad_inter, grad_self).astype(BF)
+        for half, left_s in enumerate((sum_s, prod_s)):
+            grad = tdot(left_s[...], delta_s[...])
+            first = 32 * half + 16 * at
+            for o in range(OWNERS):
+                part = grad[8 * o : 8 * o + 8, :]
+                part = jnp.concatenate([part[:, :HALF], part[:, HALF:]], axis=0)
+                a_ref[o, first : first + 16, :] = part.astype(BF)
 
 
 def rank_blocks(dest_ref, rank_s, seen_s):
@@ -127,29 +130,21 @@
     slots_s[...] = jnp.zeros_like(slots_s)
     tile_terms(user_ref, count_ref, dest_ref, adj_ref, dmsg_ref, rank_s, slots_s)
     for o in range(OWNERS):
-        b_ref[o, 0:32, :] = two_ref[0, o, 32:64, :]
-        b_ref[o, 32:96, :] = two_ref[1, o]
-        b_ref[o, 96:160, :] = slots_s[0, o]
-        b_ref[o, 160:192, :] = slots_s[1, o, 0:32, :]
-        b_ref[o, 192:200, :] = index_ref[o]
+        b_ref[o, 0:64, :] = two_ref[0, o]
+        b_ref[o, 64:128, :] = two_ref[1, o]
+        b_ref[o, 128:192, :] = slots_s[0, o]
+        b_ref[o, 192:224, :] = slots_s[1, o, 0:32, :]
+        b_ref[o, 224:232, :] = index_ref[o]
         rest_ref[o] = slots_s[1, o, 32:64, :]
 
 
-def pack_kernel(two_ref, keep_ref, got_ref, a_ref):
-    for o in range(OWNERS):
-        a_ref[o, 0:32, :] = two_ref[0, o, 0:32, :]
-        rows = slice(8 * o, 8 * o + 8)
-        for at in range(2):
-            total = keep_ref[at, rows, :] + got_ref[at, rows, :].astype(F32)
-            first = 32 + 16 * at
-            a_ref[o, first : first + 16, :] = jnp.concatenate([total[:, :HALF], total[:, HALF:]], axis=0).astype(BF)
-
-
-def chunk_kernel(a_ref, total_ref):
-    acc = a_ref[0, 32:64, :].astype(F32)
+def chunk_kernel(a_ref, keep_ref, send_ref):
+    acc = a_ref[0].astype(F32)
     for s in range(1, OWNERS):
-        acc = acc + a_ref[s, 32:64, :].astype(F32)
-    total_ref[...] = acc
+        acc = acc + a_ref[s].astype(F32)
+    even = lax.rem(lax.axis_index("rep"), 2) == 0
+    keep_ref[...] = jnp.where(even, acc[:32], acc[32:])
+    send_ref[...] = jnp.where(even, acc[32:], acc[:32])
 
 
 def last_kernel(own_ref, one_ref, two_ref, rest_ref, c_ref, slots_s):
@@ -229,30 +224,29 @@
     ranks = [pltpu.SMEM((OWNERS,), jnp.int32)] * 2
     small = dict(flops=1_000_000, bytes_accessed=2 << 20)
     tile = dict(flops=140_000_000, bytes_accessed=2 << 20)
-    dmsg2, dmsg1, user_grad, keep, send = call(
+    dmsg2, dmsg1, user_grad, a = call(
         user_kernel,
-        [user, user, user, both, (both[0], BF)],
+        [user, user, user, rows(64)],
         [HBM] * 8,
         [pltpu.VMEM((users, FEAT), BF)] * 6 + [pltpu.VMEM((2, FEAT, FEAT), BF)] * 2
         + [pltpu.VMEM((users, FEAT), BF)] * 6 + [pltpu.SemaphoreType.DMA((8 + 6 * (users // BLK),))],
         params=WIDE, flops=900_000_000, bytes_accessed=6 << 20,
     )(cotangent, pre_two, pre_one, message_two, message_one, users_zero, w_self, w_inter)
-    got = lax.ppermute(send, "rep", swap)
+    got_a = to_owners(a)
+
     two, index_rows = call(
         two_kernel, [((2, OWNERS, 64, HALF), BF), rows(8)], [SMEM] * 4 + [VMEM] * 2,
         ranks + [pltpu.SMEM((2 * OWNERS,), jnp.int32)], **tile,
     )(tile_user, counts, dest, item_block, adjacency, dmsg2)
-    (a,) = call(pack_kernel, [rows(64)], [VMEM] * 3, **small)(two, keep, got)
-    got_a = to_owners(a)
-
     b, rest = call(
-        one_kernel, [rows(200), rows(32)], [SMEM] * 3 + [VMEM] * 4,
+        one_kernel, [rows(232), rows(32)], [SMEM] * 3 + [VMEM] * 4,
         [pltpu.VMEM((2, OWNERS, 64, HALF), BF)] + ranks, **tile,
     )(tile_user, counts, dest, adjacency, dmsg1, two, index_rows)
     b, got_a = lax.optimization_barrier((b, got_a))
     got_b = to_owners(b)
 
-    (total,) = call(chunk_kernel, [chunk], [VMEM], **small)(got_a)
+    keep, send = call(chunk_kernel, [chunk] * 2, [VMEM], **small)(got_a)
+    total = keep + lax.ppermute(send, "rep", swap)
     total = total + from_z(total, lambda z: z ^ 1)
     total = total + from_z(total, lambda z: z ^ 2)
     far = [from_z(total, lambda z, k=k: (z + z_chips - NEAR * k) % z_chips) for k in (1, 2)]
@@ -260,7 +254,7 @@
     c, got_b = lax.optimization_barrier((c, got_b))
     got_c = to_owners(c)
 
-    index = got_b[:, 192:200:4, 0].astype(jnp.int32).reshape(2 * OWNERS)
+    index = got_b[:, 224:232:4, 0].astype(jnp.int32).reshape(2 * OWNERS)
 
     def collect(cuts, *arrays):
         return call(
@@ -268,10 +262,10 @@
             [pltpu.VMEM((TRASH + 1, 64, HALF), F32)], **small,
         )(index, *arrays)[0]
 
-    item_one = collect((((0, 0, 0, 32),), ((0, 0, 32, 32), (1, 32, 0, 64))), got_a, got_b)
+    item_one = collect((((0, 0, 0, 64), (1, 64, 0, 64)),), got_b)
     got_c, item_one = lax.optimization_barrier((got_c, item_one))
     other = lax.ppermute(got_c[:, 32:64], "rep", swap)
-    item_zero = collect((((0, 96, 0, 64), (1, 160, 0, 32)), ((1, 0, 32, 32),)), got_b, got_c)
+    item_zero = collect((((0, 128, 0, 64), (1, 192, 0, 32)), ((1, 0, 32, 32),)), got_b, got_c)
     self_grad, inter_grad = call(unpack_kernel, [both] * 2, [VMEM] * 2, **small)(got_c, other)
     return user_grad, item_one, item_zero, self_grad, inter_grad
 

time: 116 us -> 111 us (0.957); the launches traced: 116 us -> 109 us
  waiting for transfers between devices: 45.9 us -> 29.4 us
  starting transfers between devices: 51.9 us -> 63.9 us
    all_to_all x3, waiting for transfers between devices: 34.2 us -> 19 us  [to_owners(): return lax.all_to_all(x, 'owner', split_axis=0, concat_axis=0, tiled=True)]
    all_to_all x3, starting transfers between devices: 15.2 us -> 26.3 us  [to_owners(): return lax.all_to_all(x, 'owner', split_axis=0, concat_axis=0, tiled=True)]
    ppermute x1, starting transfers between devices: 12.4 us -> 6.19 us  [local(): total = keep + lax.ppermute(send, 'rep', swap)]
    ppermute x4, starting transfers between devices: 18 us -> 23.8 us  [from_z(): lax.ppermute(x, 'rep', [(2 * source(z) + c, 2 * z + c) for z in range(z_c...]
    ppermute x4, waiting for transfers between devices: 11.7 us -> 9.56 us  [from_z(): lax.ppermute(x, 'rep', [(2 * source(z) + c, 2 * z + c) for z in range(z_c...]
    ppermute x1, starting transfers between devices: 6.29 us -> 7.64 us  [local(): other = lax.ppermute(got_c[:, 32:64], 'rep', swap)]
    unnamed x18 -> x16, local copies, waits for them, and re-layouts: 3.25 us -> 2.29 us
    pallas_call x4 -> x3, Pallas kernels: 6.12 us -> 5.25 us  [the longest x1 4.05 us: local(): call(user_kernel, [user, user, user, rows(64)], [HBM] * 8, [pltpu.VMEM((u...]
where the time goes in v9:
time: 111 us; the launch traced here: 109 us
  starting transfers between devices  63.9 us (58%)
  waiting for transfers between devices  29.4 us (26%)
  Pallas kernels  11.9 us (11%)
  local copies, waits for them, and re-layouts  2.54 us (2%)
    all_to_all x3, starting transfers between devices, to_owners(): return lax.all_to_all(x, 'owner', split_axis=0, concat_axis=0, tiled=True)  26.3 us
    ppermute x4, starting transfers between devices, from_z(): lax.ppermute(x, 'rep', [(2 * source(z) + c, 2 * z + c) for z in range(z_c...  23.8 us
    all_to_all x3, waiting for transfers between devices, to_owners(): return lax.all_to_all(x, 'owner', split_axis=0, concat_axis=0, tiled=True)  19 us
    ppermute x4, waiting for transfers between devices, from_z(): lax.ppermute(x, 'rep', [(2 * source(z) + c, 2 * z + c) for z in range(z_c...  9.56 us
    ppermute x1, starting transfers between devices, local(): other = lax.ppermute(got_c[:, 32:64], 'rep', swap)  7.64 us
    ppermute x1, starting transfers between devices, local(): total = keep + lax.ppermute(send, 'rep', swap)  6.19 us
    pallas_call x1, Pallas kernels, local(): call(user_kernel, [user, user, user, rows(64)], [HBM] * 8, [pltpu.VMEM((u...  4.05 us
    pallas_call x2, Pallas kernels, collect(): call(functools.partial(collect_kernel, cuts), [((OWNERS * RB, FEAT), BF)]...  3.68 us
  transfers between devices with their start and end apart: 9, of which 6 were waited for; matrix products, arithmetic and copies ran while one was open for 1% of the time, Pallas kernels for 6%

profile of v9, /device:TPU:1, one launch (start us, length us, event | category | flops | bytes accessed | tf_op | source)
XLA Modules:
  0.0 109.2 jit_solution(13548005316004976839)
XLA Ops:
  0.6 0.0 copy-start.5
  0.6 0.0 copy-start.4
  0.7 0.0 copy-start
  0.7 0.0 copy-start.7
  0.7 0.0 copy-start.6
  0.7 4.1 %shard_map.164 = (bf16[768,256]{1,0:T(8,128)(2,1)}, bf16[768,256]{1,0:T(8,128)(2,1)}, bf16[768,256]{1,0:T(8,128)(2,1)}, bf16[32,64,128]{2,1,0:T(8,128)(2,1)}) custom-call(bf16[768,256]{1,0:T(8,128)(2,1)} %refs_0_.1, bf16[768,256]{1,0:T(8,128)(2,1)} %refs_1_.1, bf16[768,256]{1,0:T(8,128)(2,1)} %refs_2_.1, bf16[768,256]{1,0:T(8,128)(2,1)} %refs_3_.1, ...), custom_call_target="tpu_custom_call" | custom-call | flops 900000000 | bytes 6291456 | tf_op jit(solution)/shard_map/pallas_call | solution.py:227
  4.7 0.0 copy-start.2
  4.8 10.6 %all-to-all-start = ((bf16[32,64,128]{2,1,0:T(8,128)(2,1)}), bf16[32,64,128]{2,1,0:T(8,128)(2,1)S(1)}, u32[]{:S(2)}, u32[]{:S(2)}) async-start(bf16[32,64,128]{2,1,0:T(8,128)(2,1)} %get-tuple-element.29), calls=%async_computation | async-start | bytes 1048576 | tf_op jit(solution)/shard_map/all_to_all | solution.py:216
  15.4 0.0 copy-done.5
  15.4 0.0 copy-done.4
  15.4 0.0 copy-done
  15.4 0.0 copy-done.7
  15.4 0.0 copy-done.6
  15.5 0.0 copy-start.3
  15.5 1.0 copy-done.3
  16.5 1.1 shard_map.165
  17.5 0.0 copy-done.2
  17.5 1.1 %shard_map.166 = (bf16[32,232,128]{2,1,0:T(8,128)(2,1)S(1)}, bf16[32,32,128]{2,1,0:T(8,128)(2,1)S(1)}) custom-call(s32[4]{0:T(128)S(1)} %copy-done.4, s32[4]{0:T(128)S(1)} %copy-done.5, s32[32]{0:T(128)S(1)} %bitcast.2, bf16[4,256,256]{2,1,0:T(8,128)(2,1)S(1)} %copy-done, bf16[768,256]{1,0:T(8,128)(2,1)S(1)} %copy-done.2, ...), custom_call_target="tpu_custom_call" | custom-call | flops 140000000 | bytes 2097152 | tf_op jit(solution)/shard_map/pallas_call | solution.py:241
  18.7 0.0 copy-start.1
  18.7 1.3 %copy-done.1 = bf16[32,232,128]{2,1,0:T(8,128)(2,1)} copy-done((bf16[32,232,128]{2,1,0:T(8,128)(2,1)}, bf16[32,232,128]{2,1,0:T(8,128)(2,1)S(1)}, u32[]{:S(2)}) %copy-start.1) | copy-done | bytes 1900568
  19.9 8.4 %all-to-all-done.a_ref = bf16[32,64,128]{2,1,0:T(8,128)(2,1)S(1)} async-done(((bf16[32,64,128]{2,1,0:T(8,128)(2,1)}), bf16[32,64,128]{2,1,0:T(8,128)(2,1)S(1)}, u32[]{:S(2)}, u32[]{:S(2)}) %all-to-all-start) | async-done | bytes 524320 | tf_op jit(solution)/shard_map/all_to_all | solution.py:216
  28.3 6.2 %all-to-all-start.1 = ((bf16[32,232,128]{2,1,0:T(8,128)(2,1)}), bf16[32,232,128]{2,1,0:T(8,128)(2,1)S(1)}, u32[]{:S(2)}, u32[]{:S(2)}) async-start(bf16[32,232,128]{2,1,0:T(8,128)(2,1)} %copy-done.1), calls=%async_computation.1 | async-start | bytes 3801088 | tf_op jit(solution)/shard_map/all_to_all | solution.py:216
  34.5 0.1 shard_map.167
  34.6 6.2 %collective-permute-start = (f32[32,128]{1,0:T(8,128)S(1)}, f32[32,128]{1,0:T(8,128)S(1)}, u32[]{:S(2)}, u32[]{:S(2)}) collective-permute-start(f32[32,128]{1,0:T(8,128)S(1)} %get-tuple-element.32), channel_id=1, source_target_pairs={{0,1},{1,0},{2,3},{3,2},{4,5},{5,4},{6,7},{7,6},{8,9},{9,8},{10,11... | collective-permute-start | bytes 49160 | tf_op jit(solution)/shard_map/ppermute | solution.py:249
  40.8 0.8 collective-permute-done
  41.6 4.0 %collective-permute-start.1 = (f32[32,128]{1,0:T(8,128)S(1)}, f32[32,128]{1,0:T(8,128)S(1)}, u32[]{:S(2)}, u32[]{:S(2)}) collective-permute-start(f32[32,128]{1,0:T(8,128)S(1)} %add.9), channel_id=1, source_target_pairs={{2,0},{3,1},{0,2},{1,3},{6,4},{7,5},{4,6},{5,7},{10,8},{11,9},{8,1... | collective-permute-start | bytes 49160 | tf_op jit(solution)/shard_map/ppermute | solution.py:213
  45.6 1.4 %collective-permute-done.1 = f32[32,128]{1,0:T(8,128)S(1)} collective-permute-done((f32[32,128]{1,0:T(8,128)S(1)}, f32[32,128]{1,0:T(8,128)S(1)}, u32[]{:S(2)}, u32[]{:S(2)}) %collective-permute-start.1) | collective-permute-done | bytes 16416 | tf_op jit(solution)/shard_map/ppermute | solution.py:213
  47.0 5.8 %collective-permute-start.2 = (f32[32,128]{1,0:T(8,128)S(1)}, f32[32,128]{1,0:T(8,128)S(1)}, u32[]{:S(2)}, u32[]{:S(2)}) collective-permute-start(f32[32,128]{1,0:T(8,128)S(1)} %add.10), channel_id=1, source_target_pairs={{4,0},{5,1},{6,2},{7,3},{0,4},{1,5},{2,6},{3,7},{12,8},{13,9},{14,... | collective-permute-start | bytes 49160 | tf_op jit(solution)/shard_map/ppermute | solution.py:213
  52.8 1.4 %collective-permute-done.2 = f32[32,128]{1,0:T(8,128)S(1)} collective-permute-done((f32[32,128]{1,0:T(8,128)S(1)}, f32[32,128]{1,0:T(8,128)S(1)}, u32[]{:S(2)}, u32[]{:S(2)}) %collective-permute-start.2) | collective-permute-done | bytes 16416 | tf_op jit(solution)/shard_map/ppermute | solution.py:213
  54.2 12.1 %collective-permute-start.4 = (f32[32,128]{1,0:T(8,128)S(1)}, f32[32,128]{1,0:T(8,128)S(1)}, u32[]{:S(2)}, u32[]{:S(2)}) collective-permute-start(f32[32,128]{1,0:T(8,128)S(1)} %add.11.own_ref), channel_id=1, source_target_pairs={{8,0},{9,1},{10,2},{11,3},{12,4},{13,5},{14,6},{15,7},{16,8},{17,9... | collective-permute-start | bytes 49160 | tf_op jit(solution)/shard_map/ppermute | solution.py:213
  66.3 1.9 %collective-permute-start.3 = (f32[32,128]{1,0:T(8,128)S(1)}, f32[32,128]{1,0:T(8,128)S(1)}, u32[]{:S(2)}, u32[]{:S(2)}) collective-permute-start(f32[32,128]{1,0:T(8,128)S(1)} %add.11.own_ref), channel_id=1, source_target_pairs={{16,0},{17,1},{18,2},{19,3},{20,4},{21,5},{22,6},{23,7},{0,8},{1,9... | collective-permute-start | bytes 49160 | tf_op jit(solution)/shard_map/ppermute | solution.py:213
  68.2 0.0 collective-permute-done.4.two_ref
  68.2 6.7 %collective-permute-done.3.one_ref = f32[32,128]{1,0:T(8,128)S(1)} collective-permute-done((f32[32,128]{1,0:T(8,128)S(1)}, f32[32,128]{1,0:T(8,128)S(1)}, u32[]{:S(2)}, u32[]{:S(2)}) %collective-permute-start.3) | collective-permute-done | bytes 16416 | tf_op jit(solution)/shard_map/ppermute | solution.py:213
  75.0 0.9 shard_map.168
  75.9 0.0 all-to-all-done.1.refs_0_
  75.9 9.5 %all-to-all-start.2 = ((bf16[32,64,128]{2,1,0:T(8,128)(2,1)}), bf16[32,64,128]{2,1,0:T(8,128)(2,1)S(1)}, u32[]{:S(2)}, u32[]{:S(2)}) async-start(bf16[32,64,128]{2,1,0:T(8,128)(2,1)} %shard_map.168), calls=%async_computation.2 | async-start | bytes 1048576 | tf_op jit(solution)/shard_map/all_to_all | solution.py:216
  85.4 0.1 slice.6
  85.5 0.6 convert_reduce_fusion
  86.1 0.1 reshape.18.index_ref
  86.2 1.8 %shard_map.169 = bf16[1024,256]{1,0:T(8,128)(2,1)} custom-call(s32[64]{0:T(128)S(1)} %reshape.18.index_ref, bf16[32,232,128]{2,1,0:T(8,128)(2,1)S(1)} %all-to-all-done.1.refs_0_), custom_call_target="tpu_custom_call" | custom-call | flops 1000000 | bytes 2097152 | tf_op jit(solution)/shard_map/pallas_call | solution.py:260
  88.0 10.6 %all-to-all-done.2.refs_1_.mine_ref = bf16[32,64,128]{2,1,0:T(8,128)(2,1)S(1)} async-done(((bf16[32,64,128]{2,1,0:T(8,128)(2,1)}), bf16[32,64,128]{2,1,0:T(8,128)(2,1)S(1)}, u32[]{:S(2)}, u32[]{:S(2)}) %all-to-all-start.2) | async-done | bytes 524320 | tf_op jit(solution)/shard_map/all_to_all | solution.py:216
  98.6 7.6 %collective-permute-start.5 = (bf16[32,32,128]{2,1,0:T(8,128)(2,1)S(1)}, bf16[32,32,128]{2,1,0:T(8,128)(2,1)S(1)}, u32[]{:S(2)}, u32[]{:S(2)}) collective-permute-start(bf16[32,32,128]{2,1,0:T(8,128)(2,1)S(1)} %slice.7), channel_id=1, source_target_pairs={{0,1},{1,0},{2,3},{3,2},{4,5},{5,4},{6,7},{7,6},{8,9},{9,8},{10,11... | collective-permute-start | bytes 786440 | tf_op jit(solution)/shard_map/ppermute | solution.py:267
  106.3 1.9 %shard_map.170 = bf16[1024,256]{1,0:T(8,128)(2,1)} custom-call(s32[64]{0:T(128)S(1)} %reshape.18.index_ref, bf16[32,232,128]{2,1,0:T(8,128)(2,1)S(1)} %all-to-all-done.1.refs_0_, bf16[32,64,128]{2,1,0:T(8,128)(2,1)S(1)} %all-to-all-done.2.refs_1_.mine_ref), custom_call_target="tpu_custom_call" | custom-call | flops 1000000 | bytes 2097152 | tf_op jit(solution)/shard_map/pallas_call | solution.py:260
  108.2 0.0 collective-permute-done.5.other_ref
  108.2 1.1 shard_map.171
  (4 shorter events, 0.0 us)
Async XLA Ops:
  0.6 14.8 %copy-start.5 = (s32[4]{0:T(128)S(1)}, s32[4]{0:T(128)}, u32[]{:S(2)}) copy-start(s32[4]{0:T(128)} %count_ref.3) | copy-start | bytes 52
  0.6 14.8 %copy-start.4 = (s32[4]{0:T(128)S(1)}, s32[4]{0:T(128)}, u32[]{:S(2)}) copy-start(s32[4]{0:T(128)} %user_ref.3) | copy-start | bytes 52
  0.7 14.8 %copy-start = (bf16[4,256,256]{2,1,0:T(8,128)(2,1)S(1)}, bf16[4,256,256]{2,1,0:T(8,128)(2,1)}, u32[]{:S(2)}) copy-start(bf16[4,256,256]{2,1,0:T(8,128)(2,1)} %adj_ref.3) | copy-start | bytes 1572868
  0.7 14.8 %copy-start.7 = (s32[32]{0:T(128)S(1)}, s32[32]{0:T(128)}, u32[]{:S(2)}) copy-start(s32[32]{0:T(128)} %item_ref.1) | copy-start | bytes 388
  0.7 14.8 %copy-start.6 = (s32[32,1]{0,1:T(1,128)S(1)}, s32[32,1]{0,1:T(1,128)}, u32[]{:S(2)}) copy-start(s32[32,1]{0,1:T(1,128)} %param.24) | copy-start | bytes 388
  4.7 12.8 %copy-start.2 = (bf16[768,256]{1,0:T(8,128)(2,1)S(1)}, bf16[768,256]{1,0:T(8,128)(2,1)}, u32[]{:S(2)}) copy-start(bf16[768,256]{1,0:T(8,128)(2,1)} %get-tuple-element.24.dmsg_ref) | copy-start | bytes 1179652
  4.8 23.6 %all-to-all-start = ((bf16[32,64,128]{2,1,0:T(8,128)(2,1)}), bf16[32,64,128]{2,1,0:T(8,128)(2,1)S(1)}, u32[]{:S(2)}, u32[]{:S(2)}) async-start(bf16[32,64,128]{2,1,0:T(8,128)(2,1)} %get-tuple-element.29), calls=%async_computation | async-start | bytes 1048576 | tf_op jit(solution)/shard_map/all_to_all | solution.py:216
  15.5 1.0 copy-start.3
  18.7 1.3 %copy-start.1 = (bf16[32,232,128]{2,1,0:T(8,128)(2,1)}, bf16[32,232,128]{2,1,0:T(8,128)(2,1)S(1)}, u32[]{:S(2)}) copy-start(bf16[32,232,128]{2,1,0:T(8,128)(2,1)S(1)} %get-tuple-element.34) | copy-start | bytes 5701636
  28.3 47.5 %all-to-all-start.1 = ((bf16[32,232,128]{2,1,0:T(8,128)(2,1)}), bf16[32,232,128]{2,1,0:T(8,128)(2,1)S(1)}, u32[]{:S(2)}, u32[]{:S(2)}) async-start(bf16[32,232,128]{2,1,0:T(8,128)(2,1)} %copy-done.1), calls=%async_computation.1 | async-start | bytes 3801088 | tf_op jit(solution)/shard_map/all_to_all | solution.py:216
  34.6 7.0 %collective-permute-start = (f32[32,128]{1,0:T(8,128)S(1)}, f32[32,128]{1,0:T(8,128)S(1)}, u32[]{:S(2)}, u32[]{:S(2)}) collective-permute-start(f32[32,128]{1,0:T(8,128)S(1)} %get-tuple-element.32), channel_id=1, source_target_pairs={{0,1},{1,0},{2,3},{3,2},{4,5},{5,4},{6,7},{7,6},{8,9},{9,8},{10,11... | collective-permute-start | bytes 49160 | tf_op jit(solution)/shard_map/ppermute | solution.py:249
  41.6 5.4 %collective-permute-start.1 = (f32[32,128]{1,0:T(8,128)S(1)}, f32[32,128]{1,0:T(8,128)S(1)}, u32[]{:S(2)}, u32[]{:S(2)}) collective-permute-start(f32[32,128]{1,0:T(8,128)S(1)} %add.9), channel_id=1, source_target_pairs={{2,0},{3,1},{0,2},{1,3},{6,4},{7,5},{4,6},{5,7},{10,8},{11,9},{8,1... | collective-permute-start | bytes 49160 | tf_op jit(solution)/shard_map/ppermute | solution.py:213
  47.0 7.2 %collective-permute-start.2 = (f32[32,128]{1,0:T(8,128)S(1)}, f32[32,128]{1,0:T(8,128)S(1)}, u32[]{:S(2)}, u32[]{:S(2)}) collective-permute-start(f32[32,128]{1,0:T(8,128)S(1)} %add.10), channel_id=1, source_target_pairs={{4,0},{5,1},{6,2},{7,3},{0,4},{1,5},{2,6},{3,7},{12,8},{13,9},{14,... | collective-permute-start | bytes 49160 | tf_op jit(solution)/shard_map/ppermute | solution.py:213
  54.2 14.0 %collective-permute-start.4 = (f32[32,128]{1,0:T(8,128)S(1)}, f32[32,128]{1,0:T(8,128)S(1)}, u32[]{:S(2)}, u32[]{:S(2)}) collective-permute-start(f32[32,128]{1,0:T(8,128)S(1)} %add.11.own_ref), channel_id=1, source_target_pairs={{8,0},{9,1},{10,2},{11,3},{12,4},{13,5},{14,6},{15,7},{16,8},{17,9... | collective-permute-start | bytes 49160 | tf_op jit(solution)/shard_map/ppermute | solution.py:213
  66.3 8.7 %collective-permute-start.3 = (f32[32,128]{1,0:T(8,128)S(1)}, f32[32,128]{1,0:T(8,128)S(1)}, u32[]{:S(2)}, u32[]{:S(2)}) collective-permute-start(f32[32,128]{1,0:T(8,128)S(1)} %add.11.own_ref), channel_id=1, source_target_pairs={{16,0},{17,1},{18,2},{19,3},{20,4},{21,5},{22,6},{23,7},{0,8},{1,9... | collective-permute-start | bytes 49160 | tf_op jit(solution)/shard_map/ppermute | solution.py:213
  75.9 22.8 %all-to-all-start.2 = ((bf16[32,64,128]{2,1,0:T(8,128)(2,1)}), bf16[32,64,128]{2,1,0:T(8,128)(2,1)S(1)}, u32[]{:S(2)}, u32[]{:S(2)}) async-start(bf16[32,64,128]{2,1,0:T(8,128)(2,1)} %shard_map.168), calls=%async_computation.2 | async-start | bytes 1048576 | tf_op jit(solution)/shard_map/all_to_all | solution.py:216
  98.6 9.5 %collective-permute-start.5 = (bf16[32,32,128]{2,1,0:T(8,128)(2,1)S(1)}, bf16[32,32,128]{2,1,0:T(8,128)(2,1)S(1)}, u32[]{:S(2)}, u32[]{:S(2)}) collective-permute-start(bf16[32,32,128]{2,1,0:T(8,128)(2,1)S(1)} %slice.7), channel_id=1, source_target_pairs={{0,1},{1,0},{2,3},{3,2},{4,5},{5,4},{6,7},{7,6},{8,9},{9,8},{10,11... | collective-permute-start | bytes 786440 | tf_op jit(solution)/shard_map/ppermute | solution.py:267

commit v10 on v9

--- a/solution.py
+++ b/solution.py
@@ -36,8 +36,8 @@
 
 def user_kernel(*refs):
     ins, rest = refs[:8], refs[8:]
-    dmsg2_ref, dmsg1_ref, user_grad_ref, a_ref = rest[:4]
-    bufs, sum2_s, prod2_s, delta2_s, sum1_s, prod1_s, delta1_s, sems = rest[4:12], *rest[12:]
+    dmsg2_ref, delta1_s, a_ref = rest[:3]
+    bufs, sum2_s, prod2_s, delta2_s, sum1_s, prod1_s, sems = rest[3:11], *rest[11:]
     users = ins[0].shape[0]
     blocks = users // BLK
     weights = [pltpu.make_async_copy(ins[i], bufs[i], sems.at[i]) for i in (6, 7)]
@@ -75,10 +75,6 @@
         delta1_s[rows, :] = deltas
         sum1_s[rows, :] = (msg + prev).astype(BF)
         prod1_s[rows, :] = (msg * prev).astype(BF)
-        back_self = dot_t(deltas, ws[0])
-        back_inter = dot_t(deltas, wi[0])
-        dmsg1_ref[rows, :] = (back_self + back_inter * prev).astype(BF)
-        user_grad_ref[rows, :] = (back_self + back_inter * msg).astype(BF)
     for at, (sum_s, prod_s, delta_s) in enumerate(((sum2_s, prod2_s, delta2_s), (sum1_s, prod1_s, delta1_s))):
         for half, left_s in enumerate((sum_s, prod_s)):
             grad = tdot(left_s[...], delta_s[...])
@@ -124,9 +120,15 @@
     tile_terms(user_ref, count_ref, dest_ref, adj_ref, dmsg_ref, rank_s, slots_ref)
 
 
-def one_kernel(user_ref, count_ref, dest_ref, adj_ref, dmsg_ref, two_ref, index_ref, b_ref, rest_ref, slots_s, rank_s,
-               seen_s):
+def one_kernel(user_ref, count_ref, dest_ref, adj_ref, delta_ref, msg_ref, zero_ref, ws_ref, wi_ref, two_ref, index_ref,
+               b_ref, rest_ref, user_grad_ref, slots_s, dmsg_ref, rank_s, seen_s):
     rank_blocks(dest_ref, rank_s, seen_s)
+    for b in range(delta_ref.shape[0] // BLK):
+        rows = pl.ds(b * BLK, BLK)
+        back_self = dot_t(delta_ref[rows, :], ws_ref[0])
+        back_inter = dot_t(delta_ref[rows, :], wi_ref[0])
+        dmsg_ref[rows, :] = (back_self + back_inter * zero_ref[rows, :].astype(F32)).astype(BF)
+        user_grad_ref[rows, :] = (back_self + back_inter * msg_ref[rows, :].astype(F32)).astype(BF)
     slots_s[...] = jnp.zeros_like(slots_s)
     tile_terms(user_ref, count_ref, dest_ref, adj_ref, dmsg_ref, rank_s, slots_s)
     for o in range(OWNERS):
@@ -224,12 +226,12 @@
     ranks = [pltpu.SMEM((OWNERS,), jnp.int32)] * 2
     small = dict(flops=1_000_000, bytes_accessed=2 << 20)
     tile = dict(flops=140_000_000, bytes_accessed=2 << 20)
-    dmsg2, dmsg1, user_grad, a = call(
+    dmsg2, delta1, a = call(
         user_kernel,
-        [user, user, user, rows(64)],
+        [user, user, rows(64)],
         [HBM] * 8,
         [pltpu.VMEM((users, FEAT), BF)] * 6 + [pltpu.VMEM((2, FEAT, FEAT), BF)] * 2
-        + [pltpu.VMEM((users, FEAT), BF)] * 6 + [pltpu.SemaphoreType.DMA((8 + 6 * (users // BLK),))],
+        + [pltpu.VMEM((users, FEAT), BF)] * 5 + [pltpu.SemaphoreType.DMA((8 + 6 * (users // BLK),))],
         params=WIDE, flops=900_000_000, bytes_accessed=6 << 20,
     )(cotangent, pre_two, pre_one, message_two, message_one, users_zero, w_self, w_inter)
     got_a = to_owners(a)
@@ -238,10 +240,10 @@
         two_kernel, [((2, OWNERS, 64, HALF), BF), rows(8)], [SMEM] * 4 + [VMEM] * 2,
         ranks + [pltpu.SMEM((2 * OWNERS,), jnp.int32)], **tile,
     )(tile_user, counts, dest, item_block, adjacency, dmsg2)
-    b, rest = call(
-        one_kernel, [rows(232), rows(32)], [SMEM] * 3 + [VMEM] * 4,
-        [pltpu.VMEM((2, OWNERS, 64, HALF), BF)] + ranks, **tile,
-    )(tile_user, counts, dest, adjacency, dmsg1, two, index_rows)
+    b, rest, user_grad = call(
+        one_kernel, [rows(232), rows(32), user], [SMEM] * 3 + [VMEM] * 8,
+        [pltpu.VMEM((2, OWNERS, 64, HALF), BF), pltpu.VMEM((users, FEAT), BF)] + ranks, **tile,
+    )(tile_user, counts, dest, adjacency, delta1, message_one, users_zero, w_self, w_inter, two, index_rows)
     b, got_a = lax.optimization_barrier((b, got_a))
     got_b = to_owners(b)
 

time: 111 us -> 110 us (level)
  waiting for transfers between devices: 29.4 us -> 25.5 us
  local copies, waits for them, and re-layouts: 2.54 us -> 5.45 us
    all_to_all x3, waiting for transfers between devices: 19 us -> 15.1 us  [to_owners(): return lax.all_to_all(x, 'owner', split_axis=0, concat_axis=0, tiled=True)]
    unnamed x16 -> x24, local copies, waits for them, and re-layouts: 2.29 us -> 5.19 us
  transfers between devices with their start and end apart: 9 -> 9, of which waited for: 6 -> 6; matrix products, arithmetic and copies ran while one was open for 1% -> 1% of each run, Pallas kernels for 6% -> 7%
where the time goes in v10:
time: 110 us; the launch traced here: 109 us
  starting transfers between devices  63.8 us (58%)
  waiting for transfers between devices  25.5 us (23%)
  Pallas kernels  12.6 us (11%)
  local copies, waits for them, and re-layouts  5.45 us (5%)
    all_to_all x3, starting transfers between devices, to_owners(): return lax.all_to_all(x, 'owner', split_axis=0, concat_axis=0, tiled=True)  26.3 us
    ppermute x4, starting transfers between devices, from_z(): lax.ppermute(x, 'rep', [(2 * source(z) + c, 2 * z + c) for z in range(z_c...  23.8 us
    all_to_all x3, waiting for transfers between devices, to_owners(): return lax.all_to_all(x, 'owner', split_axis=0, concat_axis=0, tiled=True)  15.1 us
    ppermute x4, waiting for transfers between devices, from_z(): lax.ppermute(x, 'rep', [(2 * source(z) + c, 2 * z + c) for z in range(z_c...  9.56 us
    ppermute x1, starting transfers between devices, local(): other = lax.ppermute(got_c[:, 32:64], 'rep', swap)  7.61 us
    ppermute x1, starting transfers between devices, local(): total = keep + lax.ppermute(send, 'rep', swap)  6.04 us
    unnamed x24, local copies, waits for them, and re-layouts  5.19 us
    pallas_call x1, Pallas kernels, local(): call(user_kernel, [user, user, rows(64)], [HBM] * 8, [pltpu.VMEM((users,...  3.75 us
  transfers between devices with their start and end apart: 9, of which 6 were waited for; matrix products, arithmetic and copies ran while one was open for 1% of the time, Pallas kernels for 7%

profile of v10, /device:TPU:1, one launch (start us, length us, event | category | flops | bytes accessed | tf_op | source)
XLA Modules:
  0.0 108.8 jit_solution(8722435115966260712)
XLA Ops:
  0.6 0.0 copy-start.4
  0.6 0.0 copy-start.3
  0.7 0.0 copy-start.9
  0.7 0.0 copy-start.8
  0.7 0.0 copy-start
  0.7 0.0 copy-start.11
  0.7 0.0 copy-start.10
  0.7 3.7 %shard_map.164 = (bf16[768,256]{1,0:T(8,128)(2,1)}, bf16[768,256]{1,0:T(8,128)(2,1)}, bf16[32,64,128]{2,1,0:T(8,128)(2,1)}) custom-call(bf16[768,256]{1,0:T(8,128)(2,1)} %refs_0_.1, bf16[768,256]{1,0:T(8,128)(2,1)} %refs_1_.1, bf16[768,256]{1,0:T(8,128)(2,1)} %refs_2_.1, bf16[768,256]{1,0:T(8,128)(2,1)} %refs_3_.1, bf16[768,256]{1,0:T(8,128)(2,1)} %msg_ref.1, ...), custom_call_target="tpu_custom_call" | custom-call | flops 900000000 | bytes 6291456 | tf_op jit(solution)/shard_map/pallas_call | solution.py:229
  4.5 10.5 %all-to-all-start = ((bf16[32,64,128]{2,1,0:T(8,128)(2,1)}), bf16[32,64,128]{2,1,0:T(8,128)(2,1)S(1)}, u32[]{:S(2)}, u32[]{:S(2)}) async-start(bf16[32,64,128]{2,1,0:T(8,128)(2,1)} %get-tuple-element.29), calls=%async_computation | async-start | bytes 1048576 | tf_op jit(solution)/shard_map/all_to_all | solution.py:218
  15.0 0.0 copy-done.9
  15.0 0.0 copy-done.8
  15.0 0.0 copy-done
  15.0 0.0 copy-done.11
  15.0 0.0 copy-done.10
  15.0 0.0 copy-start.2
  15.1 1.0 copy-done.2
  16.0 1.1 shard_map.165
  17.1 0.0 copy-done.4
  17.1 0.0 copy-done.3
  17.1 0.0 copy-start.5
  17.2 1.0 copy-done.5
  18.1 0.0 copy-start.6
  18.1 0.9 copy-done.6
  19.1 0.0 copy-start.7
  19.1 0.9 copy-done.7
  20.0 2.1 %shard_map.166 = (bf16[32,232,128]{2,1,0:T(8,128)(2,1)S(1)}, bf16[32,32,128]{2,1,0:T(8,128)(2,1)S(1)}, bf16[768,256]{1,0:T(8,128)(2,1)}) custom-call(s32[4]{0:T(128)S(1)} %copy-done.8, s32[4]{0:T(128)S(1)} %copy-done.9, s32[32]{0:T(128)S(1)} %bitcast.2, bf16[4,256,256]{2,1,0:T(8,128)(2,1)S(1)} %copy-done, bf16[768,256]{1,0:T(8,128)(2,1)S(1)} %copy-done.5, ...), custom_call_target="tpu_custom_call" | custom-call | flops 140000000 | bytes 2097152 | tf_op jit(solution)/shard_map/pallas_call | solution.py:243
  22.2 0.0 copy-start.1
  22.2 1.3 %copy-done.1 = bf16[32,232,128]{2,1,0:T(8,128)(2,1)} copy-done((bf16[32,232,128]{2,1,0:T(8,128)(2,1)}, bf16[32,232,128]{2,1,0:T(8,128)(2,1)S(1)}, u32[]{:S(2)}) %copy-start.1) | copy-done | bytes 1900568
  23.4 4.4 %all-to-all-done.a_ref = bf16[32,64,128]{2,1,0:T(8,128)(2,1)S(1)} async-done(((bf16[32,64,128]{2,1,0:T(8,128)(2,1)}), bf16[32,64,128]{2,1,0:T(8,128)(2,1)S(1)}, u32[]{:S(2)}, u32[]{:S(2)}) %all-to-all-start) | async-done | bytes 524320 | tf_op jit(solution)/shard_map/all_to_all | solution.py:218
  27.9 6.3 %all-to-all-start.1 = ((bf16[32,232,128]{2,1,0:T(8,128)(2,1)}), bf16[32,232,128]{2,1,0:T(8,128)(2,1)S(1)}, u32[]{:S(2)}, u32[]{:S(2)}) async-start(bf16[32,232,128]{2,1,0:T(8,128)(2,1)} %copy-done.1), calls=%async_computation.1 | async-start | bytes 3801088 | tf_op jit(solution)/shard_map/all_to_all | solution.py:218
  34.2 0.1 shard_map.167
  34.3 6.0 %collective-permute-start = (f32[32,128]{1,0:T(8,128)S(1)}, f32[32,128]{1,0:T(8,128)S(1)}, u32[]{:S(2)}, u32[]{:S(2)}) collective-permute-start(f32[32,128]{1,0:T(8,128)S(1)} %get-tuple-element.32), channel_id=1, source_target_pairs={{0,1},{1,0},{2,3},{3,2},{4,5},{5,4},{6,7},{7,6},{8,9},{9,8},{10,11... | collective-permute-start | bytes 49160 | tf_op jit(solution)/shard_map/ppermute | solution.py:251
  40.4 0.8 collective-permute-done
  41.2 4.0 %collective-permute-start.1 = (f32[32,128]{1,0:T(8,128)S(1)}, f32[32,128]{1,0:T(8,128)S(1)}, u32[]{:S(2)}, u32[]{:S(2)}) collective-permute-start(f32[32,128]{1,0:T(8,128)S(1)} %add.9), channel_id=1, source_target_pairs={{2,0},{3,1},{0,2},{1,3},{6,4},{7,5},{4,6},{5,7},{10,8},{11,9},{8,1... | collective-permute-start | bytes 49160 | tf_op jit(solution)/shard_map/ppermute | solution.py:215
  45.2 1.4 %collective-permute-done.1 = f32[32,128]{1,0:T(8,128)S(1)} collective-permute-done((f32[32,128]{1,0:T(8,128)S(1)}, f32[32,128]{1,0:T(8,128)S(1)}, u32[]{:S(2)}, u32[]{:S(2)}) %collective-permute-start.1) | collective-permute-done | bytes 16416 | tf_op jit(solution)/shard_map/ppermute | solution.py:215
  46.6 5.8 %collective-permute-start.2 = (f32[32,128]{1,0:T(8,128)S(1)}, f32[32,128]{1,0:T(8,128)S(1)}, u32[]{:S(2)}, u32[]{:S(2)}) collective-permute-start(f32[32,128]{1,0:T(8,128)S(1)} %add.10), channel_id=1, source_target_pairs={{4,0},{5,1},{6,2},{7,3},{0,4},{1,5},{2,6},{3,7},{12,8},{13,9},{14,... | collective-permute-start | bytes 49160 | tf_op jit(solution)/shard_map/ppermute | solution.py:215
  52.4 1.4 %collective-permute-done.2 = f32[32,128]{1,0:T(8,128)S(1)} collective-permute-done((f32[32,128]{1,0:T(8,128)S(1)}, f32[32,128]{1,0:T(8,128)S(1)}, u32[]{:S(2)}, u32[]{:S(2)}) %collective-permute-start.2) | collective-permute-done | bytes 16416 | tf_op jit(solution)/shard_map/ppermute | solution.py:215
  53.8 12.1 %collective-permute-start.4 = (f32[32,128]{1,0:T(8,128)S(1)}, f32[32,128]{1,0:T(8,128)S(1)}, u32[]{:S(2)}, u32[]{:S(2)}) collective-permute-start(f32[32,128]{1,0:T(8,128)S(1)} %add.11.own_ref), channel_id=1, source_target_pairs={{8,0},{9,1},{10,2},{11,3},{12,4},{13,5},{14,6},{15,7},{16,8},{17,9... | collective-permute-start | bytes 49160 | tf_op jit(solution)/shard_map/ppermute | solution.py:215
  65.9 1.9 %collective-permute-start.3 = (f32[32,128]{1,0:T(8,128)S(1)}, f32[32,128]{1,0:T(8,128)S(1)}, u32[]{:S(2)}, u32[]{:S(2)}) collective-permute-start(f32[32,128]{1,0:T(8,128)S(1)} %add.11.own_ref), channel_id=1, source_target_pairs={{16,0},{17,1},{18,2},{19,3},{20,4},{21,5},{22,6},{23,7},{0,8},{1,9... | collective-permute-start | bytes 49160 | tf_op jit(solution)/shard_map/ppermute | solution.py:215
  67.8 0.0 collective-permute-done.4.two_ref
  67.8 6.7 %collective-permute-done.3.one_ref = f32[32,128]{1,0:T(8,128)S(1)} collective-permute-done((f32[32,128]{1,0:T(8,128)S(1)}, f32[32,128]{1,0:T(8,128)S(1)}, u32[]{:S(2)}, u32[]{:S(2)}) %collective-permute-start.3) | collective-permute-done | bytes 16416 | tf_op jit(solution)/shard_map/ppermute | solution.py:215
  74.6 0.9 shard_map.168
  75.4 0.0 all-to-all-done.1.refs_0_
  75.4 9.5 %all-to-all-start.2 = ((bf16[32,64,128]{2,1,0:T(8,128)(2,1)}), bf16[32,64,128]{2,1,0:T(8,128)(2,1)S(1)}, u32[]{:S(2)}, u32[]{:S(2)}) async-start(bf16[32,64,128]{2,1,0:T(8,128)(2,1)} %shard_map.168), calls=%async_computation.2 | async-start | bytes 1048576 | tf_op jit(solution)/shard_map/all_to_all | solution.py:218
  84.9 0.1 slice.6
  85.1 0.6 convert_reduce_fusion
  85.7 0.1 reshape.18.index_ref
  85.8 1.8 %shard_map.169 = bf16[1024,256]{1,0:T(8,128)(2,1)} custom-call(s32[64]{0:T(128)S(1)} %reshape.18.index_ref, bf16[32,232,128]{2,1,0:T(8,128)(2,1)S(1)} %all-to-all-done.1.refs_0_), custom_call_target="tpu_custom_call" | custom-call | flops 1000000 | bytes 2097152 | tf_op jit(solution)/shard_map/pallas_call | solution.py:262
  87.6 10.6 %all-to-all-done.2.refs_1_.mine_ref = bf16[32,64,128]{2,1,0:T(8,128)(2,1)S(1)} async-done(((bf16[32,64,128]{2,1,0:T(8,128)(2,1)}), bf16[32,64,128]{2,1,0:T(8,128)(2,1)S(1)}, u32[]{:S(2)}, u32[]{:S(2)}) %all-to-all-start.2) | async-done | bytes 524320 | tf_op jit(solution)/shard_map/all_to_all | solution.py:218
  98.2 7.6 %collective-permute-start.5 = (bf16[32,32,128]{2,1,0:T(8,128)(2,1)S(1)}, bf16[32,32,128]{2,1,0:T(8,128)(2,1)S(1)}, u32[]{:S(2)}, u32[]{:S(2)}) collective-permute-start(bf16[32,32,128]{2,1,0:T(8,128)(2,1)S(1)} %slice.7), channel_id=1, source_target_pairs={{0,1},{1,0},{2,3},{3,2},{4,5},{5,4},{6,7},{7,6},{8,9},{9,8},{10,11... | collective-permute-start | bytes 786440 | tf_op jit(solution)/shard_map/ppermute | solution.py:269
  105.8 1.9 %shard_map.170 = bf16[1024,256]{1,0:T(8,128)(2,1)} custom-call(s32[64]{0:T(128)S(1)} %reshape.18.index_ref, bf16[32,232,128]{2,1,0:T(8,128)(2,1)S(1)} %all-to-all-done.1.refs_0_, bf16[32,64,128]{2,1,0:T(8,128)(2,1)S(1)} %all-to-all-done.2.refs_1_.mine_ref), custom_call_target="tpu_custom_call" | custom-call | flops 1000000 | bytes 2097152 | tf_op jit(solution)/shard_map/pallas_call | solution.py:262
  107.7 0.0 collective-permute-done.5.other_ref
  107.7 1.1 shard_map.171
  (4 shorter events, 0.0 us)
Async XLA Ops:
  0.6 16.5 %copy-start.4 = (bf16[768,256]{1,0:T(8,128)(2,1)S(1)}, bf16[768,256]{1,0:T(8,128)(2,1)}, u32[]{:S(2)}) copy-start(bf16[768,256]{1,0:T(8,128)(2,1)} %zero_ref.1) | copy-start | bytes 1179652
  0.6 16.5 %copy-start.3 = (bf16[768,256]{1,0:T(8,128)(2,1)S(1)}, bf16[768,256]{1,0:T(8,128)(2,1)}, u32[]{:S(2)}) copy-start(bf16[768,256]{1,0:T(8,128)(2,1)} %msg_ref.1) | copy-start | bytes 1179652
  0.7 14.3 %copy-start.9 = (s32[4]{0:T(128)S(1)}, s32[4]{0:T(128)}, u32[]{:S(2)}) copy-start(s32[4]{0:T(128)} %count_ref.3) | copy-start | bytes 52
  0.7 14.3 %copy-start.8 = (s32[4]{0:T(128)S(1)}, s32[4]{0:T(128)}, u32[]{:S(2)}) copy-start(s32[4]{0:T(128)} %user_ref.3) | copy-start | bytes 52
  0.7 14.3 %copy-start = (bf16[4,256,256]{2,1,0:T(8,128)(2,1)S(1)}, bf16[4,256,256]{2,1,0:T(8,128)(2,1)}, u32[]{:S(2)}) copy-start(bf16[4,256,256]{2,1,0:T(8,128)(2,1)} %adj_ref.3) | copy-start | bytes 1572868
  0.7 14.3 %copy-start.11 = (s32[32]{0:T(128)S(1)}, s32[32]{0:T(128)}, u32[]{:S(2)}) copy-start(s32[32]{0:T(128)} %item_ref.1) | copy-start | bytes 388
  0.7 14.3 %copy-start.10 = (s32[32,1]{0,1:T(1,128)S(1)}, s32[32,1]{0,1:T(1,128)}, u32[]{:S(2)}) copy-start(s32[32,1]{0,1:T(1,128)} %param.24) | copy-start | bytes 388
  4.5 23.4 %all-to-all-start = ((bf16[32,64,128]{2,1,0:T(8,128)(2,1)}), bf16[32,64,128]{2,1,0:T(8,128)(2,1)S(1)}, u32[]{:S(2)}, u32[]{:S(2)}) async-start(bf16[32,64,128]{2,1,0:T(8,128)(2,1)} %get-tuple-element.29), calls=%async_computation | async-start | bytes 1048576 | tf_op jit(solution)/shard_map/all_to_all | solution.py:218
  15.0 1.0 copy-start.2
  17.1 1.0 copy-start.5
  18.1 0.9 copy-start.6
  19.1 0.9 copy-start.7
  22.2 1.3 %copy-start.1 = (bf16[32,232,128]{2,1,0:T(8,128)(2,1)}, bf16[32,232,128]{2,1,0:T(8,128)(2,1)S(1)}, u32[]{:S(2)}) copy-start(bf16[32,232,128]{2,1,0:T(8,128)(2,1)S(1)} %get-tuple-element.34) | copy-start | bytes 5701636
  27.9 47.5 %all-to-all-start.1 = ((bf16[32,232,128]{2,1,0:T(8,128)(2,1)}), bf16[32,232,128]{2,1,0:T(8,128)(2,1)S(1)}, u32[]{:S(2)}, u32[]{:S(2)}) async-start(bf16[32,232,128]{2,1,0:T(8,128)(2,1)} %copy-done.1), calls=%async_computation.1 | async-start | bytes 3801088 | tf_op jit(solution)/shard_map/all_to_all | solution.py:218
  34.3 6.9 %collective-permute-start = (f32[32,128]{1,0:T(8,128)S(1)}, f32[32,128]{1,0:T(8,128)S(1)}, u32[]{:S(2)}, u32[]{:S(2)}) collective-permute-start(f32[32,128]{1,0:T(8,128)S(1)} %get-tuple-element.32), channel_id=1, source_target_pairs={{0,1},{1,0},{2,3},{3,2},{4,5},{5,4},{6,7},{7,6},{8,9},{9,8},{10,11... | collective-permute-start | bytes 49160 | tf_op jit(solution)/shard_map/ppermute | solution.py:251
  41.2 5.4 %collective-permute-start.1 = (f32[32,128]{1,0:T(8,128)S(1)}, f32[32,128]{1,0:T(8,128)S(1)}, u32[]{:S(2)}, u32[]{:S(2)}) collective-permute-start(f32[32,128]{1,0:T(8,128)S(1)} %add.9), channel_id=1, source_target_pairs={{2,0},{3,1},{0,2},{1,3},{6,4},{7,5},{4,6},{5,7},{10,8},{11,9},{8,1... | collective-permute-start | bytes 49160 | tf_op jit(solution)/shard_map/ppermute | solution.py:215
  46.6 7.2 %collective-permute-start.2 = (f32[32,128]{1,0:T(8,128)S(1)}, f32[32,128]{1,0:T(8,128)S(1)}, u32[]{:S(2)}, u32[]{:S(2)}) collective-permute-start(f32[32,128]{1,0:T(8,128)S(1)} %add.10), channel_id=1, source_target_pairs={{4,0},{5,1},{6,2},{7,3},{0,4},{1,5},{2,6},{3,7},{12,8},{13,9},{14,... | collective-permute-start | bytes 49160 | tf_op jit(solution)/shard_map/ppermute | solution.py:215
  53.8 14.0 %collective-permute-start.4 = (f32[32,128]{1,0:T(8,128)S(1)}, f32[32,128]{1,0:T(8,128)S(1)}, u32[]{:S(2)}, u32[]{:S(2)}) collective-permute-start(f32[32,128]{1,0:T(8,128)S(1)} %add.11.own_ref), channel_id=1, source_target_pairs={{8,0},{9,1},{10,2},{11,3},{12,4},{13,5},{14,6},{15,7},{16,8},{17,9... | collective-permute-start | bytes 49160 | tf_op jit(solution)/shard_map/ppermute | solution.py:215
  65.9 8.7 %collective-permute-start.3 = (f32[32,128]{1,0:T(8,128)S(1)}, f32[32,128]{1,0:T(8,128)S(1)}, u32[]{:S(2)}, u32[]{:S(2)}) collective-permute-start(f32[32,128]{1,0:T(8,128)S(1)} %add.11.own_ref), channel_id=1, source_target_pairs={{16,0},{17,1},{18,2},{19,3},{20,4},{21,5},{22,6},{23,7},{0,8},{1,9... | collective-permute-start | bytes 49160 | tf_op jit(solution)/shard_map/ppermute | solution.py:215
  75.4 22.8 %all-to-all-start.2 = ((bf16[32,64,128]{2,1,0:T(8,128)(2,1)}), bf16[32,64,128]{2,1,0:T(8,128)(2,1)S(1)}, u32[]{:S(2)}, u32[]{:S(2)}) async-start(bf16[32,64,128]{2,1,0:T(8,128)(2,1)} %shard_map.168), calls=%async_computation.2 | async-start | bytes 1048576 | tf_op jit(solution)/shard_map/all_to_all | solution.py:218
  98.2 9.5 %collective-permute-start.5 = (bf16[32,32,128]{2,1,0:T(8,128)(2,1)S(1)}, bf16[32,32,128]{2,1,0:T(8,128)(2,1)S(1)}, u32[]{:S(2)}, u32[]{:S(2)}) collective-permute-start(bf16[32,32,128]{2,1,0:T(8,128)(2,1)S(1)} %slice.7), channel_id=1, source_target_pairs={{0,1},{1,0},{2,3},{3,2},{4,5},{5,4},{6,7},{7,6},{8,9},{9,8},{10,11... | collective-permute-start | bytes 786440 | tf_op jit(solution)/shard_map/ppermute | solution.py:269
